TPU v7x, 128 devices: a whole 4x4x4 slice. The times are simulated.
128 devices in a mesh: dp: 8 (over z, core), list: 16 (over x, y).
Axes of the slice: x: 4, y: 4, z: 4, core: 2. Of those that a mesh axis runs over, the one named last changes fastest.
Arguments:
- candidates: bfloat16 [8, 2048, 1024], P('dp', 'list'), may hold values from -6 to 6
- counts: int32 [8], P('dp'), may hold values from 204 to 2048, as said below
- hist_keys: bfloat16 [8, 256, 1024], P('dp', 'list'), may hold values from -60 to 60
- hist_values: bfloat16 [8, 256, 1024], P('dp', 'list'), may hold values from -6 to 6
- hist_lengths: int32 [8], P('dp'), may hold values from 25 to 256, as said below
- gain: float32 [1024], replicated, may hold values from 0.5 to 1.5
- w_query: bfloat16 [1024, 1024], replicated, may hold values from -0.1875 to 0.1875
- w_key: bfloat16 [1024, 1024], replicated, may hold values from -0.1875 to 0.1875
- w_value: bfloat16 [1024, 1024], replicated, may hold values from -0.1875 to 0.1875
- cotangent: bfloat16 [8, 2048, 1024], P('dp', 'list'), may hold values from -6 to 6
Outputs:
- output: bfloat16 [8, 2048, 1024], P('dp', 'list')
- grad_x: bfloat16 [8, 2048, 1024], P('dp', 'list')
- grad_wq: float32 [1024, 1024], P(('dp', 'list'))
- grad_wk: float32 [1024, 1024], P(('dp', 'list'))
- grad_wv: float32 [1024, 1024], P(('dp', 'list'))
- grad_gain: float32 [1024], P(('dp', 'list'))
Inputs may be any that keep to these rules, and one draw needn't show every extreme that they name: `counts`: one request in every draw has exactly 2048 live candidates, another the fewest. `hist_lengths`: one request in every draw has exactly 256 live history actions, another the fewest.
All inputs are finite; a program needn't handle non-finite values.
Results may differ from a plain program's by a relative error of at most 0.025.
The roundings to bfloat16 on the way count: a program that leaves them out, or rounds other values in their place, can miss the bound.
Values may be sent and summed in bfloat16 or wider, within the bound.
No kernel may reach another device: no remote copies, remote signals or barrier semaphores. Data moves between devices by JAX's collectives and lax.ppermute only.
A program may use at most 192 MiB of HBM per device.

v0:
```python
import math

import jax
import jax.numpy as jnp
from jax import lax
from jax.sharding import PartitionSpec as P

D = 1024
H = 16
HEAD = 64


negative_fill = -1e30


def body(
    candidates,
    counts,
    hist_keys,
    hist_values,
    hist_lengths,
    gain,
    w_query,
    w_key,
    w_value,
    cotangent,
):
    scale = 1.0 / math.sqrt(HEAD)
    rows = candidates.shape[1]
    count = counts[0]
    hlength = hist_lengths[0]
    feats = candidates[0].astype(jnp.float32)
    mean_sq = jnp.mean(feats * feats, axis=-1, keepdims=True)
    inv_rms = lax.rsqrt(mean_sq + 1e-05)
    normed = (feats * inv_rms * gain).astype(jnp.bfloat16)
    query = jnp.dot(normed, w_query, preferred_element_type=jnp.float32).astype(jnp.bfloat16)
    key_rows = jnp.dot(normed, w_key, preferred_element_type=jnp.float32).astype(jnp.bfloat16)
    value_rows = jnp.dot(normed, w_value, preferred_element_type=jnp.float32).astype(jnp.bfloat16)
    past_keys, past_values = (
        lax.all_gather(hist_keys[0], "list", axis=0, tiled=True),
        lax.all_gather(hist_values[0], "list", axis=0, tiled=True),
    )
    cand_keys, cand_values = (
        lax.all_gather(key_rows, "list", axis=0, tiled=True),
        lax.all_gather(value_rows, "list", axis=0, tiled=True),
    )
    past = past_keys.shape[0]
    whole = cand_keys.shape[0]
    own_start = lax.axis_index("list") * rows
    heads_q = query.reshape(rows, H, HEAD)
    heads_k = jnp.concatenate([past_keys, cand_keys], 0).reshape(past + whole, H, HEAD)
    heads_v = jnp.concatenate([past_values, cand_values], 0).reshape(past + whole, H, HEAD)
    scores = (
        jnp.einsum("qhd,khd->hqk", heads_q, heads_k, preferred_element_type=jnp.float32) * scale
    )
    spots = jnp.arange(past + whole)
    usable = jnp.where(spots < past, spots < hlength, spots - past < count)
    scores = jnp.where(usable, scores, negative_fill)
    top = jnp.max(scores, axis=-1, keepdims=True)
    expo = jnp.where(usable, jnp.exp(scores - top), 0.0)
    total = jnp.sum(expo, axis=-1, keepdims=True)
    probs = expo / total
    probs_b = probs.astype(jnp.bfloat16)
    mixed = jnp.einsum("hqk,khd->qhd", probs_b, heads_v, preferred_element_type=jnp.float32)
    mixed = mixed.reshape(rows, D).astype(jnp.bfloat16)
    output = (feats + mixed.astype(jnp.float32)).astype(jnp.bfloat16)
    live = (own_start + jnp.arange(rows) < count).astype(jnp.float32)[:, None]
    grad_out = cotangent[0].astype(jnp.float32) * live
    grad_mix = grad_out.astype(jnp.bfloat16)
    heads_g = grad_mix.reshape(rows, H, HEAD)
    grad_probs = jnp.einsum("qhd,khd->hqk", heads_g, heads_v, preferred_element_type=jnp.float32)
    row_dot = jnp.sum(probs * grad_probs, axis=-1, keepdims=True)
    grad_scores = (probs * (grad_probs - row_dot) * scale).astype(jnp.bfloat16)
    grad_query = jnp.einsum(
        "hqk,khd->qhd", grad_scores, heads_k, preferred_element_type=jnp.float32
    )
    grad_query = grad_query.reshape(rows, D).astype(jnp.bfloat16)
    span = lax.axis_size("list") * rows
    score_part = lax.dynamic_slice_in_dim(grad_scores, past, span, 2)
    prob_part = lax.dynamic_slice_in_dim(probs_b, past, span, 2)
    term_k = jnp.einsum("hqk,qhd->khd", score_part, heads_q, preferred_element_type=jnp.float32)
    term_v = jnp.einsum("hqk,qhd->khd", prob_part, heads_g, preferred_element_type=jnp.float32)
    summed = lax.psum_scatter(
        jnp.concatenate([term_k.reshape(span, D), term_v.reshape(span, D)], 1),
        "list",
        scatter_dimension=0,
        tiled=True,
    )
    grad_key = summed[:, :D].astype(jnp.bfloat16)
    grad_value = summed[:, D:].astype(jnp.bfloat16)
    grad_normed = jnp.dot(grad_query, w_query.T, preferred_element_type=jnp.float32)
    grad_normed = grad_normed + jnp.dot(grad_key, w_key.T, preferred_element_type=jnp.float32)
    grad_normed = grad_normed + jnp.dot(grad_value, w_value.T, preferred_element_type=jnp.float32)
    scaled = grad_normed * gain
    grad_feats = (
        grad_out
        + inv_rms * scaled
        - feats * inv_rms**3 * jnp.mean(scaled * feats, axis=-1, keepdims=True)
    )
    grad_gain = jnp.sum(grad_normed * feats * inv_rms, axis=0)
    part_q = jnp.dot(normed.T, grad_query, preferred_element_type=jnp.float32)
    part_k = jnp.dot(normed.T, grad_key, preferred_element_type=jnp.float32)
    part_v = jnp.dot(normed.T, grad_value, preferred_element_type=jnp.float32)
    sum_q, sum_kw, sum_vw, sum_gain = (
        lax.psum_scatter(part_q, ("dp", "list"), scatter_dimension=0, tiled=True),
        lax.psum_scatter(part_k, ("dp", "list"), scatter_dimension=0, tiled=True),
        lax.psum_scatter(part_v, ("dp", "list"), scatter_dimension=0, tiled=True),
        lax.psum_scatter(grad_gain, ("dp", "list"), scatter_dimension=0, tiled=True),
    )
    return (output[None], grad_feats.astype(jnp.bfloat16)[None], sum_q, sum_kw, sum_vw, sum_gain)


def solution(mesh):
    in_specs = (
        P("dp", "list", None),
        P("dp"),
        P("dp", "list", None),
        P("dp", "list", None),
        P("dp"),
        P(),
        P(),
        P(),
        P(),
        P("dp", "list", None),
    )
    out_specs = (
        P("dp", "list", None),
        P("dp", "list", None),
        P(("dp", "list"), None),
        P(("dp", "list"), None),
        P(("dp", "list"), None),
        P(("dp", "list")),
    )
    return jax.shard_map(body, mesh=mesh, in_specs=in_specs, out_specs=out_specs, check_vma=False)
```

profile of v0, /device:TPU:0, one launch (start us, length us, event | category | flops | bytes accessed | tf_op | source)
XLA Modules:
  0.0 2238.6 jit_solution(13925131776132637830)
XLA Ops:
  7.2 0.0 copy-start
  7.2 0.0 copy-start.3
  7.2 0.0 copy-start.5
  7.2 0.0 copy-start.6
  7.2 0.0 all-gather.7.cloned.1.call-start
  7.3 1.2 fusion.23
  8.5 2.9 convolution_convert_fusion.2
  11.4 0.0 all-gather.7.cloned.1.call-update
  11.4 0.0 all-gather.5.cloned.1.call-start
  11.5 0.0 copy-done
  11.5 2.2 convolution_convert_fusion.4
  13.6 0.0 all-gather.5.cloned.1.call-update
  13.7 0.0 reduce-scatter.5.cloned.1.call-start
  15.0 2.2 convolution_convert_fusion.3
  17.2 0.2 copy.30
  17.4 0.0 copy-done.3
  17.4 0.1 copy.33
  17.6 0.0 copy-done.5
  17.6 27.1 %all-gather.1 = bf16[1,256,1024]{2,1,0:T(8,128)(2,1)} all-gather(bf16[1,16,1024]{2,1,0:T(8,128)(2,1)S(1)} %copy-done.5), channel_id=3, replica_groups=mesh['dp'=8,'list'=16] {'list'}, dimensions={1}, use_global_device_ids=true | all-gather | bytes 557056 | tf_op jit(solution)/shard_map/all_gather | solution.py:40
  44.7 0.0 copy-done.6
  44.7 23.8 %all-gather = bf16[1,256,1024]{2,1,0:T(8,128)(2,1)S(1)} all-gather(bf16[1,16,1024]{2,1,0:T(8,128)(2,1)S(1)} %copy-done.6), channel_id=2, replica_groups=mesh['dp'=8,'list'=16] {'list'}, dimensions={1}, use_global_device_ids=true | all-gather | bytes 557056 | tf_op jit(solution)/shard_map/all_gather | solution.py:41
  68.6 0.0 all-gather.7.cloned.1.call-done
  68.6 4.9 pad_maximum_fusion.2
  73.5 6.7 copy.31
  80.2 42.1 %all-gather.5.cloned.1.call-done = bf16[2048,1024]{1,0:T(8,128)(2,1)} async-done(((bf16[128,1024]{1,0:T(8,128)(2,1)}), bf16[2048,1024]{1,0:T(8,128)(2,1)}) %all-gather.5.cloned.1.call-update) | async-done | bytes 4194320 | tf_op jit(solution)/shard_map/all_gather | solution.py:45
  122.4 4.8 pad_maximum_fusion.1
  127.2 6.7 copy.29
  133.9 12.0 fusion.57
  146.0 10.2 fusion.56
  156.2 21.9 multiply_convert_fusion
  178.1 0.0 copy-start.1
  178.1 4.8 fusion.9
  182.9 1.3 copy-done.1
  184.2 1.3 fusion.11
  185.4 6.3 pad_maximum_fusion
  191.7 0.0 reduce-scatter.5.cloned.1.call-update
  191.7 0.0 copy-start.2
  191.7 0.0 copy-start.4
  191.8 0.2 reduce-scatter.7.cloned.1.call-start
  192.0 8.4 convolution_convert_fusion
  200.4 0.0 copy-done.2
  200.4 0.0 copy-done.4
  200.4 2.9 fusion.37
  203.3 0.0 reduce-scatter.7.cloned.1.call-update
  203.3 0.0 reduce-scatter.9.cloned.1.call-start
  203.4 98.8 %reduce-scatter.5.cloned.1.call-done = f32[128,2048]{0,1:T(8,128)} async-done(((f32[2048,2048]{0,1:T(8,128)}), f32[128,2048]{0,1:T(8,128)}) %reduce-scatter.5.cloned.1.call-update) | async-done | bytes 1048592 | tf_op jit(solution)/shard_map/reduce_scatter | solution.py:83
  302.1 1.3 convert.9
  303.4 2.8 fusion.45
  306.2 0.0 reduce-scatter.9.cloned.1.call-update
  306.2 0.0 reduce-scatter.11.cloned.1.call-start
  306.3 2.7 fusion.42
  309.0 0.0 reduce-scatter.11.cloned.1.call-update
  309.0 9.2 fusion.17
  318.3 2.0 copy.32
  320.3 1.8 fusion.32
  322.1 2.4 fusion.58
  324.5 2.4 convolution_add_fusion.1
  327.0 1.0 fusion.31
  327.9 65.7 %all-reduce = f32[1024]{0:T(1024)S(1)} all-reduce(f32[1024]{0:T(1024)S(1)} %get-tuple-element.6), channel_id=8, replica_groups=mesh['dp'=8,'list'=16] {'dp','list'}, use_global_device_ids=true, to_apply=%region_10.11.clone | all-reduce | flops 1024 | bytes 8192
  393.6 0.6 dynamic-slice
  394.2 1.9 fusion.39
  396.1 553.2 %reduce-scatter.7.cloned.1.call-done = f32[8,1024]{1,0:T(8,128)} async-done(((f32[1024,1024]{1,0:T(8,128)}), f32[8,1024]{1,0:T(8,128)}) %reduce-scatter.7.cloned.1.call-update) | async-done | bytes 32784 | tf_op jit(solution)/shard_map/reduce_scatter | solution.py:105
  949.3 641.8 %reduce-scatter.9.cloned.1.call-done = f32[8,1024]{1,0:T(8,128)} async-done(((f32[1024,1024]{1,0:T(8,128)}), f32[8,1024]{1,0:T(8,128)}) %reduce-scatter.9.cloned.1.call-update) | async-done | bytes 32784 | tf_op jit(solution)/shard_map/reduce_scatter | solution.py:106
  1591.0 640.7 %reduce-scatter.11.cloned.1.call-done = f32[8,1024]{1,0:T(8,128)} async-done(((f32[1024,1024]{1,0:T(8,128)}), f32[8,1024]{1,0:T(8,128)}) %reduce-scatter.11.cloned.1.call-update) | async-done | bytes 32784 | tf_op jit(solution)/shard_map/reduce_scatter | solution.py:107
  (4 shorter events, 0.0 us)
Async XLA Ops:
  7.2 4.3 copy-start
  7.2 10.2 copy-start.3
  7.2 10.4 copy-start.5
  7.2 37.5 %copy-start.6 = (bf16[1,16,1024]{2,1,0:T(8,128)(2,1)S(1)}, bf16[1,16,1024]{2,1,0:T(8,128)(2,1)}, u32[]{:S(2)}) copy-start(bf16[1,16,1024]{2,1,0:T(8,128)(2,1)} %param.13) | copy-start | bytes 98308
  7.2 61.4 %all-gather.7.cloned.1.call-start = ((), (), s32[]{:S(2)}) async-start(), calls=%async_computation.5 | async-start | bytes 4456448 | tf_op jit(solution)/shard_map/all_gather | solution.py:44
  11.4 110.9 %all-gather.5.cloned.1.call-start = ((), (), s32[]{:S(2)}) async-start(), calls=%async_computation.4 | async-start | bytes 4456448 | tf_op jit(solution)/shard_map/all_gather | solution.py:45
  13.7 288.5 %reduce-scatter.5.cloned.1.call-start = ((), (), s32[]{:S(2)}) async-start(), calls=%async_computation.6 | async-start | bytes 17825792 | tf_op jit(solution)/shard_map/reduce_scatter | solution.py:83
  178.1 6.1 copy-start.1
  191.7 8.7 copy-start.2
  191.7 8.7 copy-start.4
  191.8 757.5 %reduce-scatter.7.cloned.1.call-start = ((), (), s32[]{:S(2)}) async-start(), calls=%async_computation.7 | async-start | bytes 4227072 | tf_op jit(solution)/shard_map/reduce_scatter | solution.py:105
  203.3 1387.7 %reduce-scatter.9.cloned.1.call-start = ((), (), s32[]{:S(2)}) async-start(), calls=%async_computation.8 | async-start | bytes 4227072 | tf_op jit(solution)/shard_map/reduce_scatter | solution.py:106
  306.2 1925.6 %reduce-scatter.11.cloned.1.call-start = ((), (), s32[]{:S(2)}) async-start(), calls=%async_computation.9 | async-start | bytes 4227072 | tf_op jit(solution)/shard_map/reduce_scatter | solution.py:107
Sparse Core Ops, SparseCore 0:
  11.6 56.5 all-gather.6
  70.9 51.4 all-gather.4
  191.9 110.2 reduce-scatter.4
  304.9 644.3 reduce-scatter.6
  952.2 638.8 reduce-scatter.8
  1593.8 637.9 reduce-scatter.10
where the time goes:
time: 2240 us
  waiting for transfers between devices  1980 us (88%)
  blocking collectives  117 us (5%)
  matrix products  79.1 us (4%)
  other arithmetic  32.4 us (1%)
    reduce_scatter x1, waiting for transfers between devices, body(): lax.psum_scatter(part_k, ('dp', 'list'), scatter_dimension=0, tiled=True)  642 us
    reduce_scatter x1, waiting for transfers between devices, body(): lax.psum_scatter(part_v, ('dp', 'list'), scatter_dimension=0, tiled=True)  641 us
    reduce_scatter x1, waiting for transfers between devices, body(): lax.psum_scatter(part_q, ('dp', 'list'), scatter_dimension=0, tiled=True)  553 us
    reduce_scatter x1, waiting for transfers between devices, body(): lax.psum_scatter(jnp.concatenate([term_k.reshape(span, D), term_v.reshape...  98.8 us
    unnamed x1, blocking collectives  65.7 us
  transfers between devices with their start and end apart: 6, of which 5 were waited for; matrix products, arithmetic and copies ran while one was open for 2% of the time, Pallas kernels for 0%

commit v1 on v0

v1 whole, which is shorter than its diff:
```python
import math

import jax
import jax.numpy as jnp
from jax import lax
from jax.experimental import pallas as pl
from jax.experimental.pallas import tpu as pltpu
from jax.sharding import PartitionSpec as P

D = 1024
H = 16
HEAD = 64
ROWS = 128
PAST = 16
CAND = 2048
KEYS = 2304
BLOCK = ROWS + PAST
BF = jnp.bfloat16
F32 = jnp.float32
DEAD = -1e30
SCALE = 0.125
SCALE2 = SCALE / math.log(2.0)
MIB = 1 << 20


def lanes(shape):
    return lax.broadcasted_iota(jnp.int32, shape, len(shape) - 1)


def rows_of(shape):
    return lax.broadcasted_iota(jnp.int32, shape, len(shape) - 2)


def dot(a, b):
    return jnp.dot(a, b, preferred_element_type=F32)


def swap(x):
    return pltpu.roll(x, 64, 1)


def norm_rows(x, gain):
    inv = lax.rsqrt(jnp.mean(x * x, axis=-1, keepdims=True) + 1e-05)
    return x * inv, inv


def project_kernel(live_ref, x_ref, cot_ref, hk_ref, hv_ref, gain_ref, wq_ref, wk_ref, wv_ref, out_ref, normed_ref):
    @pl.when(pl.program_id(0) == 0)
    def _():
        x = x_ref[...].astype(F32)
        hat, _ = norm_rows(x, None)
        normed_ref[...] = (hat * gain_ref[...]).astype(BF)

    normed = normed_ref[...]
    q = dot(normed, wq_ref[...])
    k = dot(normed, wk_ref[...])
    v = dot(normed, wv_ref[...])
    g = cot_ref[...].astype(F32)
    g = jnp.where(rows_of(g.shape) < live_ref[0], g, 0.0)
    hk = hk_ref[...].astype(F32)
    hv = hv_ref[...].astype(F32)
    low = lanes((ROWS, 128)) < 64
    low_h = lanes((PAST, 128)) < 64
    for p in range(q.shape[1] // 128):
        s = slice(128 * p, 128 * p + 128)
        q1, k1, v1, g1, hk1, hv1 = q[:, s], k[:, s], v[:, s], g[:, s], hk[:, s], hv[:, s]
        a, b = 2 * p, 2 * p + 1
        out_ref[a, :ROWS, :128] = jnp.where(low, q1, swap(k1)).astype(BF)
        out_ref[b, :ROWS, :128] = jnp.where(low, swap(q1), k1).astype(BF)
        out_ref[a, :ROWS, 128:] = jnp.where(low, v1, swap(g1)).astype(BF)
        out_ref[b, :ROWS, 128:] = jnp.where(low, swap(v1), g1).astype(BF)
        out_ref[a, ROWS:, :128] = jnp.where(low_h, 0.0, swap(hk1)).astype(BF)
        out_ref[b, ROWS:, :128] = jnp.where(low_h, 0.0, hk1).astype(BF)
        out_ref[a, ROWS:, 128:] = jnp.where(low_h, hv1, 0.0).astype(BF)
        out_ref[b, ROWS:, 128:] = jnp.where(low_h, swap(hv1), 0.0).astype(BF)


def project(live, x, cot, hk, hv, gain, wq, wk, wv):
    n = 4
    w = D // n
    column = lambda j: (0, j)
    whole = lambda j: (0, 0)
    return pl.pallas_call(
        project_kernel,
        grid=(n,),
        in_specs=[
            pl.BlockSpec(memory_space=pltpu.SMEM),
            pl.BlockSpec((ROWS, D), whole),
            pl.BlockSpec((ROWS, w), column),
            pl.BlockSpec((PAST, w), column),
            pl.BlockSpec((PAST, w), column),
            pl.BlockSpec((1, D), whole),
            pl.BlockSpec((D, w), column),
            pl.BlockSpec((D, w), column),
            pl.BlockSpec((D, w), column),
        ],
        out_specs=pl.BlockSpec((H // n, BLOCK, 256), lambda j: (j, 0, 0)),
        out_shape=jax.ShapeDtypeStruct((H, BLOCK, 256), BF),
        scratch_shapes=[pltpu.VMEM((ROWS, D), BF)],
        compiler_params=pltpu.CompilerParams(vmem_limit_bytes=60 * MIB),
        cost_estimate=pl.CostEstimate(flops=6 * ROWS * D * D, bytes_accessed=8 * MIB, transcendentals=0),
        name="project",
    )(live, x, cot, hk, hv, gain, wq, wk, wv)


QB = 256
KC = 256


def attend_kernel(count_ref, past_ref, in_ref, out_ref, kn_ref, vx_ref, kt_ref, vt_ref, dk_ref, dv_ref, s_ref, p_ref, d_ref):
    count = count_ref[0]
    past = past_ref[0]
    low = lanes((128, 128)) < 64
    top = rows_of((128, 128)) == 0
    ones = jnp.where(rows_of((64, 128)) < 3, 1.0, 0.0).astype(BF)

    for j in range(KEYS // 128):
        if j < H:
            raw = in_ref[j, :ROWS, :]
            dead = lanes((128, 128)) + 128 * j >= count
        else:
            t = j - H
            raw = in_ref[8 * t : 8 * t + 8, ROWS:, :].reshape(128, 256)
            dead = lanes((128, 128)) + 128 * t >= past
        c = slice(128 * j, 128 * j + 128)
        kn_ref[c, :] = raw[:, :128]
        vg = raw[:, 128:].astype(F32)
        vx_ref[c, :] = jnp.where(low, vg, 1.0).astype(BF)
        kt = raw[:, :128].astype(F32).T[64:, :].astype(BF)
        kt_ref[0:64, c] = kt
        kt_ref[64:128, c] = kt
        kt_ref[128:256, c] = jnp.where(top & dead, DEAD, 0.0).astype(BF)
        vt_ref[0:64, c] = vg.T[:64, :].astype(BF)
        vt_ref[64:128, c] = ones
    dk_ref[...] = jnp.zeros_like(dk_ref)
    dv_ref[...] = jnp.zeros_like(dv_ref)

    lane = lanes((QB, 128))
    lowq = lane < 64
    unit = jnp.where(lane == 0, 1.0, 0.0).astype(BF)

    def step(i, carry):
        rows = in_ref[pl.ds(2 * i, 2), :ROWS, :].reshape(QB, 256)
        qk = rows[:, :128].astype(F32)
        vg = rows[:, 128:].astype(F32)
        qs = qk * SCALE2
        hi = qs.astype(BF).astype(F32)
        qx = jnp.concatenate([jnp.where(lowq, hi, swap(qs - hi)).astype(BF), unit], axis=1)
        top = None
        for c in range(KEYS // KC):
            cs = slice(c * KC, c * KC + KC)
            s = dot(qx, kt_ref[:, cs])
            s_ref[:, cs] = s
            for h in range(KC // 128):
                part = s[:, 128 * h : 128 * h + 128]
                top = part if top is None else jnp.maximum(top, part)
        top = jnp.max(top, axis=1, keepdims=True)
        pv = None
        for c in range(KEYS // KC):
            cs = slice(c * KC, c * KC + KC)
            e = jnp.exp2(s_ref[:, cs] - top)
            s_ref[:, cs] = e
            e = e.astype(BF)
            p_ref[:, cs] = e
            t = dot(e, vx_ref[cs, :])
            pv = t if pv is None else pv + t
        inv = 1.0 / jnp.where(lowq, swap(pv), 1.0)
        mixed = pv * inv
        g = (swap(vg) * inv).astype(BF)
        gf = g.astype(F32)
        rd = jnp.sum(jnp.where(lowq, gf * mixed, 0.0), axis=1, keepdims=True)
        r1 = rd.astype(BF).astype(F32)
        r2 = (rd - r1).astype(BF).astype(F32)
        r3 = rd - r1 - r2
        gx = jnp.where(lane == 64, -r1, jnp.where(lane == 65, -r2, jnp.where(lane == 66, -r3, 0.0)))
        gx = jnp.where(lowq, gf, gx).astype(BF)
        gq = None
        for c in range(KEYS // KC):
            cs = slice(c * KC, c * KC + KC)
            ds = (s_ref[:, cs] * dot(gx, vt_ref[:, cs])).astype(BF)
            d_ref[:, cs] = ds
            t = dot(ds, kn_ref[cs, :])
            gq = t if gq is None else gq + t
        both = jnp.where(lowq, mixed, gq * SCALE).T.astype(BF)
        out_ref[2 * i, 0:128, :] = both[:, :128]
        out_ref[2 * i + 1, 0:128, :] = both[:, 128:]
        qt = qk.T[:64, :].astype(BF)
        gt = gf.T[:64, :].astype(BF)
        for c in range(KEYS // KC):
            cs = slice(c * KC, c * KC + KC)
            dk_ref[:, cs] += dot(qt, d_ref[:, cs])
            dv_ref[:, cs] += dot(gt, p_ref[:, cs])
        return carry

    lax.fori_loop(0, CAND // QB, step, 0)
    for j in range(H):
        c = slice(128 * j, 128 * j + 128)
        out_ref[j, 128:192, :] = (dk_ref[:, c] * SCALE).astype(BF)
        out_ref[j, 192:256, :] = dv_ref[:, c].astype(BF)


def attend(count, past, packed):
    smem = pl.BlockSpec(memory_space=pltpu.SMEM)
    vmem = pl.BlockSpec(memory_space=pltpu.VMEM)
    return pl.pallas_call(
        attend_kernel,
        in_specs=[smem, smem, vmem],
        out_specs=vmem,
        out_shape=jax.ShapeDtypeStruct((H, 256, ROWS), BF),
        scratch_shapes=[
            pltpu.VMEM((KEYS, 128), BF),
            pltpu.VMEM((KEYS, 128), BF),
            pltpu.VMEM((256, KEYS), BF),
            pltpu.VMEM((128, KEYS), BF),
            pltpu.VMEM((64, KEYS), F32),
            pltpu.VMEM((64, KEYS), F32),
            pltpu.VMEM((QB, KEYS), F32),
            pltpu.VMEM((QB, KEYS), BF),
            pltpu.VMEM((QB, KEYS), BF),
        ],
        compiler_params=pltpu.CompilerParams(vmem_limit_bytes=60 * MIB),
        cost_estimate=pl.CostEstimate(flops=12 * CAND * KEYS * 256, bytes_accessed=3 * MIB, transcendentals=CAND * KEYS),
        name="attend",
    )(count, past, packed)


def weigh_kernel(x_ref, gain_ref, g_ref, out_ref, acc_ref):
    i = pl.program_id(0)

    @pl.when(i == 0)
    def _():
        acc_ref[...] = jnp.zeros_like(acc_ref)

    hat, _ = norm_rows(x_ref[...].astype(F32), None)
    normed = (hat * gain_ref[...]).astype(BF)
    gt = jnp.concatenate([g_ref[0, 64:, :], g_ref[1, 64:, :]], axis=1)
    acc_ref[0:192, :] += dot(gt, normed)

    @pl.when(i == pl.num_programs(0) - 1)
    def _():
        out_ref[...] = acc_ref[...].T.reshape(128, 8, 256).astype(BF)


def weigh(x, gain, grads):
    return pl.pallas_call(
        weigh_kernel,
        grid=(CAND // 256,),
        in_specs=[
            pl.BlockSpec((256, D), lambda i: (i, 0)),
            pl.BlockSpec((1, D), lambda i: (0, 0)),
            pl.BlockSpec((2, 256, ROWS), lambda i: (i, 0, 0)),
        ],
        out_specs=pl.BlockSpec((128, 8, 256), lambda i: (0, 0, 0)),
        out_shape=jax.ShapeDtypeStruct((128, 8, 256), BF),
        scratch_shapes=[pltpu.VMEM((256, D), F32)],
        compiler_params=pltpu.CompilerParams(vmem_limit_bytes=60 * MIB),
        cost_estimate=pl.CostEstimate(flops=2 * CAND * D * 256, bytes_accessed=6 * MIB, transcendentals=0),
        name="weigh",
    )(x, gain, grads)


def finish_kernel(live_ref, x_ref, cot_ref, gain_ref, g_ref, wq_ref, wk_ref, wv_ref, y_ref, gx_ref, acc_ref):
    t = pl.program_id(0)
    grad = lambda n: g_ref[:, 64 * n : 64 * n + 64, :].reshape(D, ROWS)

    @pl.when(t == 0)
    def _():
        mixed = grad(0).astype(F32).T
        y_ref[...] = (x_ref[...].astype(F32) + mixed).astype(BF)

    c = wq_ref.shape[0]
    total = dot(wq_ref[...], grad(1)) + dot(wk_ref[...], grad(2)) + dot(wv_ref[...], grad(3))
    acc_ref[pl.ds(pl.multiple_of(t * c, c), c), :] = total

    @pl.when(t == pl.num_programs(0) - 1)
    def _():
        x = x_ref[...].astype(F32)
        hat, inv = norm_rows(x, None)
        scaled = acc_ref[...].T * gain_ref[...]
        g = cot_ref[...].astype(F32)
        g = jnp.where(rows_of(g.shape) < live_ref[0], g, 0.0)
        mean = jnp.mean(scaled * x, axis=-1, keepdims=True)
        gx_ref[...] = (g + inv * scaled - x * (inv * inv * inv * mean)).astype(BF)


def finish(live, x, cot, gain, grads, wq, wk, wv):
    n = 4
    w = D // n
    whole = lambda j: (0, 0)
    row = lambda j: (j, 0)
    return pl.pallas_call(
        finish_kernel,
        grid=(n,),
        in_specs=[
            pl.BlockSpec(memory_space=pltpu.SMEM),
            pl.BlockSpec((ROWS, D), whole),
            pl.BlockSpec((ROWS, D), whole),
            pl.BlockSpec((1, D), whole),
            pl.BlockSpec((H, 256, ROWS), lambda j: (0, 0, 0)),
            pl.BlockSpec((w, D), row),
            pl.BlockSpec((w, D), row),
            pl.BlockSpec((w, D), row),
        ],
        out_specs=[pl.BlockSpec((ROWS, D), whole), pl.BlockSpec((ROWS, D), whole)],
        out_shape=[jax.ShapeDtypeStruct((ROWS, D), BF)] * 2,
        scratch_shapes=[pltpu.VMEM((D, ROWS), F32)],
        compiler_params=pltpu.CompilerParams(vmem_limit_bytes=60 * MIB),
        cost_estimate=pl.CostEstimate(flops=6 * ROWS * D * D, bytes_accessed=8 * MIB, transcendentals=0),
        name="finish",
    )(live, x, cot, gain, grads, wq, wk, wv)


def settle_kernel(in_ref, gain_ref, wq_ref, wk_ref, wv_ref, q_ref, k_ref, v_ref, gain_out_ref):
    low = lanes((8, 128)) < 64
    total = None
    for r in range(8):
        part = in_ref[16 * r : 16 * r + 16].astype(F32)
        total = part if total is None else total + part
    for p in range(H // 2):
        s = slice(128 * p, 128 * p + 128)
        a, b = total[2 * p], total[2 * p + 1]
        q_ref[:, s] = jnp.where(low, a[:, :128], swap(b[:, :128]))
        k_ref[:, s] = jnp.where(low, swap(a[:, :128]), b[:, :128])
        v_ref[:, s] = jnp.where(low, a[:, 128:], swap(b[:, 128:]))
    back = q_ref[...] * wq_ref[...].astype(F32) + k_ref[...] * wk_ref[...].astype(F32) + v_ref[...] * wv_ref[...].astype(F32)
    back = jnp.sum(back, axis=1, keepdims=True)
    wide = jnp.broadcast_to(back, (8, 128)).T
    gain_out_ref[...] = wide[0:1, :8] / gain_ref[...]


def settle(parts, gain, wq, wk, wv):
    vmem = pl.BlockSpec(memory_space=pltpu.VMEM)
    return pl.pallas_call(
        settle_kernel,
        in_specs=[vmem] * 5,
        out_specs=[vmem] * 4,
        out_shape=[jax.ShapeDtypeStruct((8, D), F32)] * 3 + [jax.ShapeDtypeStruct((1, 8), F32)],
        compiler_params=pltpu.CompilerParams(vmem_limit_bytes=60 * MIB),
        name="settle",
    )(parts, gain, wq, wk, wv)


def body(candidates, counts, hist_keys, hist_values, hist_lengths, gain, w_query, w_key, w_value, cotangent):
    x, cot = candidates[0], cotangent[0]
    spot = lax.axis_index("list")
    place = lax.axis_index("dp") * 16 + spot
    live = counts - spot * ROWS
    gains = gain[None]
    own = lambda w: lax.dynamic_slice_in_dim(w, place * 8, 8, 0)
    own_gain = lax.dynamic_slice_in_dim(gain, place * 8, 8, 0)[None]
    everyone = lax.all_gather(x, "list", axis=0, tiled=True)
    packed = project(live, x, cot, hist_keys[0], hist_values[0], gains, w_query, w_key, w_value)
    packed = lax.all_to_all(packed, "list", 0, 0, tiled=True)
    grads = attend(counts, hist_lengths, packed)
    back = lax.all_to_all(grads, "list", 0, 0, tiled=True)
    parts = weigh(everyone, gains, grads)
    parts = lax.all_to_all(parts, ("dp", "list"), 0, 0, tiled=True)
    y, grad_x = finish(live, x, cot, gains, back, w_query, w_key, w_value)
    gq, gk, gv, ggain = settle(parts, own_gain, own(w_query), own(w_key), own(w_value))
    return (y[None], grad_x[None], gq, gk, gv, ggain.reshape(8))


def solution(mesh):
    rows = P("dp", "list", None)
    weights = P(("dp", "list"), None)
    return jax.shard_map(
        body,
        mesh=mesh,
        in_specs=(rows, P("dp"), rows, rows, P("dp"), P(), P(), P(), P(), rows),
        out_specs=(rows, rows, weights, weights, weights, P(("dp", "list"))),
        check_vma=False,
    )
```

time: 2240 us -> 121 us (0.05)
  waiting for transfers between devices: 1980 us -> 33.7 us
  blocking collectives: 117 us -> 0 us
  matrix products: 79.1 us -> 0 us
  Pallas kernels: 0 us -> 44.6 us
  other arithmetic: 32.4 us -> 0 us
    reduce_scatter x4 -> x0, waiting for transfers between devices: 1930 us -> none  [the longest x1 642 us: body(): lax.psum_scatter(part_k, ('dp', 'list'), scatter_dimension=0, tiled=True)]
    unnamed x1 -> x0, blocking collectives: 65.7 us -> none
    all_gather x2 -> x0, blocking collectives: 51 us -> none  [the longest x1 27.1 us: body(): lax.all_gather(hist_keys[0], 'list', axis=0, tiled=True)]
    dot_general x13 -> x0, matrix products: 45.2 us -> none  [the longest x1 9.25 us: body(): jnp.einsum('hqk,khd->qhd', probs_b, heads_v, preferred_element_type=jnp.f...]
    pallas_call x0 -> x5, Pallas kernels: none -> 44.6 us  [the longest x1 22.6 us: attend(): pl.pallas_call(attend_kernel, in_specs=[smem, smem, vmem], out_specs=vmem...]
    all_gather x2 -> x1, waiting for transfers between devices: 42.2 us -> 1.81 us  [body(): everyone = lax.all_gather(x, 'list', axis=0, tiled=True)]
    sub x2 -> x0, matrix products: 34 us -> none  [the longest x1 21.9 us: body(): grad_scores = (probs * (grad_probs - row_dot) * scale).astype(jnp.bfloat16)]
    all_to_all x0 -> x3, waiting for transfers between devices: none -> 31.2 us  [the longest x1 22.4 us: body(): packed = lax.all_to_all(packed, 'list', 0, 0, tiled=True)]
  transfers between devices with their start and end apart: 6 -> 4, of which waited for: 5 -> 4; matrix products, arithmetic and copies ran while one was open for 2% -> 3% of each run, Pallas kernels for 0% -> 36%
where the time goes in v1:
time: 121 us; the launch traced here: 120 us
  Pallas kernels  44.6 us (37%)
  waiting for transfers between devices  33.7 us (28%)
  starting transfers between devices  20.8 us (17%)
  between operations  15.4 us (13%)
  local copies, waits for them, and re-layouts  5.81 us (5%)
    pallas_call x1, Pallas kernels, attend(): pl.pallas_call(attend_kernel, in_specs=[smem, smem, vmem], out_specs=vmem...  22.6 us
    all_to_all x1, waiting for transfers between devices, body(): packed = lax.all_to_all(packed, 'list', 0, 0, tiled=True)  22.4 us
    all_to_all x1, starting transfers between devices, body(): parts = lax.all_to_all(parts, ('dp', 'list'), 0, 0, tiled=True)  10 us
    pallas_call x1, Pallas kernels, weigh(): pl.pallas_call(weigh_kernel, grid=(CAND // 256,), in_specs=[pl.BlockSpec(...  7.67 us
    all_to_all x1, starting transfers between devices, body(): packed = lax.all_to_all(packed, 'list', 0, 0, tiled=True)  7.12 us
    pallas_call x1, Pallas kernels, finish(): pl.pallas_call(finish_kernel, grid=(n,), in_specs=[pl.BlockSpec(memory_sp...  6.53 us
    pallas_call x1, Pallas kernels, project(): pl.pallas_call(project_kernel, grid=(n,), in_specs=[pl.BlockSpec(memory_s...  5.91 us
    all_to_all x1, waiting for transfers between devices, body(): back = lax.all_to_all(grads, 'list', 0, 0, tiled=True)  5.66 us
  transfers between devices with their start and end apart: 4, of which 4 were waited for; matrix products, arithmetic and copies ran while one was open for 3% of the time, Pallas kernels for 36%

profile of v1, /device:TPU:0, one launch (start us, length us, event | category | flops | bytes accessed | tf_op | source)
XLA Modules:
  0.0 120.2 jit_solution(6493941826605777691)
XLA Ops:
  7.2 0.0 all-gather.3.cloned.1.call-start
  7.2 0.7 all-gather.3.cloned.1.call-update
  8.6 5.9 %project.1 = bf16[16,144,256]{2,1,0:T(8,128)(2,1)} custom-call(s32[1]{0:T(128)S(6)} %sub.7.live_ref, bf16[128,1024]{1,0:T(8,128)(2,1)} %bitcast.13, bf16[128,1024]{1,0:T(8,128)(2,1)} %bitcast.15, bf16[16,1024]{1,0:T(8,128)(2,1)} %bitcast.20, bf16[16,1024]{1,0:T(8,128)(2,1)} %bitcast.21, f32[1,1024]{1,0:T(1,128)} %bitcast.17, bf16[1024,1024]{1,0:T(8,128)(2,1)} %wq_ref.3, ...), custom_call_target="tpu_custom_call" | custom-call | flops 805306368 | bytes 8388608 | tf_op jit(solution)/shard_map/project/pallas_call | solution.py:83
  14.5 7.1 %all-to-all-start = ((bf16[16,144,256]{2,1,0:T(8,128)(2,1)}), bf16[16,144,256]{2,1,0:T(8,128)(2,1)S(1)}, u32[]{:S(2)}, u32[]{:S(2)}) async-start(bf16[16,144,256]{2,1,0:T(8,128)(2,1)} %project.1), calls=%async_computation | async-start | bytes 2359296 | tf_op jit(solution)/shard_map/all_to_all | solution.py:353
  22.2 22.4 %all-to-all-done.in_ref = bf16[16,144,256]{2,1,0:T(8,128)(2,1)S(1)} async-done(((bf16[16,144,256]{2,1,0:T(8,128)(2,1)}), bf16[16,144,256]{2,1,0:T(8,128)(2,1)S(1)}, u32[]{:S(2)}, u32[]{:S(2)}) %all-to-all-start) | async-done | bytes 1179680 | tf_op jit(solution)/shard_map/all_to_all | solution.py:353
  44.7 0.0 copy-start.2
  44.7 1.0 copy-done.2
  45.7 22.6 %attend.1.g_ref = bf16[16,256,128]{2,1,0:T(8,128)(2,1)} custom-call(s32[1]{0:T(128)S(6)} %copy.16.count_ref, s32[1]{0:T(128)S(6)} %copy.17.past_ref, bf16[16,144,256]{2,1,0:T(8,128)(2,1)} %copy-done.2), custom_call_target="tpu_custom_call" | custom-call | flops 14495514624 | bytes 3145728 | tf_op jit(solution)/shard_map/attend/pallas_call | solution.py:205
  68.3 3.7 %all-to-all-start.1 = ((bf16[16,256,128]{2,1,0:T(8,128)(2,1)}), bf16[16,256,128]{2,1,0:T(8,128)(2,1)S(1)}, u32[]{:S(2)}, u32[]{:S(2)}) async-start(bf16[16,256,128]{2,1,0:T(8,128)(2,1)} %attend.1.g_ref), calls=%async_computation.1 | async-start | bytes 2097152 | tf_op jit(solution)/shard_map/all_to_all | solution.py:355
  72.0 1.8 %all-gather.3.cloned.1.call-done = bf16[1,2048,1024]{2,1,0:T(8,128)(2,1)} async-done(((bf16[1,128,1024]{2,1,0:T(8,128)(2,1)}), bf16[1,2048,1024]{2,1,0:T(8,128)(2,1)}) %all-gather.3.cloned.1.call-update) | async-done | bytes 4194320 | tf_op jit(solution)/shard_map/all_gather | solution.py:351
  73.8 7.7 %weigh.1 = bf16[128,8,256]{2,1,0:T(8,128)(2,1)} custom-call(bf16[2048,1024]{1,0:T(8,128)(2,1)} %bitcast.12, f32[1,1024]{1,0:T(1,128)} %bitcast.18, bf16[16,256,128]{2,1,0:T(8,128)(2,1)} %attend.1.g_ref), custom_call_target="tpu_custom_call" | custom-call | flops 1073741824 | bytes 6291456 | tf_op jit(solution)/shard_map/weigh/pallas_call | solution.py:245
  81.5 5.7 %all-to-all-done.1.g_ref = bf16[16,256,128]{2,1,0:T(8,128)(2,1)S(1)} async-done(((bf16[16,256,128]{2,1,0:T(8,128)(2,1)}), bf16[16,256,128]{2,1,0:T(8,128)(2,1)S(1)}, u32[]{:S(2)}, u32[]{:S(2)}) %all-to-all-start.1) | async-done | bytes 1048608 | tf_op jit(solution)/shard_map/all_to_all | solution.py:355
  87.1 0.0 copy-start
  87.1 10.0 %all-to-all-start.2 = ((bf16[128,8,256]{2,1,0:T(8,128)(2,1)}), bf16[128,8,256]{2,1,0:T(8,128)(2,1)S(1)}, u32[]{:S(2)}, u32[]{:S(2)}) async-start(bf16[128,8,256]{2,1,0:T(8,128)(2,1)} %weigh.1), calls=%async_computation.2 | async-start | bytes 1048576 | tf_op jit(solution)/shard_map/all_to_all | solution.py:357
  97.2 1.3 %dynamic-slice_bitcast_fusion.gain_ref = f32[1,8]{1,0:T(1,128)} fusion(f32[1024]{0:T(1024)} %param.15, s32[]{:T(128)S(6)} %select_n.2), kind=kLoop, calls=%fused_computation.3 | loop fusion | bytes 68 | tf_op jit(solution)/shard_map/broadcast_in_dim | solution.py:350
  98.5 1.3 %constant_dynamic-slice_fusion.2.wq_ref = bf16[8,1024]{1,0:T(8,128)(2,1)} fusion(bf16[1024,1024]{1,0:T(8,128)(2,1)} %wq_ref.3, s32[]{:T(128)S(6)} %select_n.2), kind=kLoop, calls=%fused_computation.2 | loop fusion | bytes 32772 | tf_op jit(solution)/shard_map/dynamic_slice | solution.py:349
  99.8 1.3 %constant_dynamic-slice_fusion = (bf16[8,1024]{1,0:T(8,128)(2,1)}, bf16[8,1024]{1,0:T(8,128)(2,1)}) fusion(bf16[1024,1024]{1,0:T(8,128)(2,1)} %wv_ref.3, s32[]{:T(128)S(6)} %select_n.2, bf16[1024,1024]{1,0:T(8,128)(2,1)} %wk_ref.3), kind=kLoop, calls=%fused_computation | loop fusion | bytes 65540 | tf_op jit(solution)/shard_map/dynamic_slice | solution.py:349
  101.2 0.0 copy-done
  101.2 6.5 %finish.1 = (bf16[128,1024]{1,0:T(8,128)(2,1)}, bf16[128,1024]{1,0:T(8,128)(2,1)}) custom-call(s32[1]{0:T(128)S(6)} %sub.7.live_ref, bf16[128,1024]{1,0:T(8,128)(2,1)} %bitcast.14, bf16[128,1024]{1,0:T(8,128)(2,1)} %bitcast.16, f32[1,1024]{1,0:T(1,128)} %bitcast.19, bf16[16,256,128]{2,1,0:T(8,128)(2,1)} %copy-done, bf16[1024,1024]{1,0:T(8,128)(2,1)} %wq_ref.3, ...), custom_call_target="tpu_custom_call" | custom-call | flops 805306368 | bytes 8388608 | tf_op jit(solution)/shard_map/finish/pallas_call | solution.py:291
  107.7 3.1 %all-to-all-done.2.in_ref = bf16[128,8,256]{2,1,0:T(8,128)(2,1)S(1)} async-done(((bf16[128,8,256]{2,1,0:T(8,128)(2,1)}), bf16[128,8,256]{2,1,0:T(8,128)(2,1)S(1)}, u32[]{:S(2)}, u32[]{:S(2)}) %all-to-all-start.2) | async-done | bytes 524320 | tf_op jit(solution)/shard_map/all_to_all | solution.py:357
  110.8 0.0 copy-start.1
  110.8 0.8 copy-done.1
  111.5 1.9 %settle.1 = (f32[8,1024]{1,0:T(8,128)}, f32[8,1024]{1,0:T(8,128)}, f32[8,1024]{1,0:T(8,128)}, f32[1,8]{1,0:T(1,128)}) custom-call(bf16[128,8,256]{2,1,0:T(8,128)(2,1)} %copy-done.1, f32[1,8]{1,0:T(1,128)} %dynamic-slice_bitcast_fusion.gain_ref, bf16[8,1024]{1,0:T(8,128)(2,1)} %constant_dynamic-slice_fusion.2.wq_ref, ...), custom_call_target="tpu_custom_call" | custom-call | tf_op jit(solution)/shard_map/settle/pallas_call | solution.py:333
Async XLA Ops:
  7.2 66.6 %all-gather.3.cloned.1.call-start = ((), (), s32[]{:S(2)}) async-start(), calls=%async_computation.3 | async-start | bytes 4456448 | tf_op jit(solution)/shard_map/all_gather | solution.py:351
  14.5 30.2 %all-to-all-start = ((bf16[16,144,256]{2,1,0:T(8,128)(2,1)}), bf16[16,144,256]{2,1,0:T(8,128)(2,1)S(1)}, u32[]{:S(2)}, u32[]{:S(2)}) async-start(bf16[16,144,256]{2,1,0:T(8,128)(2,1)} %project.1), calls=%async_computation | async-start | bytes 2359296 | tf_op jit(solution)/shard_map/all_to_all | solution.py:353
  44.7 1.0 copy-start.2
  68.3 18.8 %all-to-all-start.1 = ((bf16[16,256,128]{2,1,0:T(8,128)(2,1)}), bf16[16,256,128]{2,1,0:T(8,128)(2,1)S(1)}, u32[]{:S(2)}, u32[]{:S(2)}) async-start(bf16[16,256,128]{2,1,0:T(8,128)(2,1)} %attend.1.g_ref), calls=%async_computation.1 | async-start | bytes 2097152 | tf_op jit(solution)/shard_map/all_to_all | solution.py:355
  87.1 14.0 %copy-start = (bf16[16,256,128]{2,1,0:T(8,128)(2,1)}, bf16[16,256,128]{2,1,0:T(8,128)(2,1)S(1)}, u32[]{:S(2)}) copy-start(bf16[16,256,128]{2,1,0:T(8,128)(2,1)S(1)} %all-to-all-done.1.g_ref) | copy-start | bytes 3145732
  87.1 23.6 %all-to-all-start.2 = ((bf16[128,8,256]{2,1,0:T(8,128)(2,1)}), bf16[128,8,256]{2,1,0:T(8,128)(2,1)S(1)}, u32[]{:S(2)}, u32[]{:S(2)}) async-start(bf16[128,8,256]{2,1,0:T(8,128)(2,1)} %weigh.1), calls=%async_computation.2 | async-start | bytes 1048576 | tf_op jit(solution)/shard_map/all_to_all | solution.py:357
  110.8 0.8 copy-start.1
Sparse Core Ops, SparseCore 0:
  10.1 63.6 all-gather.2

commit v2 on v1

v2 whole, which is shorter than its diff:
```python
import math

import jax
import jax.numpy as jnp
from jax import lax
from jax.experimental import pallas as pl
from jax.experimental.pallas import tpu as pltpu
from jax.sharding import PartitionSpec as P

D = 1024
H = 16
HEAD = 64
ROWS = 128
PAST = 16
CAND = 2048
KEYS = 2304
BLOCK = ROWS + PAST
BF = jnp.bfloat16
F32 = jnp.float32
DEAD = -1e30
SCALE = 0.125
SCALE2 = SCALE / math.log(2.0)
MIB = 1 << 20


def lanes(shape):
    return lax.broadcasted_iota(jnp.int32, shape, len(shape) - 1)


def rows_of(shape):
    return lax.broadcasted_iota(jnp.int32, shape, len(shape) - 2)


def dot(a, b):
    return jnp.dot(a, b, preferred_element_type=F32)


def swap(x):
    return pltpu.roll(x, 64, 1)


def inverse_rms(x):
    return lax.rsqrt(jnp.mean(x * x, axis=-1, keepdims=True) + 1e-05)


def norm_rows(x, gain):
    return (x * inverse_rms(x) * gain).astype(BF)


SMEM = pl.BlockSpec(memory_space=pltpu.SMEM)
VMEM = pl.BlockSpec(memory_space=pltpu.VMEM)
ANY = pl.BlockSpec(memory_space=pl.ANY)
WHOLE = pl.BlockSpec()
SOON = pl.CostEstimate(flops=1, bytes_accessed=1, transcendentals=0)


PARTS = 4
WIDE = D // PARTS


def project_kernel(live_ref, place_ref, x_ref, cot_ref, hk_ref, hv_ref, gain_ref, wq_ref, wk_ref, wv_ref, out_ref, own_ref, w_ref, sems):
    copies = [
        [
            pltpu.make_async_copy(w.at[:, pl.ds(j * WIDE, WIDE)], w_ref.at[t, j], sems.at[t, j])
            for t, w in enumerate((wq_ref, wk_ref, wv_ref))
        ]
        for j in range(PARTS)
    ]
    for row in copies:
        for copy in row:
            copy.start()
    normed = norm_rows(x_ref[...].astype(F32), gain_ref[...])
    low = lanes((ROWS, 128)) < 64
    low_h = lanes((PAST, 128)) < 64
    alive = rows_of((ROWS, 128)) < live_ref[0]
    own = pl.ds(pl.multiple_of(place_ref[0] // 2 * 16, 16), 16)
    for j in range(PARTS):
        for copy in copies[j]:
            copy.wait()
        q = dot(normed, w_ref[0, j])
        k = dot(normed, w_ref[1, j])
        v = dot(normed, w_ref[2, j])
        for t in range(3):
            own_ref[16 * t : 16 * t + 16, j * WIDE : j * WIDE + WIDE] = w_ref[t, j, own, :]
        for p in range(WIDE // 128):
            s = slice(128 * p, 128 * p + 128)
            c = slice(j * WIDE + 128 * p, j * WIDE + 128 * p + 128)
            q1, k1, v1 = q[:, s], k[:, s], v[:, s]
            g1 = jnp.where(alive, cot_ref[:, c].astype(F32), 0.0)
            hk1, hv1 = hk_ref[:, c].astype(F32), hv_ref[:, c].astype(F32)
            a = (j * WIDE + 128 * p) // HEAD
            b = a + 1
            out_ref[a, :ROWS, :128] = jnp.where(low, q1, swap(k1)).astype(BF)
            out_ref[b, :ROWS, :128] = jnp.where(low, swap(q1), k1).astype(BF)
            out_ref[a, :ROWS, 128:] = jnp.where(low, v1, swap(g1)).astype(BF)
            out_ref[b, :ROWS, 128:] = jnp.where(low, swap(v1), g1).astype(BF)
            out_ref[a, ROWS:, :128] = jnp.where(low_h, 0.0, swap(hk1)).astype(BF)
            out_ref[b, ROWS:, :128] = jnp.where(low_h, 0.0, hk1).astype(BF)
            out_ref[a, ROWS:, 128:] = jnp.where(low_h, hv1, 0.0).astype(BF)
            out_ref[b, ROWS:, 128:] = jnp.where(low_h, swap(hv1), 0.0).astype(BF)


def project(live, place, x, cot, hk, hv, gain, wq, wk, wv):
    return pl.pallas_call(
        project_kernel,
        in_specs=[SMEM] * 2 + [WHOLE] * 5 + [ANY] * 3,
        out_specs=[WHOLE] * 2,
        out_shape=[jax.ShapeDtypeStruct((H, BLOCK, 256), BF), jax.ShapeDtypeStruct((48, D), BF)],
        scratch_shapes=[pltpu.VMEM((3, PARTS, D, WIDE), BF), pltpu.SemaphoreType.DMA((3, PARTS))],
        compiler_params=pltpu.CompilerParams(vmem_limit_bytes=60 * MIB),
        cost_estimate=pl.CostEstimate(flops=60 * ROWS * D * D, bytes_accessed=8 * MIB, transcendentals=0),
        name="project",
    )(live, place, x, cot, hk, hv, gain, wq, wk, wv)


def gather_kernel(a_ref, b_ref, c_ref, d_ref, gain_ref, out_ref):
    for i, ref in enumerate((a_ref, b_ref, c_ref, d_ref)):
        out_ref[ROWS * i : ROWS * i + ROWS, :] = norm_rows(ref[...].astype(F32), gain_ref[...])


def gather(blocks, gain):
    return pl.pallas_call(
        gather_kernel,
        in_specs=[VMEM] * 5,
        out_specs=VMEM,
        out_shape=jax.ShapeDtypeStruct((4 * ROWS, D), BF),
        cost_estimate=SOON,
        compiler_params=pltpu.CompilerParams(vmem_limit_bytes=16 * MIB),
        name="gather",
    )(*blocks, gain)


QB = 256
KC = 768


def attend_kernel(count_ref, past_ref, in_ref, out_ref, kn_ref, vx_ref, kt_ref, vt_ref, dk_ref, dv_ref, s_ref, p_ref, d_ref):
    count = count_ref[0]
    past = past_ref[0]
    low = lanes((128, 128)) < 64
    top = rows_of((128, 128)) == 0
    ones = jnp.where(rows_of((64, 128)) < 3, 1.0, 0.0).astype(BF)

    for j in range(KEYS // 128):
        if j < H:
            raw = in_ref[j, :ROWS, :]
            dead = lanes((128, 128)) + 128 * j >= count
        else:
            t = j - H
            raw = in_ref[8 * t : 8 * t + 8, ROWS:, :].reshape(128, 256)
            dead = lanes((128, 128)) + 128 * t >= past
        c = slice(128 * j, 128 * j + 128)
        kn_ref[c, :] = raw[:, :128]
        vg = raw[:, 128:].astype(F32)
        vx_ref[c, :] = jnp.where(low, vg, 1.0).astype(BF)
        kt = raw[:, :128].astype(F32).T[64:, :].astype(BF)
        kt_ref[0:64, c] = kt
        kt_ref[64:128, c] = kt
        kt_ref[128:256, c] = jnp.where(top & dead, DEAD, 0.0).astype(BF)
        vt_ref[0:64, c] = vg.T[:64, :].astype(BF)
        vt_ref[64:128, c] = ones
    dk_ref[...] = jnp.zeros_like(dk_ref)
    dv_ref[...] = jnp.zeros_like(dv_ref)

    lane = lanes((QB, 128))
    lowq = lane < 64
    unit = jnp.where(lane == 0, 1.0, 0.0).astype(BF)

    def step(i, carry):
        rows = in_ref[pl.ds(2 * i, 2), :ROWS, :].reshape(QB, 256)
        qk = rows[:, :128].astype(F32)
        vg = rows[:, 128:].astype(F32)
        qs = qk * SCALE2
        hi = qs.astype(BF).astype(F32)
        qx = jnp.concatenate([jnp.where(lowq, hi, swap(qs - hi)).astype(BF), unit], axis=1)
        top = None
        for c in range(KEYS // KC):
            cs = slice(c * KC, c * KC + KC)
            s = dot(qx, kt_ref[:, cs])
            s_ref[:, cs] = s
            for h in range(KC // 128):
                part = s[:, 128 * h : 128 * h + 128]
                top = part if top is None else jnp.maximum(top, part)
        top = jnp.max(top, axis=1, keepdims=True)
        pv = None
        for c in range(KEYS // KC):
            cs = slice(c * KC, c * KC + KC)
            e = jnp.exp2(s_ref[:, cs] - top)
            s_ref[:, cs] = e
            e = e.astype(BF)
            p_ref[:, cs] = e
            t = dot(e, vx_ref[cs, :])
            pv = t if pv is None else pv + t
        inv = 1.0 / jnp.where(lowq, swap(pv), 1.0)
        mixed = pv * inv
        g = (swap(vg) * inv).astype(BF)
        gf = g.astype(F32)
        rd = jnp.sum(jnp.where(lowq, gf * mixed, 0.0), axis=1, keepdims=True)
        r1 = rd.astype(BF).astype(F32)
        r2 = (rd - r1).astype(BF).astype(F32)
        r3 = rd - r1 - r2
        gx = jnp.where(lane == 64, -r1, jnp.where(lane == 65, -r2, jnp.where(lane == 66, -r3, 0.0)))
        gx = jnp.where(lowq, gf, gx).astype(BF)
        gq = None
        for c in range(KEYS // KC):
            cs = slice(c * KC, c * KC + KC)
            ds = (s_ref[:, cs] * dot(gx, vt_ref[:, cs])).astype(BF)
            d_ref[:, cs] = ds
            t = dot(ds, kn_ref[cs, :])
            gq = t if gq is None else gq + t
        both = jnp.where(lowq, mixed, gq * SCALE).T.astype(BF)
        out_ref[2 * i, 0:128, :] = both[:, :128]
        out_ref[2 * i + 1, 0:128, :] = both[:, 128:]
        qt = qk.T[:64, :].astype(BF)
        gt = gf.T[:64, :].astype(BF)
        for c in range(KEYS // KC):
            cs = slice(c * KC, c * KC + KC)
            dk_ref[:, cs] += dot(qt, d_ref[:, cs])
            dv_ref[:, cs] += dot(gt, p_ref[:, cs])
        return carry

    lax.fori_loop(0, CAND // QB, step, 0)
    for j in range(H):
        c = slice(128 * j, 128 * j + 128)
        out_ref[j, 128:192, :] = (dk_ref[:, c] * SCALE).astype(BF)
        out_ref[j, 192:256, :] = dv_ref[:, c].astype(BF)


def attend(count, past, packed):
    return pl.pallas_call(
        attend_kernel,
        in_specs=[SMEM, SMEM, VMEM],
        out_specs=VMEM,
        out_shape=jax.ShapeDtypeStruct((H, 256, ROWS), BF),
        scratch_shapes=[
            pltpu.VMEM((KEYS, 128), BF),
            pltpu.VMEM((KEYS, 128), BF),
            pltpu.VMEM((256, KEYS), BF),
            pltpu.VMEM((128, KEYS), BF),
            pltpu.VMEM((64, KEYS), F32),
            pltpu.VMEM((64, KEYS), F32),
            pltpu.VMEM((QB, KEYS), F32),
            pltpu.VMEM((QB, KEYS), BF),
            pltpu.VMEM((QB, KEYS), BF),
        ],
        compiler_params=pltpu.CompilerParams(vmem_limit_bytes=24 * MIB),
        cost_estimate=pl.CostEstimate(flops=12 * CAND * KEYS * 256, bytes_accessed=3 * MIB, transcendentals=CAND * KEYS),
        name="attend",
    )(count, past, packed)


def weigh_kernel(where_ref, n0, n1, n2, n3, g0, g1, g2, g3, keep_ref, give_ref, acc_ref):
    i = pl.program_id(0)
    left = jnp.concatenate([g[0, 64:, :] for g in (g0, g1, g2, g3)], axis=1)
    right = jnp.concatenate([n[...] for n in (n0, n1, n2, n3)], axis=0)
    part = dot(left, right)

    @pl.when(i == 0)
    def _():
        acc_ref[...] = part

    @pl.when(i > 0)
    def _():
        acc_ref[...] += part

    @pl.when(i == pl.num_programs(0) - 1)
    def _():
        core = where_ref[16]
        for z in range(4):
            mine = pl.ds(pl.multiple_of((2 * z + core) * 128, 128), 128)
            other = pl.ds(pl.multiple_of((2 * z + 1 - core) * 128, 128), 128)
            keep_ref[z] = acc_ref[:, mine]
            give_ref[z] = acc_ref[:, other].astype(BF)


def weigh(where, normed, grads):
    fixed = lambda i, w: (0, 0, 0)
    return pl.pallas_call(
        weigh_kernel,
        grid_spec=pltpu.PrefetchScalarGridSpec(
            num_scalar_prefetch=1,
            grid=(4,),
            in_specs=[pl.BlockSpec((ROWS, D), lambda i, w: (i, 0))] * 4
            + [pl.BlockSpec((1, 256, ROWS), lambda i, w, a=a: (w[4 * a + i], 0, 0)) for a in range(4)],
            out_specs=[pl.BlockSpec((4, 192, 128), fixed), pl.BlockSpec((4, 192, 128), fixed)],
            scratch_shapes=[pltpu.VMEM((192, D), F32)],
        ),
        out_shape=[jax.ShapeDtypeStruct((4, 192, 128), F32), jax.ShapeDtypeStruct((4, 192, 128), BF)],
        compiler_params=pltpu.CompilerParams(vmem_limit_bytes=24 * MIB),
        cost_estimate=SOON,
        name="weigh",
    )(where, *normed, *([grads] * 4))


def pair_kernel(where_ref, keep_ref, came_ref, own_ref, a_ref, b_ref, c_ref):
    z = where_ref[17]
    total = lambda s: keep_ref[(z + s) % 4] + came_ref[(z + s) % 4].astype(F32)
    own_ref[...] = total(0)
    a_ref[...] = total(1).astype(BF)
    b_ref[...] = total(2).astype(BF)
    c_ref[...] = total(3).astype(BF)


def pair(where, keep, came):
    return pl.pallas_call(
        pair_kernel,
        in_specs=[SMEM, VMEM, VMEM],
        out_specs=[VMEM] * 4,
        out_shape=[jax.ShapeDtypeStruct((192, 128), F32)] + [jax.ShapeDtypeStruct((192, 128), BF)] * 3,
        cost_estimate=SOON,
        compiler_params=pltpu.CompilerParams(vmem_limit_bytes=16 * MIB),
        name="pair",
    )(where, keep, came)


def line_kernel(own_ref, a_ref, b_ref, c_ref, out_ref):
    total = own_ref[...] + a_ref[...].astype(F32) + b_ref[...].astype(F32) + c_ref[...].astype(F32)
    total = jnp.concatenate([total, jnp.zeros((64, 128), F32)], axis=0)
    out_ref[...] = total.T.reshape(16, 8, 256)


def line(own, a, b, c):
    return pl.pallas_call(
        line_kernel,
        in_specs=[VMEM] * 4,
        out_specs=VMEM,
        out_shape=jax.ShapeDtypeStruct((16, 8, 256), F32),
        cost_estimate=SOON,
        compiler_params=pltpu.CompilerParams(vmem_limit_bytes=16 * MIB),
        name="line",
    )(own, a, b, c)


def finish_kernel(live_ref, x_ref, cot_ref, gain_ref, g_ref, wq_ref, wk_ref, wv_ref, y_ref, gx_ref, w_ref, acc_ref, sems):
    copies = [
        [
            pltpu.make_async_copy(w.at[pl.ds(j * WIDE, WIDE), :], w_ref.at[t, j], sems.at[t, j])
            for t, w in enumerate((wq_ref, wk_ref, wv_ref))
        ]
        for j in range(PARTS)
    ]
    for row in copies:
        for copy in row:
            copy.start()
    grad = lambda n: g_ref[:, 64 * n : 64 * n + 64, :].reshape(D, ROWS)
    x = x_ref[...].astype(F32)
    y_ref[...] = (x + grad(0).astype(F32).T).astype(BF)
    for j in range(PARTS):
        for copy in copies[j]:
            copy.wait()
        total = dot(w_ref[0, j], grad(1)) + dot(w_ref[1, j], grad(2)) + dot(w_ref[2, j], grad(3))
        acc_ref[:, WIDE * j : WIDE * j + WIDE] = total.T
    inv = inverse_rms(x)
    scaled = acc_ref[...] * gain_ref[...]
    g = cot_ref[...].astype(F32)
    g = jnp.where(rows_of(g.shape) < live_ref[0], g, 0.0)
    mean = jnp.mean(scaled * x, axis=-1, keepdims=True)
    gx_ref[...] = (g + inv * scaled - x * (inv * inv * inv * mean)).astype(BF)


def finish(live, x, cot, gain, grads, wq, wk, wv):
    return pl.pallas_call(
        finish_kernel,
        in_specs=[SMEM] + [WHOLE] * 4 + [ANY] * 3,
        out_specs=[WHOLE] * 2,
        out_shape=[jax.ShapeDtypeStruct((ROWS, D), BF)] * 2,
        scratch_shapes=[
            pltpu.VMEM((3, PARTS, WIDE, D), BF),
            pltpu.VMEM((ROWS, D), F32),
            pltpu.SemaphoreType.DMA((3, PARTS)),
        ],
        compiler_params=pltpu.CompilerParams(vmem_limit_bytes=60 * MIB),
        cost_estimate=pl.CostEstimate(flops=6 * ROWS * D * D, bytes_accessed=8 * MIB, transcendentals=0),
        name="finish",
    )(live, x, cot, gain, grads, wq, wk, wv)


def settle_kernel(place_ref, in_ref, gain_ref, w_ref, q_ref, k_ref, v_ref, gain_out_ref):
    low = lanes((8, 128)) < 64
    for p in range(H // 2):
        s = slice(128 * p, 128 * p + 128)
        a, b = in_ref[2 * p], in_ref[2 * p + 1]
        q_ref[:, s] = jnp.where(low, a[:, :128], swap(b[:, :128]))
        k_ref[:, s] = jnp.where(low, swap(a[:, :128]), b[:, :128])
        v_ref[:, s] = jnp.where(low, a[:, 128:], swap(b[:, 128:]))
    w = w_ref[...].astype(F32)
    odd = jnp.broadcast_to(place_ref[0] % 2, (8, D)) == 1
    back = 0.0
    for t, ref in enumerate((q_ref, k_ref, v_ref)):
        back = back + ref[...] * jnp.where(odd, w[16 * t + 8 : 16 * t + 16], w[16 * t : 16 * t + 8])
    back = jnp.sum(back, axis=1, keepdims=True)
    own = lanes((8, D)) == 8 * place_ref[0] + rows_of((8, D))
    gain = jnp.sum(jnp.where(own, gain_ref[...], 0.0), axis=1, keepdims=True)
    gain_out_ref[...] = jnp.broadcast_to(back / gain, (8, 128)).T[0:1, :8]


def settle(place, parts, gain, weights):
    return pl.pallas_call(
        settle_kernel,
        in_specs=[SMEM, VMEM, VMEM, VMEM],
        out_specs=[WHOLE] * 4,
        out_shape=[jax.ShapeDtypeStruct((8, D), F32)] * 3 + [jax.ShapeDtypeStruct((1, 8), F32)],
        compiler_params=pltpu.CompilerParams(vmem_limit_bytes=16 * MIB),
        name="settle",
    )(place, parts, gain, weights)


def neighbour(first, s):
    pairs = []
    for i in range(128):
        spot = i % 16
        if (i // 16 % 2 == 0) == first:
            spot = spot // 4 * 4 + (spot + s) % 4
        else:
            spot = (spot + 4 * s) % 16
        pairs.append((i, i // 16 * 16 + spot))
    return pairs


def near(a, s):
    return lax.ppermute(a, ("dp", "list"), neighbour(True, s))


def far(a, s):
    return lax.ppermute(a, ("dp", "list"), neighbour(False, s))


def along_z(a, s):
    return lax.ppermute(a, "dp", [(i, (i + 2 * s) % 8) for i in range(8)])


def other_core(a):
    return lax.ppermute(a, "dp", [(i, i ^ 1) for i in range(8)])


def body(candidates, counts, hist_keys, hist_values, hist_lengths, gain, w_query, w_key, w_value, cotangent):
    x, cot = candidates[0], cotangent[0]
    spot, part = lax.axis_index("list"), lax.axis_index("dp")
    live = counts - spot * ROWS
    gains = gain[None]
    a, i = jnp.arange(16) // 4, jnp.arange(16) % 4
    core = part % 2
    dx, dy = jnp.where(core == 0, a, i), jnp.where(core == 0, i, a)
    source = 4 * ((spot // 4 - dx) % 4) + (spot % 4 - dy) % 4
    where = jnp.concatenate([source, jnp.stack([core, part // 2])]).astype(jnp.int32)
    place = (part * 16 + spot).astype(jnp.int32)[None]

    blocks = [x] + [near(x, s) for s in (1, 2, 3)]
    packed, own_weights = project(live, place, x, cot, hist_keys[0], hist_values[0], gains, w_query, w_key, w_value)
    packed, where, *blocks = lax.optimization_barrier((packed, where, *blocks))
    packed = lax.all_to_all(packed, "list", 0, 0, tiled=True)
    normed = gather(blocks, gains)
    normed, packed = lax.optimization_barrier((normed, packed))
    normed = [normed] + [far(normed, s) for s in (1, 2, 3)]
    grads = attend(counts, hist_lengths, packed)
    back = lax.all_to_all(grads, "list", 0, 0, tiled=True)
    keep, give = weigh(where, normed, grads)
    own, *give = pair(where, keep, other_core(give))
    parts = line(own, *[along_z(g, s) for g, s in zip(give, (1, 2, 3))])
    parts, back = lax.optimization_barrier((parts, back))
    parts = lax.all_to_all(parts, "list", 0, 0, tiled=True)
    y, grad_x = finish(live, x, cot, gains, back, w_query, w_key, w_value)
    gq, gk, gv, ggain = settle(place, parts, gains, own_weights)
    return (y[None], grad_x[None], gq, gk, gv, ggain.reshape(8))


def solution(mesh):
    rows = P("dp", "list", None)
    weights = P(("dp", "list"), None)
    return jax.shard_map(
        body,
        mesh=mesh,
        in_specs=(rows, P("dp"), rows, rows, P("dp"), P(), P(), P(), P(), rows),
        out_specs=(rows, rows, weights, weights, weights, P(("dp", "list"))),
        check_vma=False,
    )
```

time: 121 us -> 100 us (0.83)
  between operations: 15.4 us -> 2.14 us
  starting transfers between devices: 20.8 us -> 33.8 us
  waiting for transfers between devices: 33.7 us -> 24.3 us
  local copies, waits for them, and re-layouts: 5.81 us -> 0.03 us
  Pallas kernels: 44.6 us -> 39.2 us
    ppermute x0 -> x10, starting transfers between devices: none -> 16.2 us  [the longest x3 6.56 us: along_z(): return lax.ppermute(a, 'dp', [(i, (i + 2 * s) % 8) for i in range(8)])]
    ppermute x0 -> x10, waiting for transfers between devices: none -> 6.24 us  [the longest x3 3.09 us: along_z(): return lax.ppermute(a, 'dp', [(i, (i + 2 * s) % 8) for i in range(8)])]
    all_to_all x1, waiting for transfers between devices: 22.4 us -> 16.5 us  [body(): packed = lax.all_to_all(packed, 'list', 0, 0, tiled=True)]
    all_to_all x1, waiting for transfers between devices: 5.66 us -> 0.01 us  [body(): back = lax.all_to_all(grads, 'list', 0, 0, tiled=True)]
    pallas_call x5 -> x8, Pallas kernels: 44.6 us -> 39.2 us  [the longest x1 20.4 us: attend(): pl.pallas_call(attend_kernel, in_specs=[SMEM, SMEM, VMEM], out_specs=VMEM...]
    all_to_all x1, starting transfers between devices: 10 us -> 6.97 us  [body(): parts = lax.all_to_all(parts, 'list', 0, 0, tiled=True)]
    dynamic_slice x2 -> x0, local copies, waits for them, and re-layouts: 2.65 us -> none  [body(): own = lambda w: lax.dynamic_slice_in_dim(w, place * 8, 8, 0)]
    all_gather x1 -> x0, waiting for transfers between devices: 1.81 us -> none  [body(): everyone = lax.all_gather(x, 'list', axis=0, tiled=True)]
  transfers between devices with their start and end apart: 4 -> 13, of which waited for: 4 -> 6; matrix products, arithmetic and copies ran while one was open for 3% -> 0% of each run, Pallas kernels for 36% -> 39%
where the time goes in v2:
time: 100 us; the launch traced here: 99.5 us
  Pallas kernels  39.2 us (39%)
  starting transfers between devices  33.8 us (34%)
  waiting for transfers between devices  24.3 us (24%)
  between operations  2.14 us (2%)
    pallas_call x1, Pallas kernels, attend(): pl.pallas_call(attend_kernel, in_specs=[SMEM, SMEM, VMEM], out_specs=VMEM...  20.4 us
    all_to_all x1, waiting for transfers between devices, body(): packed = lax.all_to_all(packed, 'list', 0, 0, tiled=True)  16.5 us
    all_to_all x1, starting transfers between devices, body(): parts = lax.all_to_all(parts, 'list', 0, 0, tiled=True)  6.97 us
    ppermute x3, starting transfers between devices, along_z(): return lax.ppermute(a, 'dp', [(i, (i + 2 * s) % 8) for i in range(8)])  6.56 us
    pallas_call x1, Pallas kernels, finish(): pl.pallas_call(finish_kernel, in_specs=[SMEM] + [WHOLE] * 4 + [ANY] * 3,...  6.24 us
    all_to_all x1, starting transfers between devices, body(): packed = lax.all_to_all(packed, 'list', 0, 0, tiled=True)  6.18 us
    ppermute x3, starting transfers between devices, near(): return lax.ppermute(a, ('dp', 'list'), neighbour(True, s))  5.98 us
    pallas_call x1, Pallas kernels, project(): pl.pallas_call(project_kernel, in_specs=[SMEM] * 2 + [WHOLE] * 5 + [ANY]...  5.69 us
  transfers between devices with their start and end apart: 13, of which 6 were waited for; matrix products, arithmetic and copies ran while one was open for 0% of the time, Pallas kernels for 39%

profile of v2, /device:TPU:0, one launch (start us, length us, event | category | flops | bytes accessed | tf_op | source)
XLA Modules:
  0.0 99.5 jit_solution(17942493094290071014)
XLA Ops:
  0.6 1.7 %collective-permute-start = (bf16[128,1024]{1,0:T(8,128)(2,1)}, bf16[128,1024]{1,0:T(8,128)(2,1)S(1)}, u32[]{:S(2)}, u32[]{:S(2)}) collective-permute-start(bf16[128,1024]{1,0:T(8,128)(2,1)} %bitcast.12), channel_id=1, source_target_pairs={{0,1},{1,2},{2,3},{3,0},{4,5},{5,6},{6,7},{7,4},{8,9},{9,10},{10,1... | collective-permute-start | bytes 786440 | tf_op jit(solution)/shard_map/ppermute | solution.py:421
  2.4 2.9 %collective-permute-start.1 = (bf16[128,1024]{1,0:T(8,128)(2,1)}, bf16[128,1024]{1,0:T(8,128)(2,1)S(1)}, u32[]{:S(2)}, u32[]{:S(2)}) collective-permute-start(bf16[128,1024]{1,0:T(8,128)(2,1)} %bitcast.13), channel_id=1, source_target_pairs={{0,2},{1,3},{2,0},{3,1},{4,6},{5,7},{6,4},{7,5},{8,10},{9,11},{10,... | collective-permute-start | bytes 786440 | tf_op jit(solution)/shard_map/ppermute | solution.py:421
  5.3 1.3 %collective-permute-start.2 = (bf16[128,1024]{1,0:T(8,128)(2,1)}, bf16[128,1024]{1,0:T(8,128)(2,1)S(1)}, u32[]{:S(2)}, u32[]{:S(2)}) collective-permute-start(bf16[128,1024]{1,0:T(8,128)(2,1)} %bitcast.14), channel_id=1, source_target_pairs={{0,3},{1,0},{2,1},{3,2},{4,7},{5,4},{6,5},{7,6},{8,11},{9,8},{10,9... | collective-permute-start | bytes 786440 | tf_op jit(solution)/shard_map/ppermute | solution.py:421
  7.3 5.7 %project.1 = (bf16[16,144,256]{2,1,0:T(8,128)(2,1)}, bf16[48,1024]{1,0:T(8,128)(2,1)}) custom-call(s32[1]{0:T(128)S(6)} %sub.32.live_ref, s32[1]{0:T(128)} %bitcast.4.place_ref, bf16[128,1024]{1,0:T(8,128)(2,1)} %bitcast.15, bf16[128,1024]{1,0:T(8,128)(2,1)} %bitcast.22, bf16[16,1024]{1,0:T(8,128)(2,1)} %bitcast.26, bf16[16,1024]{1,0:T(8,128)(2,1)} %bitcast.27, ...), custom_call_target="tpu_custom_call" | custom-call | flops 8053063680 | bytes 8388608 | tf_op jit(solution)/shard_map/project/pallas_call | solution.py:104
  13.0 0.0 copy-start
  13.0 0.0 copy-start.2
  13.0 0.1 pad_add_fusion.where_ref
  13.1 0.0 collective-permute-done.b_ref
  13.1 0.0 collective-permute-done.1.c_ref
  13.1 0.0 collective-permute-done.2.d_ref
  13.1 6.2 %all-to-all-start = ((bf16[16,144,256]{2,1,0:T(8,128)(2,1)}), bf16[16,144,256]{2,1,0:T(8,128)(2,1)S(1)}, u32[]{:S(2)}, u32[]{:S(2)}) async-start(bf16[16,144,256]{2,1,0:T(8,128)(2,1)} %get-tuple-element.36), calls=%async_computation | async-start | bytes 2359296 | tf_op jit(solution)/shard_map/all_to_all | solution.py:451
  20.0 0.0 copy-done
  20.0 0.0 copy-done.2
  20.0 0.4 gather.1.n0
  20.4 16.5 %all-to-all-done.in_ref = bf16[16,144,256]{2,1,0:T(8,128)(2,1)S(1)} async-done(((bf16[16,144,256]{2,1,0:T(8,128)(2,1)}), bf16[16,144,256]{2,1,0:T(8,128)(2,1)S(1)}, u32[]{:S(2)}, u32[]{:S(2)}) %all-to-all-start) | async-done | bytes 1179680 | tf_op jit(solution)/shard_map/all_to_all | solution.py:451
  36.9 0.1 collective-permute-start.3
  37.0 2.5 %collective-permute-start.4 = (bf16[512,1024]{1,0:T(8,128)(2,1)S(1)}, bf16[512,1024]{1,0:T(8,128)(2,1)}, u32[]{:S(2)}, u32[]{:S(2)}) collective-permute-start(bf16[512,1024]{1,0:T(8,128)(2,1)S(1)} %gather.1.n0), channel_id=1, source_target_pairs={{0,8},{1,9},{2,10},{3,11},{4,12},{5,13},{6,14},{7,15},{8,0},{9,1},... | collective-permute-start | bytes 3145736 | tf_op jit(solution)/shard_map/ppermute | solution.py:425
  39.5 1.0 collective-permute-start.5
  40.5 20.4 %attend.1.g0.g1.g2.g3 = bf16[16,256,128]{2,1,0:T(8,128)(2,1)} custom-call(s32[1]{0:T(128)S(6)} %copy.16.count_ref, s32[1]{0:T(128)S(6)} %copy.17.past_ref, bf16[16,144,256]{2,1,0:T(8,128)(2,1)S(1)} %all-to-all-done.in_ref), custom_call_target="tpu_custom_call" | custom-call | flops 14495514624 | bytes 3145728 | tf_op jit(solution)/shard_map/attend/pallas_call | solution.py:230
  60.9 4.4 %all-to-all-start.1 = ((bf16[16,256,128]{2,1,0:T(8,128)(2,1)}), bf16[16,256,128]{2,1,0:T(8,128)(2,1)S(1)}, u32[]{:S(2)}, u32[]{:S(2)}) async-start(bf16[16,256,128]{2,1,0:T(8,128)(2,1)} %attend.1.g0.g1.g2.g3), calls=%async_computation.1 | async-start | bytes 2097152 | tf_op jit(solution)/shard_map/all_to_all | solution.py:456
  65.3 0.0 collective-permute-done.3.n1
  65.3 0.0 collective-permute-done.4.n2
  65.3 1.7 %collective-permute-done.5.n3 = bf16[512,1024]{1,0:T(8,128)(2,1)} collective-permute-done((bf16[512,1024]{1,0:T(8,128)(2,1)S(1)}, bf16[512,1024]{1,0:T(8,128)(2,1)}, u32[]{:S(2)}, u32[]{:S(2)}) %collective-permute-start.5) | collective-permute-done | bytes 1048608 | tf_op jit(solution)/shard_map/ppermute | solution.py:425
  67.0 4.3 %weigh.1 = (f32[4,192,128]{2,1,0:T(8,128)S(1)}, bf16[4,192,128]{2,1,0:T(8,128)(2,1)S(1)}) custom-call(s32[18]{0:T(128)S(1)} %pad_add_fusion.where_ref, bf16[512,1024]{1,0:T(8,128)(2,1)S(1)} %gather.1.n0, bf16[512,1024]{1,0:T(8,128)(2,1)S(1)} %collective-permute-done.3.n1, bf16[512,1024]{1,0:T(8,128)(2,1)} %collective-permute-done.4.n2, ...), custom_call_target="tpu_custom_call" | custom-call | flops 1 | bytes 1 | tf_op jit(solution)/shard_map/weigh/pallas_call | solution.py:278
  71.4 0.1 collective-permute-start.6
  71.5 1.4 %collective-permute-done.6.came_ref = bf16[4,192,128]{2,1,0:T(8,128)(2,1)S(1)} collective-permute-done((bf16[4,192,128]{2,1,0:T(8,128)(2,1)S(1)}, bf16[4,192,128]{2,1,0:T(8,128)(2,1)S(1)}, u32[]{:S(2)}, u32[]{:S(2)}) %collective-permute-start.6) | collective-permute-done | bytes 196640 | tf_op jit(solution)/shard_map/ppermute | solution.py:433
  72.9 0.6 pair.1
  73.5 2.0 %collective-permute-start.7 = (bf16[192,128]{1,0:T(8,128)(2,1)S(1)}, bf16[192,128]{1,0:T(8,128)(2,1)S(1)}, u32[]{:S(2)}, u32[]{:S(2)}) collective-permute-start(bf16[192,128]{1,0:T(8,128)(2,1)S(1)} %get-tuple-element.42), channel_id=1, source_target_pairs={{0,32},{16,48},{32,64},{48,80},{64,96},{80,112},{96,0},{112,16},{1... | collective-permute-start | bytes 147464 | tf_op jit(solution)/shard_map/ppermute | solution.py:429
  75.5 3.6 %collective-permute-start.8 = (bf16[192,128]{1,0:T(8,128)(2,1)S(1)}, bf16[192,128]{1,0:T(8,128)(2,1)S(1)}, u32[]{:S(2)}, u32[]{:S(2)}) collective-permute-start(bf16[192,128]{1,0:T(8,128)(2,1)S(1)} %get-tuple-element.43), channel_id=1, source_target_pairs={{0,64},{16,80},{32,96},{48,112},{64,0},{80,16},{96,32},{112,48},{1... | collective-permute-start | bytes 147464 | tf_op jit(solution)/shard_map/ppermute | solution.py:429
  79.1 1.0 %collective-permute-start.9 = (bf16[192,128]{1,0:T(8,128)(2,1)S(1)}, bf16[192,128]{1,0:T(8,128)(2,1)S(1)}, u32[]{:S(2)}, u32[]{:S(2)}) collective-permute-start(bf16[192,128]{1,0:T(8,128)(2,1)S(1)} %get-tuple-element.44), channel_id=1, source_target_pairs={{0,96},{16,112},{32,0},{48,16},{64,32},{80,48},{96,64},{112,80},{1... | collective-permute-start | bytes 147464 | tf_op jit(solution)/shard_map/ppermute | solution.py:429
  80.0 0.0 collective-permute-done.7.a_ref
  80.1 1.8 %collective-permute-done.8.b_ref = bf16[192,128]{1,0:T(8,128)(2,1)S(1)} collective-permute-done((bf16[192,128]{1,0:T(8,128)(2,1)S(1)}, bf16[192,128]{1,0:T(8,128)(2,1)S(1)}, u32[]{:S(2)}, u32[]{:S(2)}) %collective-permute-start.8) | collective-permute-done | bytes 49184 | tf_op jit(solution)/shard_map/ppermute | solution.py:429
  81.9 1.3 %collective-permute-done.9.c_ref = bf16[192,128]{1,0:T(8,128)(2,1)S(1)} collective-permute-done((bf16[192,128]{1,0:T(8,128)(2,1)S(1)}, bf16[192,128]{1,0:T(8,128)(2,1)S(1)}, u32[]{:S(2)}, u32[]{:S(2)}) %collective-permute-start.9) | collective-permute-done | bytes 49184 | tf_op jit(solution)/shard_map/ppermute | solution.py:429
  83.1 0.8 line.1
  83.9 0.0 all-to-all-done.1.g_ref
  83.9 0.0 copy-start.4
  83.9 7.0 %all-to-all-start.2 = ((f32[16,8,256]{2,1,0:T(8,128)}), f32[16,8,256]{2,1,0:T(8,128)S(1)}, u32[]{:S(2)}, u32[]{:S(2)}) async-start(f32[16,8,256]{2,1,0:T(8,128)} %line.1), calls=%async_computation.2 | async-start | bytes 262144 | tf_op jit(solution)/shard_map/all_to_all | solution.py:461
  90.9 0.0 copy-done.4
  90.9 0.0 copy-start.1
  90.9 0.0 copy-start.3
  90.9 6.2 %finish.1 = (bf16[128,1024]{1,0:T(8,128)(2,1)}, bf16[128,1024]{1,0:T(8,128)(2,1)}) custom-call(s32[1]{0:T(128)S(6)} %sub.32.live_ref, bf16[128,1024]{1,0:T(8,128)(2,1)} %bitcast.16, bf16[128,1024]{1,0:T(8,128)(2,1)} %bitcast.23, f32[1,1024]{1,0:T(1,128)} %bitcast.19, bf16[16,256,128]{2,1,0:T(8,128)(2,1)} %copy-done.4, bf16[1024,1024]{1,0:T(8,128)(2,1)} %wq_ref.3, ...), custom_call_target="tpu_custom_call" | custom-call | flops 805306368 | bytes 8388608 | tf_op jit(solution)/shard_map/finish/pallas_call | solution.py:362
  97.2 1.6 %all-to-all-done.2.in_ref = f32[16,8,256]{2,1,0:T(8,128)S(1)} async-done(((f32[16,8,256]{2,1,0:T(8,128)}), f32[16,8,256]{2,1,0:T(8,128)S(1)}, u32[]{:S(2)}, u32[]{:S(2)}) %all-to-all-start.2) | async-done | bytes 131104 | tf_op jit(solution)/shard_map/all_to_all | solution.py:461
  98.7 0.0 copy-done.1
  98.7 0.0 copy-done.3
  98.7 0.8 settle.1
  (1 shorter events, 0.0 us)
Async XLA Ops:
  0.6 12.5 %collective-permute-start = (bf16[128,1024]{1,0:T(8,128)(2,1)}, bf16[128,1024]{1,0:T(8,128)(2,1)S(1)}, u32[]{:S(2)}, u32[]{:S(2)}) collective-permute-start(bf16[128,1024]{1,0:T(8,128)(2,1)} %bitcast.12), channel_id=1, source_target_pairs={{0,1},{1,2},{2,3},{3,0},{4,5},{5,6},{6,7},{7,4},{8,9},{9,10},{10,1... | collective-permute-start | bytes 786440 | tf_op jit(solution)/shard_map/ppermute | solution.py:421
  2.4 10.8 %collective-permute-start.1 = (bf16[128,1024]{1,0:T(8,128)(2,1)}, bf16[128,1024]{1,0:T(8,128)(2,1)S(1)}, u32[]{:S(2)}, u32[]{:S(2)}) collective-permute-start(bf16[128,1024]{1,0:T(8,128)(2,1)} %bitcast.13), channel_id=1, source_target_pairs={{0,2},{1,3},{2,0},{3,1},{4,6},{5,7},{6,4},{7,5},{8,10},{9,11},{10,... | collective-permute-start | bytes 786440 | tf_op jit(solution)/shard_map/ppermute | solution.py:421
  5.3 7.9 %collective-permute-start.2 = (bf16[128,1024]{1,0:T(8,128)(2,1)}, bf16[128,1024]{1,0:T(8,128)(2,1)S(1)}, u32[]{:S(2)}, u32[]{:S(2)}) collective-permute-start(bf16[128,1024]{1,0:T(8,128)(2,1)} %bitcast.14), channel_id=1, source_target_pairs={{0,3},{1,0},{2,1},{3,2},{4,7},{5,4},{6,5},{7,6},{8,11},{9,8},{10,9... | collective-permute-start | bytes 786440 | tf_op jit(solution)/shard_map/ppermute | solution.py:421
  13.0 7.0 %copy-start = (bf16[1,128,1024]{2,1,0:T(8,128)(2,1)S(1)}, bf16[1,128,1024]{2,1,0:T(8,128)(2,1)}, u32[]{:S(2)}) copy-start(bf16[1,128,1024]{2,1,0:T(8,128)(2,1)} %param.10) | copy-start | bytes 786436
  13.0 7.0 %copy-start.2 = (f32[1024]{0:T(1024)S(1)}, f32[1024]{0:T(1024)}, u32[]{:S(2)}) copy-start(f32[1024]{0:T(1024)} %param.15) | copy-start | bytes 12292
  13.1 23.7 %all-to-all-start = ((bf16[16,144,256]{2,1,0:T(8,128)(2,1)}), bf16[16,144,256]{2,1,0:T(8,128)(2,1)S(1)}, u32[]{:S(2)}, u32[]{:S(2)}) async-start(bf16[16,144,256]{2,1,0:T(8,128)(2,1)} %get-tuple-element.36), calls=%async_computation | async-start | bytes 2359296 | tf_op jit(solution)/shard_map/all_to_all | solution.py:451
  36.9 28.4 %collective-permute-start.3 = (bf16[512,1024]{1,0:T(8,128)(2,1)S(1)}, bf16[512,1024]{1,0:T(8,128)(2,1)S(1)}, u32[]{:S(2)}, u32[]{:S(2)}) collective-permute-start(bf16[512,1024]{1,0:T(8,128)(2,1)S(1)} %gather.1.n0), channel_id=1, source_target_pairs={{0,4},{1,5},{2,6},{3,7},{4,8},{5,9},{6,10},{7,11},{8,12},{9,13},{1... | collective-permute-start | bytes 3145736 | tf_op jit(solution)/shard_map/ppermute | solution.py:425
  37.0 28.3 %collective-permute-start.4 = (bf16[512,1024]{1,0:T(8,128)(2,1)S(1)}, bf16[512,1024]{1,0:T(8,128)(2,1)}, u32[]{:S(2)}, u32[]{:S(2)}) collective-permute-start(bf16[512,1024]{1,0:T(8,128)(2,1)S(1)} %gather.1.n0), channel_id=1, source_target_pairs={{0,8},{1,9},{2,10},{3,11},{4,12},{5,13},{6,14},{7,15},{8,0},{9,1},... | collective-permute-start | bytes 3145736 | tf_op jit(solution)/shard_map/ppermute | solution.py:425
  39.5 27.5 %collective-permute-start.5 = (bf16[512,1024]{1,0:T(8,128)(2,1)S(1)}, bf16[512,1024]{1,0:T(8,128)(2,1)}, u32[]{:S(2)}, u32[]{:S(2)}) collective-permute-start(bf16[512,1024]{1,0:T(8,128)(2,1)S(1)} %gather.1.n0), channel_id=1, source_target_pairs={{0,12},{1,13},{2,14},{3,15},{4,0},{5,1},{6,2},{7,3},{8,4},{9,5},{1... | collective-permute-start | bytes 3145736 | tf_op jit(solution)/shard_map/ppermute | solution.py:425
  60.9 23.0 %all-to-all-start.1 = ((bf16[16,256,128]{2,1,0:T(8,128)(2,1)}), bf16[16,256,128]{2,1,0:T(8,128)(2,1)S(1)}, u32[]{:S(2)}, u32[]{:S(2)}) async-start(bf16[16,256,128]{2,1,0:T(8,128)(2,1)} %attend.1.g0.g1.g2.g3), calls=%async_computation.1 | async-start | bytes 2097152 | tf_op jit(solution)/shard_map/all_to_all | solution.py:456
  71.4 1.5 %collective-permute-start.6 = (bf16[4,192,128]{2,1,0:T(8,128)(2,1)S(1)}, bf16[4,192,128]{2,1,0:T(8,128)(2,1)S(1)}, u32[]{:S(2)}, u32[]{:S(2)}) collective-permute-start(bf16[4,192,128]{2,1,0:T(8,128)(2,1)S(1)} %get-tuple-element.40), channel_id=1, source_target_pairs={{0,16},{16,0},{32,48},{48,32},{64,80},{80,64},{96,112},{112,96},{1... | collective-permute-start | bytes 589832 | tf_op jit(solution)/shard_map/ppermute | solution.py:433
  73.5 6.6 %collective-permute-start.7 = (bf16[192,128]{1,0:T(8,128)(2,1)S(1)}, bf16[192,128]{1,0:T(8,128)(2,1)S(1)}, u32[]{:S(2)}, u32[]{:S(2)}) collective-permute-start(bf16[192,128]{1,0:T(8,128)(2,1)S(1)} %get-tuple-element.42), channel_id=1, source_target_pairs={{0,32},{16,48},{32,64},{48,80},{64,96},{80,112},{96,0},{112,16},{1... | collective-permute-start | bytes 147464 | tf_op jit(solution)/shard_map/ppermute | solution.py:429
  75.5 6.4 %collective-permute-start.8 = (bf16[192,128]{1,0:T(8,128)(2,1)S(1)}, bf16[192,128]{1,0:T(8,128)(2,1)S(1)}, u32[]{:S(2)}, u32[]{:S(2)}) collective-permute-start(bf16[192,128]{1,0:T(8,128)(2,1)S(1)} %get-tuple-element.43), channel_id=1, source_target_pairs={{0,64},{16,80},{32,96},{48,112},{64,0},{80,16},{96,32},{112,48},{1... | collective-permute-start | bytes 147464 | tf_op jit(solution)/shard_map/ppermute | solution.py:429
  79.1 4.1 %collective-permute-start.9 = (bf16[192,128]{1,0:T(8,128)(2,1)S(1)}, bf16[192,128]{1,0:T(8,128)(2,1)S(1)}, u32[]{:S(2)}, u32[]{:S(2)}) collective-permute-start(bf16[192,128]{1,0:T(8,128)(2,1)S(1)} %get-tuple-element.44), channel_id=1, source_target_pairs={{0,96},{16,112},{32,0},{48,16},{64,32},{80,48},{96,64},{112,80},{1... | collective-permute-start | bytes 147464 | tf_op jit(solution)/shard_map/ppermute | solution.py:429
  83.9 7.0 %copy-start.4 = (bf16[16,256,128]{2,1,0:T(8,128)(2,1)}, bf16[16,256,128]{2,1,0:T(8,128)(2,1)S(1)}, u32[]{:S(2)}) copy-start(bf16[16,256,128]{2,1,0:T(8,128)(2,1)S(1)} %all-to-all-done.1.g_ref) | copy-start | bytes 3145732
  83.9 14.8 %all-to-all-start.2 = ((f32[16,8,256]{2,1,0:T(8,128)}), f32[16,8,256]{2,1,0:T(8,128)S(1)}, u32[]{:S(2)}, u32[]{:S(2)}) async-start(f32[16,8,256]{2,1,0:T(8,128)} %line.1), calls=%async_computation.2 | async-start | bytes 262144 | tf_op jit(solution)/shard_map/all_to_all | solution.py:461
  90.9 7.8 %copy-start.1 = (bf16[48,1024]{1,0:T(8,128)(2,1)S(1)}, bf16[48,1024]{1,0:T(8,128)(2,1)}, u32[]{:S(2)}) copy-start(bf16[48,1024]{1,0:T(8,128)(2,1)} %get-tuple-element.49.w_ref) | copy-start | bytes 294916
  90.9 7.8 %copy-start.3 = (f32[1024]{0:T(1024)S(1)}, f32[1024]{0:T(1024)}, u32[]{:S(2)}) copy-start(f32[1024]{0:T(1024)} %param.15) | copy-start | bytes 12292

commit v3 on v2

--- a/solution.py
+++ b/solution.py
@@ -405,24 +405,16 @@
     )(place, parts, gain, weights)
 
 
-def neighbour(first, s):
+def in_plane(a, first, move):
     pairs = []
     for i in range(128):
         spot = i % 16
         if (i // 16 % 2 == 0) == first:
-            spot = spot // 4 * 4 + (spot + s) % 4
+            spot = spot // 4 * 4 + move(spot % 4)
         else:
-            spot = (spot + 4 * s) % 16
+            spot = move(spot // 4) * 4 + spot % 4
         pairs.append((i, i // 16 * 16 + spot))
-    return pairs
-
-
-def near(a, s):
-    return lax.ppermute(a, ("dp", "list"), neighbour(True, s))
-
-
-def far(a, s):
-    return lax.ppermute(a, ("dp", "list"), neighbour(False, s))
+    return lax.ppermute(a, ("dp", "list"), pairs)
 
 
 def along_z(a, s):
@@ -440,18 +432,16 @@
     gains = gain[None]
     a, i = jnp.arange(16) // 4, jnp.arange(16) % 4
     core = part % 2
-    dx, dy = jnp.where(core == 0, a, i), jnp.where(core == 0, i, a)
-    source = 4 * ((spot // 4 - dx) % 4) + (spot % 4 - dy) % 4
+    source = spot ^ jnp.where(core == 0, 4 * a + i, 4 * i + a)
     where = jnp.concatenate([source, jnp.stack([core, part // 2])]).astype(jnp.int32)
     place = (part * 16 + spot).astype(jnp.int32)[None]
 
-    blocks = [x] + [near(x, s) for s in (1, 2, 3)]
+    blocks = [x] + [in_plane(x, True, lambda p, s=s: p ^ s) for s in (1, 2, 3)]
     packed, own_weights = project(live, place, x, cot, hist_keys[0], hist_values[0], gains, w_query, w_key, w_value)
     packed, where, *blocks = lax.optimization_barrier((packed, where, *blocks))
     packed = lax.all_to_all(packed, "list", 0, 0, tiled=True)
     normed = gather(blocks, gains)
-    normed, packed = lax.optimization_barrier((normed, packed))
-    normed = [normed] + [far(normed, s) for s in (1, 2, 3)]
+    normed = [normed] + [in_plane(normed, False, lambda p, s=s: p ^ s) for s in (1, 2, 3)]
     grads = attend(counts, hist_lengths, packed)
     back = lax.all_to_all(grads, "list", 0, 0, tiled=True)
     keep, give = weigh(where, normed, grads)

time: 100 us -> 95.2 us (0.952)
  waiting for transfers between devices: 24.3 us -> 21 us
  starting transfers between devices: 33.8 us -> 32.3 us
    all_to_all x1, waiting for transfers between devices: 16.5 us -> 11.4 us  [body(): packed = lax.all_to_all(packed, 'list', 0, 0, tiled=True)]
    ppermute x6, waiting for transfers between devices: 1.71 us -> 3.56 us  [in_plane(): return lax.ppermute(a, ('dp', 'list'), pairs)]
    all_to_all x1, starting transfers between devices: 6.18 us -> 4.4 us  [body(): packed = lax.all_to_all(packed, 'list', 0, 0, tiled=True)]
  transfers between devices with their start and end apart: 13 -> 13, of which waited for: 6 -> 7; matrix products, arithmetic and copies ran while one was open for 0% -> 0% of each run, Pallas kernels for 39% -> 41%
where the time goes in v3:
time: 95.2 us; the launch traced here: 94.8 us
  Pallas kernels  39.2 us (41%)
  starting transfers between devices  32.3 us (34%)
  waiting for transfers between devices  21 us (22%)
  between operations  2.12 us (2%)
    pallas_call x1, Pallas kernels, attend(): pl.pallas_call(attend_kernel, in_specs=[SMEM, SMEM, VMEM], out_specs=VMEM...  20.4 us
    all_to_all x1, waiting for transfers between devices, body(): packed = lax.all_to_all(packed, 'list', 0, 0, tiled=True)  11.4 us
    ppermute x6, starting transfers between devices, in_plane(): return lax.ppermute(a, ('dp', 'list'), pairs)  9.56 us
    all_to_all x1, starting transfers between devices, body(): parts = lax.all_to_all(parts, 'list', 0, 0, tiled=True)  7.21 us
    ppermute x3, starting transfers between devices, along_z(): return lax.ppermute(a, 'dp', [(i, (i + 2 * s) % 8) for i in range(8)])  6.57 us
    pallas_call x1, Pallas kernels, finish(): pl.pallas_call(finish_kernel, in_specs=[SMEM] + [WHOLE] * 4 + [ANY] * 3,...  6.24 us
    pallas_call x1, Pallas kernels, project(): pl.pallas_call(project_kernel, in_specs=[SMEM] * 2 + [WHOLE] * 5 + [ANY]...  5.68 us
    all_to_all x1, starting transfers between devices, body(): back = lax.all_to_all(grads, 'list', 0, 0, tiled=True)  4.52 us
  transfers between devices with their start and end apart: 13, of which 7 were waited for; matrix products, arithmetic and copies ran while one was open for 0% of the time, Pallas kernels for 41%

profile of v3, /device:TPU:0, one launch (start us, length us, event | category | flops | bytes accessed | tf_op | source)
XLA Modules:
  0.0 94.8 jit_solution(12337519931448964611)
XLA Ops:
  0.6 1.7 %collective-permute-start = (bf16[128,1024]{1,0:T(8,128)(2,1)}, bf16[128,1024]{1,0:T(8,128)(2,1)S(1)}, u32[]{:S(2)}, u32[]{:S(2)}) collective-permute-start(bf16[128,1024]{1,0:T(8,128)(2,1)} %bitcast.12), channel_id=1, source_target_pairs={{0,1},{1,0},{2,3},{3,2},{4,5},{5,4},{6,7},{7,6},{8,9},{9,8},{10,11... | collective-permute-start | bytes 786440 | tf_op jit(solution)/shard_map/ppermute | solution.py:417
  2.4 2.9 %collective-permute-start.1 = (bf16[128,1024]{1,0:T(8,128)(2,1)}, bf16[128,1024]{1,0:T(8,128)(2,1)S(1)}, u32[]{:S(2)}, u32[]{:S(2)}) collective-permute-start(bf16[128,1024]{1,0:T(8,128)(2,1)} %bitcast.13), channel_id=1, source_target_pairs={{0,2},{1,3},{2,0},{3,1},{4,6},{5,7},{6,4},{7,5},{8,10},{9,11},{10,... | collective-permute-start | bytes 786440 | tf_op jit(solution)/shard_map/ppermute | solution.py:417
  5.3 0.1 collective-permute-start.2
  6.1 5.7 %project.1 = (bf16[16,144,256]{2,1,0:T(8,128)(2,1)}, bf16[48,1024]{1,0:T(8,128)(2,1)}) custom-call(s32[1]{0:T(128)S(6)} %sub.17.live_ref, s32[1]{0:T(128)} %bitcast.4.place_ref, bf16[128,1024]{1,0:T(8,128)(2,1)} %bitcast.15, bf16[128,1024]{1,0:T(8,128)(2,1)} %bitcast.22, bf16[16,1024]{1,0:T(8,128)(2,1)} %bitcast.26, bf16[16,1024]{1,0:T(8,128)(2,1)} %bitcast.27, ...), custom_call_target="tpu_custom_call" | custom-call | flops 8053063680 | bytes 8388608 | tf_op jit(solution)/shard_map/project/pallas_call | solution.py:104
  11.8 0.0 copy-start
  11.8 0.0 copy-start.2
  11.8 0.1 pad_add_fusion.where_ref
  11.9 0.0 collective-permute-done.b_ref
  11.9 0.8 collective-permute-done.1.c_ref
  12.7 2.7 %collective-permute-done.2.d_ref = bf16[128,1024]{1,0:T(8,128)(2,1)S(1)} collective-permute-done((bf16[128,1024]{1,0:T(8,128)(2,1)}, bf16[128,1024]{1,0:T(8,128)(2,1)S(1)}, u32[]{:S(2)}, u32[]{:S(2)}) %collective-permute-start.2) | collective-permute-done | bytes 262176 | tf_op jit(solution)/shard_map/ppermute | solution.py:417
  15.4 4.4 %all-to-all-start = ((bf16[16,144,256]{2,1,0:T(8,128)(2,1)}), bf16[16,144,256]{2,1,0:T(8,128)(2,1)S(1)}, u32[]{:S(2)}, u32[]{:S(2)}) async-start(bf16[16,144,256]{2,1,0:T(8,128)(2,1)} %get-tuple-element.34), calls=%async_computation | async-start | bytes 2359296 | tf_op jit(solution)/shard_map/all_to_all | solution.py:442
  20.5 0.0 copy-done
  20.5 0.0 copy-done.2
  20.5 0.4 gather.1.n0
  20.9 2.0 %collective-permute-start.3 = (bf16[512,1024]{1,0:T(8,128)(2,1)S(1)}, bf16[512,1024]{1,0:T(8,128)(2,1)S(1)}, u32[]{:S(2)}, u32[]{:S(2)}) collective-permute-start(bf16[512,1024]{1,0:T(8,128)(2,1)S(1)} %gather.1.n0), channel_id=1, source_target_pairs={{0,4},{1,5},{2,6},{3,7},{4,0},{5,1},{6,2},{7,3},{8,12},{9,13},{10,... | collective-permute-start | bytes 3145736 | tf_op jit(solution)/shard_map/ppermute | solution.py:417
  22.9 2.7 %collective-permute-start.4 = (bf16[512,1024]{1,0:T(8,128)(2,1)S(1)}, bf16[512,1024]{1,0:T(8,128)(2,1)}, u32[]{:S(2)}, u32[]{:S(2)}) collective-permute-start(bf16[512,1024]{1,0:T(8,128)(2,1)S(1)} %gather.1.n0), channel_id=1, source_target_pairs={{0,8},{1,9},{2,10},{3,11},{4,12},{5,13},{6,14},{7,15},{8,0},{9,1},... | collective-permute-start | bytes 3145736 | tf_op jit(solution)/shard_map/ppermute | solution.py:417
  25.6 0.1 collective-permute-start.5
  25.7 11.4 %all-to-all-done.in_ref = bf16[16,144,256]{2,1,0:T(8,128)(2,1)S(1)} async-done(((bf16[16,144,256]{2,1,0:T(8,128)(2,1)}), bf16[16,144,256]{2,1,0:T(8,128)(2,1)S(1)}, u32[]{:S(2)}, u32[]{:S(2)}) %all-to-all-start) | async-done | bytes 1179680 | tf_op jit(solution)/shard_map/all_to_all | solution.py:442
  37.1 20.4 %attend.1.g0.g1.g2.g3 = bf16[16,256,128]{2,1,0:T(8,128)(2,1)} custom-call(s32[1]{0:T(128)S(6)} %copy.16.count_ref, s32[1]{0:T(128)S(6)} %copy.17.past_ref, bf16[16,144,256]{2,1,0:T(8,128)(2,1)S(1)} %all-to-all-done.in_ref), custom_call_target="tpu_custom_call" | custom-call | flops 14495514624 | bytes 3145728 | tf_op jit(solution)/shard_map/attend/pallas_call | solution.py:230
  57.5 4.5 %all-to-all-start.1 = ((bf16[16,256,128]{2,1,0:T(8,128)(2,1)}), bf16[16,256,128]{2,1,0:T(8,128)(2,1)S(1)}, u32[]{:S(2)}, u32[]{:S(2)}) async-start(bf16[16,256,128]{2,1,0:T(8,128)(2,1)} %attend.1.g0.g1.g2.g3), calls=%async_computation.1 | async-start | bytes 2097152 | tf_op jit(solution)/shard_map/all_to_all | solution.py:446
  62.0 0.0 collective-permute-done.3.n1
  62.1 0.0 collective-permute-done.4.n2
  62.1 0.0 collective-permute-done.5.n3
  62.1 4.3 %weigh.1 = (f32[4,192,128]{2,1,0:T(8,128)S(1)}, bf16[4,192,128]{2,1,0:T(8,128)(2,1)S(1)}) custom-call(s32[18]{0:T(128)S(1)} %pad_add_fusion.where_ref, bf16[512,1024]{1,0:T(8,128)(2,1)S(1)} %gather.1.n0, bf16[512,1024]{1,0:T(8,128)(2,1)S(1)} %collective-permute-done.3.n1, bf16[512,1024]{1,0:T(8,128)(2,1)} %collective-permute-done.4.n2, ...), custom_call_target="tpu_custom_call" | custom-call | flops 1 | bytes 1 | tf_op jit(solution)/shard_map/weigh/pallas_call | solution.py:278
  66.4 0.1 collective-permute-start.6
  66.5 1.4 %collective-permute-done.6.came_ref = bf16[4,192,128]{2,1,0:T(8,128)(2,1)S(1)} collective-permute-done((bf16[4,192,128]{2,1,0:T(8,128)(2,1)S(1)}, bf16[4,192,128]{2,1,0:T(8,128)(2,1)S(1)}, u32[]{:S(2)}, u32[]{:S(2)}) %collective-permute-start.6) | collective-permute-done | bytes 196640 | tf_op jit(solution)/shard_map/ppermute | solution.py:425
  68.0 0.6 pair.1
  68.5 2.0 %collective-permute-start.7 = (bf16[192,128]{1,0:T(8,128)(2,1)S(1)}, bf16[192,128]{1,0:T(8,128)(2,1)S(1)}, u32[]{:S(2)}, u32[]{:S(2)}) collective-permute-start(bf16[192,128]{1,0:T(8,128)(2,1)S(1)} %get-tuple-element.38), channel_id=1, source_target_pairs={{0,32},{16,48},{32,64},{48,80},{64,96},{80,112},{96,0},{112,16},{1... | collective-permute-start | bytes 147464 | tf_op jit(solution)/shard_map/ppermute | solution.py:421
  70.5 3.6 %collective-permute-start.8 = (bf16[192,128]{1,0:T(8,128)(2,1)S(1)}, bf16[192,128]{1,0:T(8,128)(2,1)S(1)}, u32[]{:S(2)}, u32[]{:S(2)}) collective-permute-start(bf16[192,128]{1,0:T(8,128)(2,1)S(1)} %get-tuple-element.39), channel_id=1, source_target_pairs={{0,64},{16,80},{32,96},{48,112},{64,0},{80,16},{96,32},{112,48},{1... | collective-permute-start | bytes 147464 | tf_op jit(solution)/shard_map/ppermute | solution.py:421
  74.1 1.0 %collective-permute-start.9 = (bf16[192,128]{1,0:T(8,128)(2,1)S(1)}, bf16[192,128]{1,0:T(8,128)(2,1)S(1)}, u32[]{:S(2)}, u32[]{:S(2)}) collective-permute-start(bf16[192,128]{1,0:T(8,128)(2,1)S(1)} %get-tuple-element.40), channel_id=1, source_target_pairs={{0,96},{16,112},{32,0},{48,16},{64,32},{80,48},{96,64},{112,80},{1... | collective-permute-start | bytes 147464 | tf_op jit(solution)/shard_map/ppermute | solution.py:421
  75.1 0.0 collective-permute-done.7.a_ref
  75.1 1.8 %collective-permute-done.8.b_ref = bf16[192,128]{1,0:T(8,128)(2,1)S(1)} collective-permute-done((bf16[192,128]{1,0:T(8,128)(2,1)S(1)}, bf16[192,128]{1,0:T(8,128)(2,1)S(1)}, u32[]{:S(2)}, u32[]{:S(2)}) %collective-permute-start.8) | collective-permute-done | bytes 49184 | tf_op jit(solution)/shard_map/ppermute | solution.py:421
  76.9 1.3 %collective-permute-done.9.c_ref = bf16[192,128]{1,0:T(8,128)(2,1)S(1)} collective-permute-done((bf16[192,128]{1,0:T(8,128)(2,1)S(1)}, bf16[192,128]{1,0:T(8,128)(2,1)S(1)}, u32[]{:S(2)}, u32[]{:S(2)}) %collective-permute-start.9) | collective-permute-done | bytes 49184 | tf_op jit(solution)/shard_map/ppermute | solution.py:421
  78.2 0.8 line.1
  79.0 0.0 all-to-all-done.1.g_ref
  79.0 0.0 copy-start.4
  79.0 7.2 %all-to-all-start.2 = ((f32[16,8,256]{2,1,0:T(8,128)}), f32[16,8,256]{2,1,0:T(8,128)S(1)}, u32[]{:S(2)}, u32[]{:S(2)}) async-start(f32[16,8,256]{2,1,0:T(8,128)} %line.1), calls=%async_computation.2 | async-start | bytes 262144 | tf_op jit(solution)/shard_map/all_to_all | solution.py:451
  86.2 0.0 copy-done.4
  86.2 0.0 copy-start.1
  86.2 0.0 copy-start.3
  86.2 6.2 %finish.1 = (bf16[128,1024]{1,0:T(8,128)(2,1)}, bf16[128,1024]{1,0:T(8,128)(2,1)}) custom-call(s32[1]{0:T(128)S(6)} %sub.17.live_ref, bf16[128,1024]{1,0:T(8,128)(2,1)} %bitcast.16, bf16[128,1024]{1,0:T(8,128)(2,1)} %bitcast.23, f32[1,1024]{1,0:T(1,128)} %bitcast.19, bf16[16,256,128]{2,1,0:T(8,128)(2,1)} %copy-done.4, bf16[1024,1024]{1,0:T(8,128)(2,1)} %wq_ref.3, ...), custom_call_target="tpu_custom_call" | custom-call | flops 805306368 | bytes 8388608 | tf_op jit(solution)/shard_map/finish/pallas_call | solution.py:362
  92.5 1.6 %all-to-all-done.2.in_ref = f32[16,8,256]{2,1,0:T(8,128)S(1)} async-done(((f32[16,8,256]{2,1,0:T(8,128)}), f32[16,8,256]{2,1,0:T(8,128)S(1)}, u32[]{:S(2)}, u32[]{:S(2)}) %all-to-all-start.2) | async-done | bytes 131104 | tf_op jit(solution)/shard_map/all_to_all | solution.py:451
  94.0 0.0 copy-done.1
  94.0 0.0 copy-done.3
  94.0 0.8 settle.1
  (1 shorter events, 0.0 us)
Async XLA Ops:
  0.6 11.3 %collective-permute-start = (bf16[128,1024]{1,0:T(8,128)(2,1)}, bf16[128,1024]{1,0:T(8,128)(2,1)S(1)}, u32[]{:S(2)}, u32[]{:S(2)}) collective-permute-start(bf16[128,1024]{1,0:T(8,128)(2,1)} %bitcast.12), channel_id=1, source_target_pairs={{0,1},{1,0},{2,3},{3,2},{4,5},{5,4},{6,7},{7,6},{8,9},{9,8},{10,11... | collective-permute-start | bytes 786440 | tf_op jit(solution)/shard_map/ppermute | solution.py:417
  2.4 10.4 %collective-permute-start.1 = (bf16[128,1024]{1,0:T(8,128)(2,1)}, bf16[128,1024]{1,0:T(8,128)(2,1)S(1)}, u32[]{:S(2)}, u32[]{:S(2)}) collective-permute-start(bf16[128,1024]{1,0:T(8,128)(2,1)} %bitcast.13), channel_id=1, source_target_pairs={{0,2},{1,3},{2,0},{3,1},{4,6},{5,7},{6,4},{7,5},{8,10},{9,11},{10,... | collective-permute-start | bytes 786440 | tf_op jit(solution)/shard_map/ppermute | solution.py:417
  5.3 10.2 %collective-permute-start.2 = (bf16[128,1024]{1,0:T(8,128)(2,1)}, bf16[128,1024]{1,0:T(8,128)(2,1)S(1)}, u32[]{:S(2)}, u32[]{:S(2)}) collective-permute-start(bf16[128,1024]{1,0:T(8,128)(2,1)} %bitcast.14), channel_id=1, source_target_pairs={{0,3},{1,2},{2,1},{3,0},{4,7},{5,6},{6,5},{7,4},{8,11},{9,10},{10,... | collective-permute-start | bytes 786440 | tf_op jit(solution)/shard_map/ppermute | solution.py:417
  11.8 8.8 %copy-start = (bf16[1,128,1024]{2,1,0:T(8,128)(2,1)S(1)}, bf16[1,128,1024]{2,1,0:T(8,128)(2,1)}, u32[]{:S(2)}) copy-start(bf16[1,128,1024]{2,1,0:T(8,128)(2,1)} %param.10) | copy-start | bytes 786436
  11.8 8.8 %copy-start.2 = (f32[1024]{0:T(1024)S(1)}, f32[1024]{0:T(1024)}, u32[]{:S(2)}) copy-start(f32[1024]{0:T(1024)} %param.15) | copy-start | bytes 12292
  15.4 21.7 %all-to-all-start = ((bf16[16,144,256]{2,1,0:T(8,128)(2,1)}), bf16[16,144,256]{2,1,0:T(8,128)(2,1)S(1)}, u32[]{:S(2)}, u32[]{:S(2)}) async-start(bf16[16,144,256]{2,1,0:T(8,128)(2,1)} %get-tuple-element.34), calls=%async_computation | async-start | bytes 2359296 | tf_op jit(solution)/shard_map/all_to_all | solution.py:442
  20.9 41.1 %collective-permute-start.3 = (bf16[512,1024]{1,0:T(8,128)(2,1)S(1)}, bf16[512,1024]{1,0:T(8,128)(2,1)S(1)}, u32[]{:S(2)}, u32[]{:S(2)}) collective-permute-start(bf16[512,1024]{1,0:T(8,128)(2,1)S(1)} %gather.1.n0), channel_id=1, source_target_pairs={{0,4},{1,5},{2,6},{3,7},{4,0},{5,1},{6,2},{7,3},{8,12},{9,13},{10,... | collective-permute-start | bytes 3145736 | tf_op jit(solution)/shard_map/ppermute | solution.py:417
  22.9 39.1 %collective-permute-start.4 = (bf16[512,1024]{1,0:T(8,128)(2,1)S(1)}, bf16[512,1024]{1,0:T(8,128)(2,1)}, u32[]{:S(2)}, u32[]{:S(2)}) collective-permute-start(bf16[512,1024]{1,0:T(8,128)(2,1)S(1)} %gather.1.n0), channel_id=1, source_target_pairs={{0,8},{1,9},{2,10},{3,11},{4,12},{5,13},{6,14},{7,15},{8,0},{9,1},... | collective-permute-start | bytes 3145736 | tf_op jit(solution)/shard_map/ppermute | solution.py:417
  25.6 36.5 %collective-permute-start.5 = (bf16[512,1024]{1,0:T(8,128)(2,1)S(1)}, bf16[512,1024]{1,0:T(8,128)(2,1)}, u32[]{:S(2)}, u32[]{:S(2)}) collective-permute-start(bf16[512,1024]{1,0:T(8,128)(2,1)S(1)} %gather.1.n0), channel_id=1, source_target_pairs={{0,12},{1,13},{2,14},{3,15},{4,8},{5,9},{6,10},{7,11},{8,4},{9,5},... | collective-permute-start | bytes 3145736 | tf_op jit(solution)/shard_map/ppermute | solution.py:417
  57.5 21.4 %all-to-all-start.1 = ((bf16[16,256,128]{2,1,0:T(8,128)(2,1)}), bf16[16,256,128]{2,1,0:T(8,128)(2,1)S(1)}, u32[]{:S(2)}, u32[]{:S(2)}) async-start(bf16[16,256,128]{2,1,0:T(8,128)(2,1)} %attend.1.g0.g1.g2.g3), calls=%async_computation.1 | async-start | bytes 2097152 | tf_op jit(solution)/shard_map/all_to_all | solution.py:446
  66.4 1.5 %collective-permute-start.6 = (bf16[4,192,128]{2,1,0:T(8,128)(2,1)S(1)}, bf16[4,192,128]{2,1,0:T(8,128)(2,1)S(1)}, u32[]{:S(2)}, u32[]{:S(2)}) collective-permute-start(bf16[4,192,128]{2,1,0:T(8,128)(2,1)S(1)} %get-tuple-element.36), channel_id=1, source_target_pairs={{0,16},{16,0},{32,48},{48,32},{64,80},{80,64},{96,112},{112,96},{1... | collective-permute-start | bytes 589832 | tf_op jit(solution)/shard_map/ppermute | solution.py:425
  68.5 6.6 %collective-permute-start.7 = (bf16[192,128]{1,0:T(8,128)(2,1)S(1)}, bf16[192,128]{1,0:T(8,128)(2,1)S(1)}, u32[]{:S(2)}, u32[]{:S(2)}) collective-permute-start(bf16[192,128]{1,0:T(8,128)(2,1)S(1)} %get-tuple-element.38), channel_id=1, source_target_pairs={{0,32},{16,48},{32,64},{48,80},{64,96},{80,112},{96,0},{112,16},{1... | collective-permute-start | bytes 147464 | tf_op jit(solution)/shard_map/ppermute | solution.py:421
  70.5 6.4 %collective-permute-start.8 = (bf16[192,128]{1,0:T(8,128)(2,1)S(1)}, bf16[192,128]{1,0:T(8,128)(2,1)S(1)}, u32[]{:S(2)}, u32[]{:S(2)}) collective-permute-start(bf16[192,128]{1,0:T(8,128)(2,1)S(1)} %get-tuple-element.39), channel_id=1, source_target_pairs={{0,64},{16,80},{32,96},{48,112},{64,0},{80,16},{96,32},{112,48},{1... | collective-permute-start | bytes 147464 | tf_op jit(solution)/shard_map/ppermute | solution.py:421
  74.1 4.1 %collective-permute-start.9 = (bf16[192,128]{1,0:T(8,128)(2,1)S(1)}, bf16[192,128]{1,0:T(8,128)(2,1)S(1)}, u32[]{:S(2)}, u32[]{:S(2)}) collective-permute-start(bf16[192,128]{1,0:T(8,128)(2,1)S(1)} %get-tuple-element.40), channel_id=1, source_target_pairs={{0,96},{16,112},{32,0},{48,16},{64,32},{80,48},{96,64},{112,80},{1... | collective-permute-start | bytes 147464 | tf_op jit(solution)/shard_map/ppermute | solution.py:421
  79.0 7.2 %copy-start.4 = (bf16[16,256,128]{2,1,0:T(8,128)(2,1)}, bf16[16,256,128]{2,1,0:T(8,128)(2,1)S(1)}, u32[]{:S(2)}) copy-start(bf16[16,256,128]{2,1,0:T(8,128)(2,1)S(1)} %all-to-all-done.1.g_ref) | copy-start | bytes 3145732
  79.0 15.1 %all-to-all-start.2 = ((f32[16,8,256]{2,1,0:T(8,128)}), f32[16,8,256]{2,1,0:T(8,128)S(1)}, u32[]{:S(2)}, u32[]{:S(2)}) async-start(f32[16,8,256]{2,1,0:T(8,128)} %line.1), calls=%async_computation.2 | async-start | bytes 262144 | tf_op jit(solution)/shard_map/all_to_all | solution.py:451
  86.2 7.8 %copy-start.1 = (bf16[48,1024]{1,0:T(8,128)(2,1)S(1)}, bf16[48,1024]{1,0:T(8,128)(2,1)}, u32[]{:S(2)}) copy-start(bf16[48,1024]{1,0:T(8,128)(2,1)} %get-tuple-element.45.w_ref) | copy-start | bytes 294916
  86.2 7.8 %copy-start.3 = (f32[1024]{0:T(1024)S(1)}, f32[1024]{0:T(1024)}, u32[]{:S(2)}) copy-start(f32[1024]{0:T(1024)} %param.15) | copy-start | bytes 12292

commit v4 on v3

--- a/solution.py
+++ b/solution.py
@@ -131,66 +131,79 @@
 
 
 QB = 256
-KC = 768
+KC = 2304
 
 
 def attend_kernel(count_ref, past_ref, in_ref, out_ref, kn_ref, vx_ref, kt_ref, vt_ref, dk_ref, dv_ref, s_ref, p_ref, d_ref):
     count = count_ref[0]
     past = past_ref[0]
     low = lanes((128, 128)) < 64
-    top = rows_of((128, 128)) == 0
+    top = rows_of((64, 128)) == 0
     ones = jnp.where(rows_of((64, 128)) < 3, 1.0, 0.0).astype(BF)
 
     for j in range(KEYS // 128):
         if j < H:
             raw = in_ref[j, :ROWS, :]
-            dead = lanes((128, 128)) + 128 * j >= count
+            dead = lanes((64, 128)) + 128 * j >= count
         else:
             t = j - H
             raw = in_ref[8 * t : 8 * t + 8, ROWS:, :].reshape(128, 256)
-            dead = lanes((128, 128)) + 128 * t >= past
+            dead = lanes((64, 128)) + 128 * t >= past
         c = slice(128 * j, 128 * j + 128)
         kn_ref[c, :] = raw[:, :128]
+        qk = raw[:, :128].astype(F32)
         vg = raw[:, 128:].astype(F32)
         vx_ref[c, :] = jnp.where(low, vg, 1.0).astype(BF)
-        kt = raw[:, :128].astype(F32).T[64:, :].astype(BF)
-        kt_ref[0:64, c] = kt
-        kt_ref[64:128, c] = kt
-        kt_ref[128:256, c] = jnp.where(top & dead, DEAD, 0.0).astype(BF)
-        vt_ref[0:64, c] = vg.T[:64, :].astype(BF)
+        turned = jnp.where(low, vg, qk).T.astype(BF)
+        vt_ref[0:64, c] = turned[:64, :]
         vt_ref[64:128, c] = ones
-    dk_ref[...] = jnp.zeros_like(dk_ref)
-    dv_ref[...] = jnp.zeros_like(dv_ref)
+        kt_ref[0:64, c] = turned[64:, :]
+        kt_ref[64:128, c] = jnp.where(top & dead, DEAD, 0.0).astype(BF)
 
     lane = lanes((QB, 128))
     lowq = lane < 64
-    unit = jnp.where(lane == 0, 1.0, 0.0).astype(BF)
-
-    def step(i, carry):
-        rows = in_ref[pl.ds(2 * i, 2), :ROWS, :].reshape(QB, 256)
-        qk = rows[:, :128].astype(F32)
-        vg = rows[:, 128:].astype(F32)
-        qs = qk * SCALE2
-        hi = qs.astype(BF).astype(F32)
-        qx = jnp.concatenate([jnp.where(lowq, hi, swap(qs - hi)).astype(BF), unit], axis=1)
-        top = None
-        for c in range(KEYS // KC):
-            cs = slice(c * KC, c * KC + KC)
-            s = dot(qx, kt_ref[:, cs])
-            s_ref[:, cs] = s
-            for h in range(KC // 128):
-                part = s[:, 128 * h : 128 * h + 128]
-                top = part if top is None else jnp.maximum(top, part)
+    unit = jnp.where(lane == 64, 1.0, 0.0)
+
+    blocks = CAND // QB
+    chunks = [slice(c, c + KC) for c in range(0, KEYS, KC)]
+
+    def load(i):
+        rows = in_ref[2 * i : 2 * i + 2, :ROWS, :].reshape(QB, 256)
+        return rows[:, :128].astype(F32), rows[:, 128:].astype(F32)
+
+    def scores(i, qx, cs, top):
+        s = dot(qx, kt_ref[:, cs])
+        s_ref[i % 2, :, cs] = s
+        for h in range(KC // 128):
+            part = s[:, 128 * h : 128 * h + 128]
+            top = part if top is None else jnp.maximum(top, part)
+        return top
+
+    def left(qk):
+        return jnp.where(lowq, qk, unit).astype(BF)
+
+    def collect(i, turned, cs):
+        dk, dv = dot(turned[64:, :], d_ref[i % 2, :, cs]), dot(turned[:64, :], p_ref[i % 2, :, cs])
+        dk_ref[:, cs] = dk if i == 0 else dk_ref[:, cs] + dk
+        dv_ref[:, cs] = dv if i == 0 else dv_ref[:, cs] + dv
+
+    qk, vg = load(0)
+    qx, top = left(qk), None
+    for cs in chunks:
+        top = scores(0, qx, cs, top)
+    turned = None
+    for i in range(blocks):
         top = jnp.max(top, axis=1, keepdims=True)
         pv = None
-        for c in range(KEYS // KC):
-            cs = slice(c * KC, c * KC + KC)
-            e = jnp.exp2(s_ref[:, cs] - top)
-            s_ref[:, cs] = e
+        for cs in chunks:
+            e = jnp.exp2((s_ref[i % 2, :, cs] - top) * SCALE2)
+            s_ref[i % 2, :, cs] = e
             e = e.astype(BF)
-            p_ref[:, cs] = e
-            t = dot(e, vx_ref[cs, :])
-            pv = t if pv is None else pv + t
+            p_ref[i % 2, :, cs] = e
+            part = dot(e, vx_ref[cs, :])
+            pv = part if pv is None else pv + part
+            if i > 0:
+                collect(i - 1, turned, cs)
         inv = 1.0 / jnp.where(lowq, swap(pv), 1.0)
         mixed = pv * inv
         g = (swap(vg) * inv).astype(BF)
@@ -201,25 +214,25 @@
         r3 = rd - r1 - r2
         gx = jnp.where(lane == 64, -r1, jnp.where(lane == 65, -r2, jnp.where(lane == 66, -r3, 0.0)))
         gx = jnp.where(lowq, gf, gx).astype(BF)
-        gq = None
-        for c in range(KEYS // KC):
-            cs = slice(c * KC, c * KC + KC)
-            ds = (s_ref[:, cs] * dot(gx, vt_ref[:, cs])).astype(BF)
-            d_ref[:, cs] = ds
-            t = dot(ds, kn_ref[cs, :])
-            gq = t if gq is None else gq + t
+        turned = jnp.where(lowq, gf, swap(qk)).T.astype(BF)
+        more = i + 1 < blocks
+        if more:
+            qk, vg = load(i + 1)
+            qx = left(qk)
+        gq, top = None, None
+        for cs in chunks:
+            dp = dot(gx, vt_ref[:, cs])
+            if more:
+                top = scores(i + 1, qx, cs, top)
+            ds = (s_ref[i % 2, :, cs] * dp).astype(BF)
+            d_ref[i % 2, :, cs] = ds
+            part = dot(ds, kn_ref[cs, :])
+            gq = part if gq is None else gq + part
         both = jnp.where(lowq, mixed, gq * SCALE).T.astype(BF)
         out_ref[2 * i, 0:128, :] = both[:, :128]
         out_ref[2 * i + 1, 0:128, :] = both[:, 128:]
-        qt = qk.T[:64, :].astype(BF)
-        gt = gf.T[:64, :].astype(BF)
-        for c in range(KEYS // KC):
-            cs = slice(c * KC, c * KC + KC)
-            dk_ref[:, cs] += dot(qt, d_ref[:, cs])
-            dv_ref[:, cs] += dot(gt, p_ref[:, cs])
-        return carry
-
-    lax.fori_loop(0, CAND // QB, step, 0)
+    for cs in chunks:
+        collect(blocks - 1, turned, cs)
     for j in range(H):
         c = slice(128 * j, 128 * j + 128)
         out_ref[j, 128:192, :] = (dk_ref[:, c] * SCALE).astype(BF)
@@ -235,13 +248,13 @@
         scratch_shapes=[
             pltpu.VMEM((KEYS, 128), BF),
             pltpu.VMEM((KEYS, 128), BF),
-            pltpu.VMEM((256, KEYS), BF),
+            pltpu.VMEM((128, KEYS), BF),
             pltpu.VMEM((128, KEYS), BF),
             pltpu.VMEM((64, KEYS), F32),
             pltpu.VMEM((64, KEYS), F32),
-            pltpu.VMEM((QB, KEYS), F32),
-            pltpu.VMEM((QB, KEYS), BF),
-            pltpu.VMEM((QB, KEYS), BF),
+            pltpu.VMEM((2, QB, KEYS), F32),
+            pltpu.VMEM((2, QB, KEYS), BF),
+            pltpu.VMEM((2, QB, KEYS), BF),
         ],
         compiler_params=pltpu.CompilerParams(vmem_limit_bytes=24 * MIB),
         cost_estimate=pl.CostEstimate(flops=12 * CAND * KEYS * 256, bytes_accessed=3 * MIB, transcendentals=CAND * KEYS),

time: 95.2 us -> 90.3 us (0.949)
  Pallas kernels: 39.2 us -> 34.2 us
    pallas_call x1, Pallas kernels: 20.4 us -> 15.5 us  [attend(): pl.pallas_call(attend_kernel, in_specs=[SMEM, SMEM, VMEM], out_specs=VMEM...]
  transfers between devices with their start and end apart: 13 -> 13, of which waited for: 7 -> 8; matrix products, arithmetic and copies ran while one was open for 0% -> 0% of each run, Pallas kernels for 41% -> 37%
where the time goes in v4:
time: 90.3 us; the launch traced here: 89.8 us
  Pallas kernels  34.2 us (38%)
  starting transfers between devices  32.2 us (36%)
  waiting for transfers between devices  21.2 us (23%)
  between operations  2.1 us (2%)
    pallas_call x1, Pallas kernels, attend(): pl.pallas_call(attend_kernel, in_specs=[SMEM, SMEM, VMEM], out_specs=VMEM...  15.5 us
    all_to_all x1, waiting for transfers between devices, body(): packed = lax.all_to_all(packed, 'list', 0, 0, tiled=True)  11.4 us
    ppermute x6, starting transfers between devices, in_plane(): return lax.ppermute(a, ('dp', 'list'), pairs)  9.56 us
    ppermute x3, starting transfers between devices, along_z(): return lax.ppermute(a, 'dp', [(i, (i + 2 * s) % 8) for i in range(8)])  6.59 us
    all_to_all x1, starting transfers between devices, body(): parts = lax.all_to_all(parts, 'list', 0, 0, tiled=True)  6.5 us
    pallas_call x1, Pallas kernels, finish(): pl.pallas_call(finish_kernel, in_specs=[SMEM] + [WHOLE] * 4 + [ANY] * 3,...  6.24 us
    pallas_call x1, Pallas kernels, project(): pl.pallas_call(project_kernel, in_specs=[SMEM] * 2 + [WHOLE] * 5 + [ANY]...  5.68 us
    all_to_all x1, starting transfers between devices, body(): back = lax.all_to_all(grads, 'list', 0, 0, tiled=True)  4.53 us
  transfers between devices with their start and end apart: 13, of which 8 were waited for; matrix products, arithmetic and copies ran while one was open for 0% of the time, Pallas kernels for 37%

profile of v4, /device:TPU:0, one launch (start us, length us, event | category | flops | bytes accessed | tf_op | source)
XLA Modules:
  0.0 89.8 jit_solution(11392326309571900183)
XLA Ops:
  0.6 1.7 %collective-permute-start = (bf16[128,1024]{1,0:T(8,128)(2,1)}, bf16[128,1024]{1,0:T(8,128)(2,1)S(1)}, u32[]{:S(2)}, u32[]{:S(2)}) collective-permute-start(bf16[128,1024]{1,0:T(8,128)(2,1)} %bitcast.12), channel_id=1, source_target_pairs={{0,1},{1,0},{2,3},{3,2},{4,5},{5,4},{6,7},{7,6},{8,9},{9,8},{10,11... | collective-permute-start | bytes 786440 | tf_op jit(solution)/shard_map/ppermute | solution.py:430
  2.4 2.9 %collective-permute-start.1 = (bf16[128,1024]{1,0:T(8,128)(2,1)}, bf16[128,1024]{1,0:T(8,128)(2,1)S(1)}, u32[]{:S(2)}, u32[]{:S(2)}) collective-permute-start(bf16[128,1024]{1,0:T(8,128)(2,1)} %bitcast.13), channel_id=1, source_target_pairs={{0,2},{1,3},{2,0},{3,1},{4,6},{5,7},{6,4},{7,5},{8,10},{9,11},{10,... | collective-permute-start | bytes 786440 | tf_op jit(solution)/shard_map/ppermute | solution.py:430
  5.3 0.1 collective-permute-start.2
  6.1 5.7 %project.1 = (bf16[16,144,256]{2,1,0:T(8,128)(2,1)}, bf16[48,1024]{1,0:T(8,128)(2,1)}) custom-call(s32[1]{0:T(128)S(6)} %sub.17.live_ref, s32[1]{0:T(128)} %bitcast.4.place_ref, bf16[128,1024]{1,0:T(8,128)(2,1)} %bitcast.15, bf16[128,1024]{1,0:T(8,128)(2,1)} %bitcast.22, bf16[16,1024]{1,0:T(8,128)(2,1)} %bitcast.26, bf16[16,1024]{1,0:T(8,128)(2,1)} %bitcast.27, ...), custom_call_target="tpu_custom_call" | custom-call | flops 8053063680 | bytes 8388608 | tf_op jit(solution)/shard_map/project/pallas_call | solution.py:104
  11.8 0.0 copy-start
  11.8 0.0 copy-start.2
  11.8 0.1 pad_add_fusion.where_ref
  11.9 0.0 collective-permute-done.b_ref
  11.9 0.8 collective-permute-done.1.c_ref
  12.7 2.7 %collective-permute-done.2.d_ref = bf16[128,1024]{1,0:T(8,128)(2,1)S(1)} collective-permute-done((bf16[128,1024]{1,0:T(8,128)(2,1)}, bf16[128,1024]{1,0:T(8,128)(2,1)S(1)}, u32[]{:S(2)}, u32[]{:S(2)}) %collective-permute-start.2) | collective-permute-done | bytes 262176 | tf_op jit(solution)/shard_map/ppermute | solution.py:430
  15.4 4.4 %all-to-all-start = ((bf16[16,144,256]{2,1,0:T(8,128)(2,1)}), bf16[16,144,256]{2,1,0:T(8,128)(2,1)S(1)}, u32[]{:S(2)}, u32[]{:S(2)}) async-start(bf16[16,144,256]{2,1,0:T(8,128)(2,1)} %get-tuple-element.34), calls=%async_computation | async-start | bytes 2359296 | tf_op jit(solution)/shard_map/all_to_all | solution.py:455
  20.5 0.0 copy-done
  20.5 0.0 copy-done.2
  20.5 0.4 gather.1.n0
  20.9 2.0 %collective-permute-start.3 = (bf16[512,1024]{1,0:T(8,128)(2,1)S(1)}, bf16[512,1024]{1,0:T(8,128)(2,1)S(1)}, u32[]{:S(2)}, u32[]{:S(2)}) collective-permute-start(bf16[512,1024]{1,0:T(8,128)(2,1)S(1)} %gather.1.n0), channel_id=1, source_target_pairs={{0,4},{1,5},{2,6},{3,7},{4,0},{5,1},{6,2},{7,3},{8,12},{9,13},{10,... | collective-permute-start | bytes 3145736 | tf_op jit(solution)/shard_map/ppermute | solution.py:430
  22.9 2.7 %collective-permute-start.4 = (bf16[512,1024]{1,0:T(8,128)(2,1)S(1)}, bf16[512,1024]{1,0:T(8,128)(2,1)}, u32[]{:S(2)}, u32[]{:S(2)}) collective-permute-start(bf16[512,1024]{1,0:T(8,128)(2,1)S(1)} %gather.1.n0), channel_id=1, source_target_pairs={{0,8},{1,9},{2,10},{3,11},{4,12},{5,13},{6,14},{7,15},{8,0},{9,1},... | collective-permute-start | bytes 3145736 | tf_op jit(solution)/shard_map/ppermute | solution.py:430
  25.6 0.1 collective-permute-start.5
  25.7 11.4 %all-to-all-done.in_ref = bf16[16,144,256]{2,1,0:T(8,128)(2,1)S(1)} async-done(((bf16[16,144,256]{2,1,0:T(8,128)(2,1)}), bf16[16,144,256]{2,1,0:T(8,128)(2,1)S(1)}, u32[]{:S(2)}, u32[]{:S(2)}) %all-to-all-start) | async-done | bytes 1179680 | tf_op jit(solution)/shard_map/all_to_all | solution.py:455
  37.1 15.5 %attend.1.g0.g1.g2.g3 = bf16[16,256,128]{2,1,0:T(8,128)(2,1)} custom-call(s32[1]{0:T(128)S(6)} %copy.16.count_ref, s32[1]{0:T(128)S(6)} %copy.17.past_ref, bf16[16,144,256]{2,1,0:T(8,128)(2,1)S(1)} %all-to-all-done.in_ref), custom_call_target="tpu_custom_call" | custom-call | flops 14495514624 | bytes 3145728 | tf_op jit(solution)/shard_map/attend/pallas_call | solution.py:243
  52.6 4.5 %all-to-all-start.1 = ((bf16[16,256,128]{2,1,0:T(8,128)(2,1)}), bf16[16,256,128]{2,1,0:T(8,128)(2,1)S(1)}, u32[]{:S(2)}, u32[]{:S(2)}) async-start(bf16[16,256,128]{2,1,0:T(8,128)(2,1)} %attend.1.g0.g1.g2.g3), calls=%async_computation.1 | async-start | bytes 2097152 | tf_op jit(solution)/shard_map/all_to_all | solution.py:459
  57.1 0.0 collective-permute-done.3.n1
  57.1 0.5 collective-permute-done.4.n2
  57.6 0.0 collective-permute-done.5.n3
  57.6 4.3 %weigh.1 = (f32[4,192,128]{2,1,0:T(8,128)S(1)}, bf16[4,192,128]{2,1,0:T(8,128)(2,1)S(1)}) custom-call(s32[18]{0:T(128)S(1)} %pad_add_fusion.where_ref, bf16[512,1024]{1,0:T(8,128)(2,1)S(1)} %gather.1.n0, bf16[512,1024]{1,0:T(8,128)(2,1)S(1)} %collective-permute-done.3.n1, bf16[512,1024]{1,0:T(8,128)(2,1)} %collective-permute-done.4.n2, ...), custom_call_target="tpu_custom_call" | custom-call | flops 1 | bytes 1 | tf_op jit(solution)/shard_map/weigh/pallas_call | solution.py:291
  62.0 0.7 collective-permute-start.6
  62.6 1.1 %collective-permute-done.6.came_ref = bf16[4,192,128]{2,1,0:T(8,128)(2,1)S(1)} collective-permute-done((bf16[4,192,128]{2,1,0:T(8,128)(2,1)S(1)}, bf16[4,192,128]{2,1,0:T(8,128)(2,1)S(1)}, u32[]{:S(2)}, u32[]{:S(2)}) %collective-permute-start.6) | collective-permute-done | bytes 196640 | tf_op jit(solution)/shard_map/ppermute | solution.py:438
  63.7 0.6 pair.1
  64.3 2.0 %collective-permute-start.7 = (bf16[192,128]{1,0:T(8,128)(2,1)S(1)}, bf16[192,128]{1,0:T(8,128)(2,1)S(1)}, u32[]{:S(2)}, u32[]{:S(2)}) collective-permute-start(bf16[192,128]{1,0:T(8,128)(2,1)S(1)} %get-tuple-element.38), channel_id=1, source_target_pairs={{0,32},{16,48},{32,64},{48,80},{64,96},{80,112},{96,0},{112,16},{1... | collective-permute-start | bytes 147464 | tf_op jit(solution)/shard_map/ppermute | solution.py:434
  66.3 3.6 %collective-permute-start.8 = (bf16[192,128]{1,0:T(8,128)(2,1)S(1)}, bf16[192,128]{1,0:T(8,128)(2,1)S(1)}, u32[]{:S(2)}, u32[]{:S(2)}) collective-permute-start(bf16[192,128]{1,0:T(8,128)(2,1)S(1)} %get-tuple-element.39), channel_id=1, source_target_pairs={{0,64},{16,80},{32,96},{48,112},{64,0},{80,16},{96,32},{112,48},{1... | collective-permute-start | bytes 147464 | tf_op jit(solution)/shard_map/ppermute | solution.py:434
  69.9 1.0 %collective-permute-start.9 = (bf16[192,128]{1,0:T(8,128)(2,1)S(1)}, bf16[192,128]{1,0:T(8,128)(2,1)S(1)}, u32[]{:S(2)}, u32[]{:S(2)}) collective-permute-start(bf16[192,128]{1,0:T(8,128)(2,1)S(1)} %get-tuple-element.40), channel_id=1, source_target_pairs={{0,96},{16,112},{32,0},{48,16},{64,32},{80,48},{96,64},{112,80},{1... | collective-permute-start | bytes 147464 | tf_op jit(solution)/shard_map/ppermute | solution.py:434
  70.9 0.0 collective-permute-done.7.a_ref
  70.9 2.0 %collective-permute-done.8.b_ref = bf16[192,128]{1,0:T(8,128)(2,1)S(1)} collective-permute-done((bf16[192,128]{1,0:T(8,128)(2,1)S(1)}, bf16[192,128]{1,0:T(8,128)(2,1)S(1)}, u32[]{:S(2)}, u32[]{:S(2)}) %collective-permute-start.8) | collective-permute-done | bytes 49184 | tf_op jit(solution)/shard_map/ppermute | solution.py:434
  72.9 1.1 %collective-permute-done.9.c_ref = bf16[192,128]{1,0:T(8,128)(2,1)S(1)} collective-permute-done((bf16[192,128]{1,0:T(8,128)(2,1)S(1)}, bf16[192,128]{1,0:T(8,128)(2,1)S(1)}, u32[]{:S(2)}, u32[]{:S(2)}) %collective-permute-start.9) | collective-permute-done | bytes 49184 | tf_op jit(solution)/shard_map/ppermute | solution.py:434
  74.0 0.8 line.1
  74.7 0.0 all-to-all-done.1.g_ref
  74.7 0.0 copy-start.4
  74.7 6.5 %all-to-all-start.2 = ((f32[16,8,256]{2,1,0:T(8,128)}), f32[16,8,256]{2,1,0:T(8,128)S(1)}, u32[]{:S(2)}, u32[]{:S(2)}) async-start(f32[16,8,256]{2,1,0:T(8,128)} %line.1), calls=%async_computation.2 | async-start | bytes 262144 | tf_op jit(solution)/shard_map/all_to_all | solution.py:464
  81.2 0.0 copy-done.4
  81.2 0.0 copy-start.1
  81.2 0.0 copy-start.3
  81.3 6.2 %finish.1 = (bf16[128,1024]{1,0:T(8,128)(2,1)}, bf16[128,1024]{1,0:T(8,128)(2,1)}) custom-call(s32[1]{0:T(128)S(6)} %sub.17.live_ref, bf16[128,1024]{1,0:T(8,128)(2,1)} %bitcast.16, bf16[128,1024]{1,0:T(8,128)(2,1)} %bitcast.23, f32[1,1024]{1,0:T(1,128)} %bitcast.19, bf16[16,256,128]{2,1,0:T(8,128)(2,1)} %copy-done.4, bf16[1024,1024]{1,0:T(8,128)(2,1)} %wq_ref.3, ...), custom_call_target="tpu_custom_call" | custom-call | flops 805306368 | bytes 8388608 | tf_op jit(solution)/shard_map/finish/pallas_call | solution.py:375
  87.5 1.6 %all-to-all-done.2.in_ref = f32[16,8,256]{2,1,0:T(8,128)S(1)} async-done(((f32[16,8,256]{2,1,0:T(8,128)}), f32[16,8,256]{2,1,0:T(8,128)S(1)}, u32[]{:S(2)}, u32[]{:S(2)}) %all-to-all-start.2) | async-done | bytes 131104 | tf_op jit(solution)/shard_map/all_to_all | solution.py:464
  89.1 0.0 copy-done.1
  89.1 0.0 copy-done.3
  89.1 0.8 settle.1
  (1 shorter events, 0.0 us)
Async XLA Ops:
  0.6 11.3 %collective-permute-start = (bf16[128,1024]{1,0:T(8,128)(2,1)}, bf16[128,1024]{1,0:T(8,128)(2,1)S(1)}, u32[]{:S(2)}, u32[]{:S(2)}) collective-permute-start(bf16[128,1024]{1,0:T(8,128)(2,1)} %bitcast.12), channel_id=1, source_target_pairs={{0,1},{1,0},{2,3},{3,2},{4,5},{5,4},{6,7},{7,6},{8,9},{9,8},{10,11... | collective-permute-start | bytes 786440 | tf_op jit(solution)/shard_map/ppermute | solution.py:430
  2.4 10.4 %collective-permute-start.1 = (bf16[128,1024]{1,0:T(8,128)(2,1)}, bf16[128,1024]{1,0:T(8,128)(2,1)S(1)}, u32[]{:S(2)}, u32[]{:S(2)}) collective-permute-start(bf16[128,1024]{1,0:T(8,128)(2,1)} %bitcast.13), channel_id=1, source_target_pairs={{0,2},{1,3},{2,0},{3,1},{4,6},{5,7},{6,4},{7,5},{8,10},{9,11},{10,... | collective-permute-start | bytes 786440 | tf_op jit(solution)/shard_map/ppermute | solution.py:430
  5.3 10.2 %collective-permute-start.2 = (bf16[128,1024]{1,0:T(8,128)(2,1)}, bf16[128,1024]{1,0:T(8,128)(2,1)S(1)}, u32[]{:S(2)}, u32[]{:S(2)}) collective-permute-start(bf16[128,1024]{1,0:T(8,128)(2,1)} %bitcast.14), channel_id=1, source_target_pairs={{0,3},{1,2},{2,1},{3,0},{4,7},{5,6},{6,5},{7,4},{8,11},{9,10},{10,... | collective-permute-start | bytes 786440 | tf_op jit(solution)/shard_map/ppermute | solution.py:430
  11.8 8.8 %copy-start = (bf16[1,128,1024]{2,1,0:T(8,128)(2,1)S(1)}, bf16[1,128,1024]{2,1,0:T(8,128)(2,1)}, u32[]{:S(2)}) copy-start(bf16[1,128,1024]{2,1,0:T(8,128)(2,1)} %param.10) | copy-start | bytes 786436
  11.8 8.8 %copy-start.2 = (f32[1024]{0:T(1024)S(1)}, f32[1024]{0:T(1024)}, u32[]{:S(2)}) copy-start(f32[1024]{0:T(1024)} %param.15) | copy-start | bytes 12292
  15.4 21.7 %all-to-all-start = ((bf16[16,144,256]{2,1,0:T(8,128)(2,1)}), bf16[16,144,256]{2,1,0:T(8,128)(2,1)S(1)}, u32[]{:S(2)}, u32[]{:S(2)}) async-start(bf16[16,144,256]{2,1,0:T(8,128)(2,1)} %get-tuple-element.34), calls=%async_computation | async-start | bytes 2359296 | tf_op jit(solution)/shard_map/all_to_all | solution.py:455
  20.9 36.2 %collective-permute-start.3 = (bf16[512,1024]{1,0:T(8,128)(2,1)S(1)}, bf16[512,1024]{1,0:T(8,128)(2,1)S(1)}, u32[]{:S(2)}, u32[]{:S(2)}) collective-permute-start(bf16[512,1024]{1,0:T(8,128)(2,1)S(1)} %gather.1.n0), channel_id=1, source_target_pairs={{0,4},{1,5},{2,6},{3,7},{4,0},{5,1},{6,2},{7,3},{8,12},{9,13},{10,... | collective-permute-start | bytes 3145736 | tf_op jit(solution)/shard_map/ppermute | solution.py:430
  22.9 34.7 %collective-permute-start.4 = (bf16[512,1024]{1,0:T(8,128)(2,1)S(1)}, bf16[512,1024]{1,0:T(8,128)(2,1)}, u32[]{:S(2)}, u32[]{:S(2)}) collective-permute-start(bf16[512,1024]{1,0:T(8,128)(2,1)S(1)} %gather.1.n0), channel_id=1, source_target_pairs={{0,8},{1,9},{2,10},{3,11},{4,12},{5,13},{6,14},{7,15},{8,0},{9,1},... | collective-permute-start | bytes 3145736 | tf_op jit(solution)/shard_map/ppermute | solution.py:430
  25.6 32.0 %collective-permute-start.5 = (bf16[512,1024]{1,0:T(8,128)(2,1)S(1)}, bf16[512,1024]{1,0:T(8,128)(2,1)}, u32[]{:S(2)}, u32[]{:S(2)}) collective-permute-start(bf16[512,1024]{1,0:T(8,128)(2,1)S(1)} %gather.1.n0), channel_id=1, source_target_pairs={{0,12},{1,13},{2,14},{3,15},{4,8},{5,9},{6,10},{7,11},{8,4},{9,5},... | collective-permute-start | bytes 3145736 | tf_op jit(solution)/shard_map/ppermute | solution.py:430
  52.6 22.1 %all-to-all-start.1 = ((bf16[16,256,128]{2,1,0:T(8,128)(2,1)}), bf16[16,256,128]{2,1,0:T(8,128)(2,1)S(1)}, u32[]{:S(2)}, u32[]{:S(2)}) async-start(bf16[16,256,128]{2,1,0:T(8,128)(2,1)} %attend.1.g0.g1.g2.g3), calls=%async_computation.1 | async-start | bytes 2097152 | tf_op jit(solution)/shard_map/all_to_all | solution.py:459
  62.0 1.7 %collective-permute-start.6 = (bf16[4,192,128]{2,1,0:T(8,128)(2,1)S(1)}, bf16[4,192,128]{2,1,0:T(8,128)(2,1)S(1)}, u32[]{:S(2)}, u32[]{:S(2)}) collective-permute-start(bf16[4,192,128]{2,1,0:T(8,128)(2,1)S(1)} %get-tuple-element.36), channel_id=1, source_target_pairs={{0,16},{16,0},{32,48},{48,32},{64,80},{80,64},{96,112},{112,96},{1... | collective-permute-start | bytes 589832 | tf_op jit(solution)/shard_map/ppermute | solution.py:438
  64.3 6.6 %collective-permute-start.7 = (bf16[192,128]{1,0:T(8,128)(2,1)S(1)}, bf16[192,128]{1,0:T(8,128)(2,1)S(1)}, u32[]{:S(2)}, u32[]{:S(2)}) collective-permute-start(bf16[192,128]{1,0:T(8,128)(2,1)S(1)} %get-tuple-element.38), channel_id=1, source_target_pairs={{0,32},{16,48},{32,64},{48,80},{64,96},{80,112},{96,0},{112,16},{1... | collective-permute-start | bytes 147464 | tf_op jit(solution)/shard_map/ppermute | solution.py:434
  66.3 6.6 %collective-permute-start.8 = (bf16[192,128]{1,0:T(8,128)(2,1)S(1)}, bf16[192,128]{1,0:T(8,128)(2,1)S(1)}, u32[]{:S(2)}, u32[]{:S(2)}) collective-permute-start(bf16[192,128]{1,0:T(8,128)(2,1)S(1)} %get-tuple-element.39), channel_id=1, source_target_pairs={{0,64},{16,80},{32,96},{48,112},{64,0},{80,16},{96,32},{112,48},{1... | collective-permute-start | bytes 147464 | tf_op jit(solution)/shard_map/ppermute | solution.py:434
  69.9 4.1 %collective-permute-start.9 = (bf16[192,128]{1,0:T(8,128)(2,1)S(1)}, bf16[192,128]{1,0:T(8,128)(2,1)S(1)}, u32[]{:S(2)}, u32[]{:S(2)}) collective-permute-start(bf16[192,128]{1,0:T(8,128)(2,1)S(1)} %get-tuple-element.40), channel_id=1, source_target_pairs={{0,96},{16,112},{32,0},{48,16},{64,32},{80,48},{96,64},{112,80},{1... | collective-permute-start | bytes 147464 | tf_op jit(solution)/shard_map/ppermute | solution.py:434
  74.7 6.5 %copy-start.4 = (bf16[16,256,128]{2,1,0:T(8,128)(2,1)}, bf16[16,256,128]{2,1,0:T(8,128)(2,1)S(1)}, u32[]{:S(2)}) copy-start(bf16[16,256,128]{2,1,0:T(8,128)(2,1)S(1)} %all-to-all-done.1.g_ref) | copy-start | bytes 3145732
  74.7 14.3 %all-to-all-start.2 = ((f32[16,8,256]{2,1,0:T(8,128)}), f32[16,8,256]{2,1,0:T(8,128)S(1)}, u32[]{:S(2)}, u32[]{:S(2)}) async-start(f32[16,8,256]{2,1,0:T(8,128)} %line.1), calls=%async_computation.2 | async-start | bytes 262144 | tf_op jit(solution)/shard_map/all_to_all | solution.py:464
  81.2 7.8 %copy-start.1 = (bf16[48,1024]{1,0:T(8,128)(2,1)S(1)}, bf16[48,1024]{1,0:T(8,128)(2,1)}, u32[]{:S(2)}) copy-start(bf16[48,1024]{1,0:T(8,128)(2,1)} %get-tuple-element.45.w_ref) | copy-start | bytes 294916
  81.2 7.8 %copy-start.3 = (f32[1024]{0:T(1024)S(1)}, f32[1024]{0:T(1024)}, u32[]{:S(2)}) copy-start(f32[1024]{0:T(1024)} %param.15) | copy-start | bytes 12292

commit v5 on v4

--- a/solution.py
+++ b/solution.py
@@ -221,9 +221,9 @@
             qx = left(qk)
         gq, top = None, None
         for cs in chunks:
-            dp = dot(gx, vt_ref[:, cs])
             if more:
                 top = scores(i + 1, qx, cs, top)
+            dp = dot(gx, vt_ref[:, cs])
             ds = (s_ref[i % 2, :, cs] * dp).astype(BF)
             d_ref[i % 2, :, cs] = ds
             part = dot(ds, kn_ref[cs, :])
@@ -262,9 +262,9 @@
     )(count, past, packed)
 
 
-def weigh_kernel(where_ref, n0, n1, n2, n3, g0, g1, g2, g3, keep_ref, give_ref, acc_ref):
+def weigh_kernel(where_ref, n0, n1, n2, n3, g0, g1, g2, g3, g4, g5, g6, g7, keep_ref, give_ref, acc_ref):
     i = pl.program_id(0)
-    left = jnp.concatenate([g[0, 64:, :] for g in (g0, g1, g2, g3)], axis=1)
+    left = jnp.concatenate([g[0, 64:, :] for g in (g0, g1, g2, g3, g4, g5, g6, g7)], axis=1)
     right = jnp.concatenate([n[...] for n in (n0, n1, n2, n3)], axis=0)
     part = dot(left, right)
 
@@ -292,9 +292,9 @@
         weigh_kernel,
         grid_spec=pltpu.PrefetchScalarGridSpec(
             num_scalar_prefetch=1,
-            grid=(4,),
-            in_specs=[pl.BlockSpec((ROWS, D), lambda i, w: (i, 0))] * 4
-            + [pl.BlockSpec((1, 256, ROWS), lambda i, w, a=a: (w[4 * a + i], 0, 0)) for a in range(4)],
+            grid=(2,),
+            in_specs=[pl.BlockSpec((2 * ROWS, D), lambda i, w: (i, 0))] * 4
+            + [pl.BlockSpec((1, 256, ROWS), lambda i, w, a=a: (w[a // 2 * 4 + 2 * i + a % 2], 0, 0)) for a in range(8)],
             out_specs=[pl.BlockSpec((4, 192, 128), fixed), pl.BlockSpec((4, 192, 128), fixed)],
             scratch_shapes=[pltpu.VMEM((192, D), F32)],
         ),
@@ -302,7 +302,7 @@
         compiler_params=pltpu.CompilerParams(vmem_limit_bytes=24 * MIB),
         cost_estimate=SOON,
         name="weigh",
-    )(where, *normed, *([grads] * 4))
+    )(where, *normed, *([grads] * 8))
 
 
 def pair_kernel(where_ref, keep_ref, came_ref, own_ref, a_ref, b_ref, c_ref):

time: 90.3 us -> 88.8 us (0.983)
  Pallas kernels: 34.2 us -> 32.8 us
    all_to_all x1, starting transfers between devices: 6.5 us -> 5.17 us  [body(): parts = lax.all_to_all(parts, 'list', 0, 0, tiled=True)]
  transfers between devices with their start and end apart: 13 -> 13, of which waited for: 8 -> 8; matrix products, arithmetic and copies ran while one was open for 0% -> 0% of each run, Pallas kernels for 37% -> 36%
where the time goes in v5:
time: 88.8 us; the launch traced here: 88.4 us
  Pallas kernels  32.8 us (37%)
  starting transfers between devices  31.6 us (36%)
  waiting for transfers between devices  21.8 us (25%)
  between operations  2.1 us (2%)
    pallas_call x1, Pallas kernels, attend(): pl.pallas_call(attend_kernel, in_specs=[SMEM, SMEM, VMEM], out_specs=VMEM...  14.8 us
    all_to_all x1, waiting for transfers between devices, body(): packed = lax.all_to_all(packed, 'list', 0, 0, tiled=True)  11.4 us
    ppermute x6, starting transfers between devices, in_plane(): return lax.ppermute(a, ('dp', 'list'), pairs)  9.56 us
    ppermute x3, starting transfers between devices, along_z(): return lax.ppermute(a, 'dp', [(i, (i + 2 * s) % 8) for i in range(8)])  6.59 us
    pallas_call x1, Pallas kernels, finish(): pl.pallas_call(finish_kernel, in_specs=[SMEM] + [WHOLE] * 4 + [ANY] * 3,...  6.24 us
    pallas_call x1, Pallas kernels, project(): pl.pallas_call(project_kernel, in_specs=[SMEM] * 2 + [WHOLE] * 5 + [ANY]...  5.68 us
    all_to_all x1, starting transfers between devices, body(): parts = lax.all_to_all(parts, 'list', 0, 0, tiled=True)  5.17 us
    ppermute x6, waiting for transfers between devices, in_plane(): return lax.ppermute(a, ('dp', 'list'), pairs)  4.72 us
  transfers between devices with their start and end apart: 13, of which 8 were waited for; matrix products, arithmetic and copies ran while one was open for 0% of the time, Pallas kernels for 36%

profile of v5, /device:TPU:0, one launch (start us, length us, event | category | flops | bytes accessed | tf_op | source)
XLA Modules:
  0.0 88.4 jit_solution(12464763477072318492)
XLA Ops:
  0.6 1.7 %collective-permute-start = (bf16[128,1024]{1,0:T(8,128)(2,1)}, bf16[128,1024]{1,0:T(8,128)(2,1)S(1)}, u32[]{:S(2)}, u32[]{:S(2)}) collective-permute-start(bf16[128,1024]{1,0:T(8,128)(2,1)} %bitcast.12), channel_id=1, source_target_pairs={{0,1},{1,0},{2,3},{3,2},{4,5},{5,4},{6,7},{7,6},{8,9},{9,8},{10,11... | collective-permute-start | bytes 786440 | tf_op jit(solution)/shard_map/ppermute | solution.py:430
  2.4 2.9 %collective-permute-start.1 = (bf16[128,1024]{1,0:T(8,128)(2,1)}, bf16[128,1024]{1,0:T(8,128)(2,1)S(1)}, u32[]{:S(2)}, u32[]{:S(2)}) collective-permute-start(bf16[128,1024]{1,0:T(8,128)(2,1)} %bitcast.13), channel_id=1, source_target_pairs={{0,2},{1,3},{2,0},{3,1},{4,6},{5,7},{6,4},{7,5},{8,10},{9,11},{10,... | collective-permute-start | bytes 786440 | tf_op jit(solution)/shard_map/ppermute | solution.py:430
  5.3 0.1 collective-permute-start.2
  6.1 5.7 %project.1 = (bf16[16,144,256]{2,1,0:T(8,128)(2,1)}, bf16[48,1024]{1,0:T(8,128)(2,1)}) custom-call(s32[1]{0:T(128)S(6)} %sub.17.live_ref, s32[1]{0:T(128)} %bitcast.4.place_ref, bf16[128,1024]{1,0:T(8,128)(2,1)} %bitcast.15, bf16[128,1024]{1,0:T(8,128)(2,1)} %bitcast.22, bf16[16,1024]{1,0:T(8,128)(2,1)} %bitcast.26, bf16[16,1024]{1,0:T(8,128)(2,1)} %bitcast.27, ...), custom_call_target="tpu_custom_call" | custom-call | flops 8053063680 | bytes 8388608 | tf_op jit(solution)/shard_map/project/pallas_call | solution.py:104
  11.8 0.0 copy-start
  11.8 0.0 copy-start.2
  11.8 0.1 pad_add_fusion.where_ref
  11.9 0.0 collective-permute-done.b_ref
  11.9 0.8 collective-permute-done.1.c_ref
  12.7 2.7 %collective-permute-done.2.d_ref = bf16[128,1024]{1,0:T(8,128)(2,1)S(1)} collective-permute-done((bf16[128,1024]{1,0:T(8,128)(2,1)}, bf16[128,1024]{1,0:T(8,128)(2,1)S(1)}, u32[]{:S(2)}, u32[]{:S(2)}) %collective-permute-start.2) | collective-permute-done | bytes 262176 | tf_op jit(solution)/shard_map/ppermute | solution.py:430
  15.4 4.4 %all-to-all-start = ((bf16[16,144,256]{2,1,0:T(8,128)(2,1)}), bf16[16,144,256]{2,1,0:T(8,128)(2,1)S(1)}, u32[]{:S(2)}, u32[]{:S(2)}) async-start(bf16[16,144,256]{2,1,0:T(8,128)(2,1)} %get-tuple-element.34), calls=%async_computation | async-start | bytes 2359296 | tf_op jit(solution)/shard_map/all_to_all | solution.py:455
  20.5 0.0 copy-done
  20.5 0.0 copy-done.2
  20.5 0.4 gather.1.n0
  20.9 2.0 %collective-permute-start.3 = (bf16[512,1024]{1,0:T(8,128)(2,1)S(1)}, bf16[512,1024]{1,0:T(8,128)(2,1)S(1)}, u32[]{:S(2)}, u32[]{:S(2)}) collective-permute-start(bf16[512,1024]{1,0:T(8,128)(2,1)S(1)} %gather.1.n0), channel_id=1, source_target_pairs={{0,4},{1,5},{2,6},{3,7},{4,0},{5,1},{6,2},{7,3},{8,12},{9,13},{10,... | collective-permute-start | bytes 3145736 | tf_op jit(solution)/shard_map/ppermute | solution.py:430
  22.9 2.7 %collective-permute-start.4 = (bf16[512,1024]{1,0:T(8,128)(2,1)S(1)}, bf16[512,1024]{1,0:T(8,128)(2,1)}, u32[]{:S(2)}, u32[]{:S(2)}) collective-permute-start(bf16[512,1024]{1,0:T(8,128)(2,1)S(1)} %gather.1.n0), channel_id=1, source_target_pairs={{0,8},{1,9},{2,10},{3,11},{4,12},{5,13},{6,14},{7,15},{8,0},{9,1},... | collective-permute-start | bytes 3145736 | tf_op jit(solution)/shard_map/ppermute | solution.py:430
  25.6 0.1 collective-permute-start.5
  25.7 11.4 %all-to-all-done.in_ref = bf16[16,144,256]{2,1,0:T(8,128)(2,1)S(1)} async-done(((bf16[16,144,256]{2,1,0:T(8,128)(2,1)}), bf16[16,144,256]{2,1,0:T(8,128)(2,1)S(1)}, u32[]{:S(2)}, u32[]{:S(2)}) %all-to-all-start) | async-done | bytes 1179680 | tf_op jit(solution)/shard_map/all_to_all | solution.py:455
  37.1 14.8 %attend.1.g0.g1.g2.g3.g4.g5.g6.g7 = bf16[16,256,128]{2,1,0:T(8,128)(2,1)} custom-call(s32[1]{0:T(128)S(6)} %copy.16.count_ref, s32[1]{0:T(128)S(6)} %copy.17.past_ref, bf16[16,144,256]{2,1,0:T(8,128)(2,1)S(1)} %all-to-all-done.in_ref), custom_call_target="tpu_custom_call" | custom-call | flops 14495514624 | bytes 3145728 | tf_op jit(solution)/shard_map/attend/pallas_call | solution.py:243
  51.9 4.5 %all-to-all-start.1 = ((bf16[16,256,128]{2,1,0:T(8,128)(2,1)}), bf16[16,256,128]{2,1,0:T(8,128)(2,1)S(1)}, u32[]{:S(2)}, u32[]{:S(2)}) async-start(bf16[16,256,128]{2,1,0:T(8,128)(2,1)} %attend.1.g0.g1.g2.g3.g4.g5.g6.g7), calls=%async_computation.1 | async-start | bytes 2097152 | tf_op jit(solution)/shard_map/all_to_all | solution.py:459
  56.5 0.0 collective-permute-done.3.n1
  56.5 1.2 %collective-permute-done.4.n2 = bf16[512,1024]{1,0:T(8,128)(2,1)} collective-permute-done((bf16[512,1024]{1,0:T(8,128)(2,1)S(1)}, bf16[512,1024]{1,0:T(8,128)(2,1)}, u32[]{:S(2)}, u32[]{:S(2)}) %collective-permute-start.4) | collective-permute-done | bytes 1048608 | tf_op jit(solution)/shard_map/ppermute | solution.py:430
  57.6 0.0 collective-permute-done.5.n3
  57.6 3.5 %weigh.1 = (f32[4,192,128]{2,1,0:T(8,128)S(1)}, bf16[4,192,128]{2,1,0:T(8,128)(2,1)S(1)}) custom-call(s32[18]{0:T(128)S(1)} %pad_add_fusion.where_ref, bf16[512,1024]{1,0:T(8,128)(2,1)S(1)} %gather.1.n0, bf16[512,1024]{1,0:T(8,128)(2,1)S(1)} %collective-permute-done.3.n1, bf16[512,1024]{1,0:T(8,128)(2,1)} %collective-permute-done.4.n2, ...), custom_call_target="tpu_custom_call" | custom-call | flops 1 | bytes 1 | tf_op jit(solution)/shard_map/weigh/pallas_call | solution.py:291
  61.2 1.3 %collective-permute-start.6 = (bf16[4,192,128]{2,1,0:T(8,128)(2,1)S(1)}, bf16[4,192,128]{2,1,0:T(8,128)(2,1)S(1)}, u32[]{:S(2)}, u32[]{:S(2)}) collective-permute-start(bf16[4,192,128]{2,1,0:T(8,128)(2,1)S(1)} %get-tuple-element.36), channel_id=1, source_target_pairs={{0,16},{16,0},{32,48},{48,32},{64,80},{80,64},{96,112},{112,96},{1... | collective-permute-start | bytes 589832 | tf_op jit(solution)/shard_map/ppermute | solution.py:438
  62.5 1.1 %collective-permute-done.6.came_ref = bf16[4,192,128]{2,1,0:T(8,128)(2,1)S(1)} collective-permute-done((bf16[4,192,128]{2,1,0:T(8,128)(2,1)S(1)}, bf16[4,192,128]{2,1,0:T(8,128)(2,1)S(1)}, u32[]{:S(2)}, u32[]{:S(2)}) %collective-permute-start.6) | collective-permute-done | bytes 196640 | tf_op jit(solution)/shard_map/ppermute | solution.py:438
  63.6 0.6 pair.1
  64.2 2.0 %collective-permute-start.7 = (bf16[192,128]{1,0:T(8,128)(2,1)S(1)}, bf16[192,128]{1,0:T(8,128)(2,1)S(1)}, u32[]{:S(2)}, u32[]{:S(2)}) collective-permute-start(bf16[192,128]{1,0:T(8,128)(2,1)S(1)} %get-tuple-element.38), channel_id=1, source_target_pairs={{0,32},{16,48},{32,64},{48,80},{64,96},{80,112},{96,0},{112,16},{1... | collective-permute-start | bytes 147464 | tf_op jit(solution)/shard_map/ppermute | solution.py:434
  66.2 3.6 %collective-permute-start.8 = (bf16[192,128]{1,0:T(8,128)(2,1)S(1)}, bf16[192,128]{1,0:T(8,128)(2,1)S(1)}, u32[]{:S(2)}, u32[]{:S(2)}) collective-permute-start(bf16[192,128]{1,0:T(8,128)(2,1)S(1)} %get-tuple-element.39), channel_id=1, source_target_pairs={{0,64},{16,80},{32,96},{48,112},{64,0},{80,16},{96,32},{112,48},{1... | collective-permute-start | bytes 147464 | tf_op jit(solution)/shard_map/ppermute | solution.py:434
  69.8 1.0 %collective-permute-start.9 = (bf16[192,128]{1,0:T(8,128)(2,1)S(1)}, bf16[192,128]{1,0:T(8,128)(2,1)S(1)}, u32[]{:S(2)}, u32[]{:S(2)}) collective-permute-start(bf16[192,128]{1,0:T(8,128)(2,1)S(1)} %get-tuple-element.40), channel_id=1, source_target_pairs={{0,96},{16,112},{32,0},{48,16},{64,32},{80,48},{96,64},{112,80},{1... | collective-permute-start | bytes 147464 | tf_op jit(solution)/shard_map/ppermute | solution.py:434
  70.8 0.0 collective-permute-done.7.a_ref
  70.8 2.0 %collective-permute-done.8.b_ref = bf16[192,128]{1,0:T(8,128)(2,1)S(1)} collective-permute-done((bf16[192,128]{1,0:T(8,128)(2,1)S(1)}, bf16[192,128]{1,0:T(8,128)(2,1)S(1)}, u32[]{:S(2)}, u32[]{:S(2)}) %collective-permute-start.8) | collective-permute-done | bytes 49184 | tf_op jit(solution)/shard_map/ppermute | solution.py:434
  72.8 1.1 %collective-permute-done.9.c_ref = bf16[192,128]{1,0:T(8,128)(2,1)S(1)} collective-permute-done((bf16[192,128]{1,0:T(8,128)(2,1)S(1)}, bf16[192,128]{1,0:T(8,128)(2,1)S(1)}, u32[]{:S(2)}, u32[]{:S(2)}) %collective-permute-start.9) | collective-permute-done | bytes 49184 | tf_op jit(solution)/shard_map/ppermute | solution.py:434
  73.9 0.8 line.1
  74.6 0.0 all-to-all-done.1.g_ref
  74.6 0.0 copy-start.4
  74.6 5.2 %all-to-all-start.2 = ((f32[16,8,256]{2,1,0:T(8,128)}), f32[16,8,256]{2,1,0:T(8,128)S(1)}, u32[]{:S(2)}, u32[]{:S(2)}) async-start(f32[16,8,256]{2,1,0:T(8,128)} %line.1), calls=%async_computation.2 | async-start | bytes 262144 | tf_op jit(solution)/shard_map/all_to_all | solution.py:464
  79.8 0.0 copy-done.4
  79.8 0.0 copy-start.1
  79.8 0.0 copy-start.3
  79.8 6.2 %finish.1 = (bf16[128,1024]{1,0:T(8,128)(2,1)}, bf16[128,1024]{1,0:T(8,128)(2,1)}) custom-call(s32[1]{0:T(128)S(6)} %sub.17.live_ref, bf16[128,1024]{1,0:T(8,128)(2,1)} %bitcast.16, bf16[128,1024]{1,0:T(8,128)(2,1)} %bitcast.23, f32[1,1024]{1,0:T(1,128)} %bitcast.19, bf16[16,256,128]{2,1,0:T(8,128)(2,1)} %copy-done.4, bf16[1024,1024]{1,0:T(8,128)(2,1)} %wq_ref.3, ...), custom_call_target="tpu_custom_call" | custom-call | flops 805306368 | bytes 8388608 | tf_op jit(solution)/shard_map/finish/pallas_call | solution.py:375
  86.1 1.6 %all-to-all-done.2.in_ref = f32[16,8,256]{2,1,0:T(8,128)S(1)} async-done(((f32[16,8,256]{2,1,0:T(8,128)}), f32[16,8,256]{2,1,0:T(8,128)S(1)}, u32[]{:S(2)}, u32[]{:S(2)}) %all-to-all-start.2) | async-done | bytes 131104 | tf_op jit(solution)/shard_map/all_to_all | solution.py:464
  87.6 0.0 copy-done.1
  87.6 0.0 copy-done.3
  87.7 0.8 settle.1
  (1 shorter events, 0.0 us)
Async XLA Ops:
  0.6 11.3 %collective-permute-start = (bf16[128,1024]{1,0:T(8,128)(2,1)}, bf16[128,1024]{1,0:T(8,128)(2,1)S(1)}, u32[]{:S(2)}, u32[]{:S(2)}) collective-permute-start(bf16[128,1024]{1,0:T(8,128)(2,1)} %bitcast.12), channel_id=1, source_target_pairs={{0,1},{1,0},{2,3},{3,2},{4,5},{5,4},{6,7},{7,6},{8,9},{9,8},{10,11... | collective-permute-start | bytes 786440 | tf_op jit(solution)/shard_map/ppermute | solution.py:430
  2.4 10.4 %collective-permute-start.1 = (bf16[128,1024]{1,0:T(8,128)(2,1)}, bf16[128,1024]{1,0:T(8,128)(2,1)S(1)}, u32[]{:S(2)}, u32[]{:S(2)}) collective-permute-start(bf16[128,1024]{1,0:T(8,128)(2,1)} %bitcast.13), channel_id=1, source_target_pairs={{0,2},{1,3},{2,0},{3,1},{4,6},{5,7},{6,4},{7,5},{8,10},{9,11},{10,... | collective-permute-start | bytes 786440 | tf_op jit(solution)/shard_map/ppermute | solution.py:430
  5.3 10.2 %collective-permute-start.2 = (bf16[128,1024]{1,0:T(8,128)(2,1)}, bf16[128,1024]{1,0:T(8,128)(2,1)S(1)}, u32[]{:S(2)}, u32[]{:S(2)}) collective-permute-start(bf16[128,1024]{1,0:T(8,128)(2,1)} %bitcast.14), channel_id=1, source_target_pairs={{0,3},{1,2},{2,1},{3,0},{4,7},{5,6},{6,5},{7,4},{8,11},{9,10},{10,... | collective-permute-start | bytes 786440 | tf_op jit(solution)/shard_map/ppermute | solution.py:430
  11.8 8.8 %copy-start = (bf16[1,128,1024]{2,1,0:T(8,128)(2,1)S(1)}, bf16[1,128,1024]{2,1,0:T(8,128)(2,1)}, u32[]{:S(2)}) copy-start(bf16[1,128,1024]{2,1,0:T(8,128)(2,1)} %param.10) | copy-start | bytes 786436
  11.8 8.8 %copy-start.2 = (f32[1024]{0:T(1024)S(1)}, f32[1024]{0:T(1024)}, u32[]{:S(2)}) copy-start(f32[1024]{0:T(1024)} %param.15) | copy-start | bytes 12292
  15.4 21.7 %all-to-all-start = ((bf16[16,144,256]{2,1,0:T(8,128)(2,1)}), bf16[16,144,256]{2,1,0:T(8,128)(2,1)S(1)}, u32[]{:S(2)}, u32[]{:S(2)}) async-start(bf16[16,144,256]{2,1,0:T(8,128)(2,1)} %get-tuple-element.34), calls=%async_computation | async-start | bytes 2359296 | tf_op jit(solution)/shard_map/all_to_all | solution.py:455
  20.9 35.5 %collective-permute-start.3 = (bf16[512,1024]{1,0:T(8,128)(2,1)S(1)}, bf16[512,1024]{1,0:T(8,128)(2,1)S(1)}, u32[]{:S(2)}, u32[]{:S(2)}) collective-permute-start(bf16[512,1024]{1,0:T(8,128)(2,1)S(1)} %gather.1.n0), channel_id=1, source_target_pairs={{0,4},{1,5},{2,6},{3,7},{4,0},{5,1},{6,2},{7,3},{8,12},{9,13},{10,... | collective-permute-start | bytes 3145736 | tf_op jit(solution)/shard_map/ppermute | solution.py:430
  22.9 34.7 %collective-permute-start.4 = (bf16[512,1024]{1,0:T(8,128)(2,1)S(1)}, bf16[512,1024]{1,0:T(8,128)(2,1)}, u32[]{:S(2)}, u32[]{:S(2)}) collective-permute-start(bf16[512,1024]{1,0:T(8,128)(2,1)S(1)} %gather.1.n0), channel_id=1, source_target_pairs={{0,8},{1,9},{2,10},{3,11},{4,12},{5,13},{6,14},{7,15},{8,0},{9,1},... | collective-permute-start | bytes 3145736 | tf_op jit(solution)/shard_map/ppermute | solution.py:430
  25.6 32.0 %collective-permute-start.5 = (bf16[512,1024]{1,0:T(8,128)(2,1)S(1)}, bf16[512,1024]{1,0:T(8,128)(2,1)}, u32[]{:S(2)}, u32[]{:S(2)}) collective-permute-start(bf16[512,1024]{1,0:T(8,128)(2,1)S(1)} %gather.1.n0), channel_id=1, source_target_pairs={{0,12},{1,13},{2,14},{3,15},{4,8},{5,9},{6,10},{7,11},{8,4},{9,5},... | collective-permute-start | bytes 3145736 | tf_op jit(solution)/shard_map/ppermute | solution.py:430
  51.9 22.7 %all-to-all-start.1 = ((bf16[16,256,128]{2,1,0:T(8,128)(2,1)}), bf16[16,256,128]{2,1,0:T(8,128)(2,1)S(1)}, u32[]{:S(2)}, u32[]{:S(2)}) async-start(bf16[16,256,128]{2,1,0:T(8,128)(2,1)} %attend.1.g0.g1.g2.g3.g4.g5.g6.g7), calls=%async_computation.1 | async-start | bytes 2097152 | tf_op jit(solution)/shard_map/all_to_all | solution.py:459
  61.2 2.4 %collective-permute-start.6 = (bf16[4,192,128]{2,1,0:T(8,128)(2,1)S(1)}, bf16[4,192,128]{2,1,0:T(8,128)(2,1)S(1)}, u32[]{:S(2)}, u32[]{:S(2)}) collective-permute-start(bf16[4,192,128]{2,1,0:T(8,128)(2,1)S(1)} %get-tuple-element.36), channel_id=1, source_target_pairs={{0,16},{16,0},{32,48},{48,32},{64,80},{80,64},{96,112},{112,96},{1... | collective-permute-start | bytes 589832 | tf_op jit(solution)/shard_map/ppermute | solution.py:438
  64.2 6.6 %collective-permute-start.7 = (bf16[192,128]{1,0:T(8,128)(2,1)S(1)}, bf16[192,128]{1,0:T(8,128)(2,1)S(1)}, u32[]{:S(2)}, u32[]{:S(2)}) collective-permute-start(bf16[192,128]{1,0:T(8,128)(2,1)S(1)} %get-tuple-element.38), channel_id=1, source_target_pairs={{0,32},{16,48},{32,64},{48,80},{64,96},{80,112},{96,0},{112,16},{1... | collective-permute-start | bytes 147464 | tf_op jit(solution)/shard_map/ppermute | solution.py:434
  66.2 6.6 %collective-permute-start.8 = (bf16[192,128]{1,0:T(8,128)(2,1)S(1)}, bf16[192,128]{1,0:T(8,128)(2,1)S(1)}, u32[]{:S(2)}, u32[]{:S(2)}) collective-permute-start(bf16[192,128]{1,0:T(8,128)(2,1)S(1)} %get-tuple-element.39), channel_id=1, source_target_pairs={{0,64},{16,80},{32,96},{48,112},{64,0},{80,16},{96,32},{112,48},{1... | collective-permute-start | bytes 147464 | tf_op jit(solution)/shard_map/ppermute | solution.py:434
  69.8 4.1 %collective-permute-start.9 = (bf16[192,128]{1,0:T(8,128)(2,1)S(1)}, bf16[192,128]{1,0:T(8,128)(2,1)S(1)}, u32[]{:S(2)}, u32[]{:S(2)}) collective-permute-start(bf16[192,128]{1,0:T(8,128)(2,1)S(1)} %get-tuple-element.40), channel_id=1, source_target_pairs={{0,96},{16,112},{32,0},{48,16},{64,32},{80,48},{96,64},{112,80},{1... | collective-permute-start | bytes 147464 | tf_op jit(solution)/shard_map/ppermute | solution.py:434
  74.6 5.2 %copy-start.4 = (bf16[16,256,128]{2,1,0:T(8,128)(2,1)}, bf16[16,256,128]{2,1,0:T(8,128)(2,1)S(1)}, u32[]{:S(2)}) copy-start(bf16[16,256,128]{2,1,0:T(8,128)(2,1)S(1)} %all-to-all-done.1.g_ref) | copy-start | bytes 3145732
  74.6 13.0 %all-to-all-start.2 = ((f32[16,8,256]{2,1,0:T(8,128)}), f32[16,8,256]{2,1,0:T(8,128)S(1)}, u32[]{:S(2)}, u32[]{:S(2)}) async-start(f32[16,8,256]{2,1,0:T(8,128)} %line.1), calls=%async_computation.2 | async-start | bytes 262144 | tf_op jit(solution)/shard_map/all_to_all | solution.py:464
  79.8 7.8 %copy-start.1 = (bf16[48,1024]{1,0:T(8,128)(2,1)S(1)}, bf16[48,1024]{1,0:T(8,128)(2,1)}, u32[]{:S(2)}) copy-start(bf16[48,1024]{1,0:T(8,128)(2,1)} %get-tuple-element.45.w_ref) | copy-start | bytes 294916
  79.8 7.8 %copy-start.3 = (f32[1024]{0:T(1024)S(1)}, f32[1024]{0:T(1024)}, u32[]{:S(2)}) copy-start(f32[1024]{0:T(1024)} %param.15) | copy-start | bytes 12292

commit v6 on v5

--- a/solution.py
+++ b/solution.py
@@ -329,7 +329,8 @@
 def line_kernel(own_ref, a_ref, b_ref, c_ref, out_ref):
     total = own_ref[...] + a_ref[...].astype(F32) + b_ref[...].astype(F32) + c_ref[...].astype(F32)
     total = jnp.concatenate([total, jnp.zeros((64, 128), F32)], axis=0)
-    out_ref[...] = total.T.reshape(16, 8, 256)
+    total = total.T.reshape(16, 8, 256)
+    out_ref[...] = jnp.concatenate([total[:, :, :128], total[:, :, 128:]], axis=1).astype(BF)
 
 
 def line(own, a, b, c):
@@ -337,7 +338,7 @@
         line_kernel,
         in_specs=[VMEM] * 4,
         out_specs=VMEM,
-        out_shape=jax.ShapeDtypeStruct((16, 8, 256), F32),
+        out_shape=jax.ShapeDtypeStruct((16, 16, 128), BF),
         cost_estimate=SOON,
         compiler_params=pltpu.CompilerParams(vmem_limit_bytes=16 * MIB),
         name="line",
@@ -392,10 +393,10 @@
     low = lanes((8, 128)) < 64
     for p in range(H // 2):
         s = slice(128 * p, 128 * p + 128)
-        a, b = in_ref[2 * p], in_ref[2 * p + 1]
-        q_ref[:, s] = jnp.where(low, a[:, :128], swap(b[:, :128]))
-        k_ref[:, s] = jnp.where(low, swap(a[:, :128]), b[:, :128])
-        v_ref[:, s] = jnp.where(low, a[:, 128:], swap(b[:, 128:]))
+        a, b = in_ref[2 * p].astype(F32), in_ref[2 * p + 1].astype(F32)
+        q_ref[:, s] = jnp.where(low, a[:8], swap(b[:8]))
+        k_ref[:, s] = jnp.where(low, swap(a[:8]), b[:8])
+        v_ref[:, s] = jnp.where(low, a[8:], swap(b[8:]))
     w = w_ref[...].astype(F32)
     odd = jnp.broadcast_to(place_ref[0] % 2, (8, D)) == 1
     back = 0.0

time: 88.8 us -> 88.6 us (level)
  no operation moved by 1% of the time
where the time goes in v6:
time: 88.6 us; the launch traced here: 88.2 us
  Pallas kernels  32.7 us (37%)
  starting transfers between devices  31.6 us (36%)
  waiting for transfers between devices  21.7 us (24%)
  between operations  2.1 us (2%)
    pallas_call x1, Pallas kernels, attend(): pl.pallas_call(attend_kernel, in_specs=[SMEM, SMEM, VMEM], out_specs=VMEM...  14.8 us
    all_to_all x1, waiting for transfers between devices, body(): packed = lax.all_to_all(packed, 'list', 0, 0, tiled=True)  11.4 us
    ppermute x6, starting transfers between devices, in_plane(): return lax.ppermute(a, ('dp', 'list'), pairs)  9.56 us
    ppermute x3, starting transfers between devices, along_z(): return lax.ppermute(a, 'dp', [(i, (i + 2 * s) % 8) for i in range(8)])  6.59 us
    pallas_call x1, Pallas kernels, finish(): pl.pallas_call(finish_kernel, in_specs=[SMEM] + [WHOLE] * 4 + [ANY] * 3,...  6.24 us
    pallas_call x1, Pallas kernels, project(): pl.pallas_call(project_kernel, in_specs=[SMEM] * 2 + [WHOLE] * 5 + [ANY]...  5.68 us
    all_to_all x1, starting transfers between devices, body(): parts = lax.all_to_all(parts, 'list', 0, 0, tiled=True)  5.17 us
    ppermute x6, waiting for transfers between devices, in_plane(): return lax.ppermute(a, ('dp', 'list'), pairs)  4.72 us
  transfers between devices with their start and end apart: 13, of which 8 were waited for; matrix products, arithmetic and copies ran while one was open for 0% of the time, Pallas kernels for 36%

profile of v6, /device:TPU:0, one launch (start us, length us, event | category | flops | bytes accessed | tf_op | source)
XLA Modules:
  0.0 88.2 jit_solution(7835866220801338114)
XLA Ops:
  0.6 1.7 %collective-permute-start = (bf16[128,1024]{1,0:T(8,128)(2,1)}, bf16[128,1024]{1,0:T(8,128)(2,1)S(1)}, u32[]{:S(2)}, u32[]{:S(2)}) collective-permute-start(bf16[128,1024]{1,0:T(8,128)(2,1)} %bitcast.12), channel_id=1, source_target_pairs={{0,1},{1,0},{2,3},{3,2},{4,5},{5,4},{6,7},{7,6},{8,9},{9,8},{10,11... | collective-permute-start | bytes 786440 | tf_op jit(solution)/shard_map/ppermute | solution.py:431
  2.4 2.9 %collective-permute-start.1 = (bf16[128,1024]{1,0:T(8,128)(2,1)}, bf16[128,1024]{1,0:T(8,128)(2,1)S(1)}, u32[]{:S(2)}, u32[]{:S(2)}) collective-permute-start(bf16[128,1024]{1,0:T(8,128)(2,1)} %bitcast.13), channel_id=1, source_target_pairs={{0,2},{1,3},{2,0},{3,1},{4,6},{5,7},{6,4},{7,5},{8,10},{9,11},{10,... | collective-permute-start | bytes 786440 | tf_op jit(solution)/shard_map/ppermute | solution.py:431
  5.3 0.1 collective-permute-start.2
  6.1 5.7 %project.1 = (bf16[16,144,256]{2,1,0:T(8,128)(2,1)}, bf16[48,1024]{1,0:T(8,128)(2,1)}) custom-call(s32[1]{0:T(128)S(6)} %sub.17.live_ref, s32[1]{0:T(128)} %bitcast.4.place_ref, bf16[128,1024]{1,0:T(8,128)(2,1)} %bitcast.15, bf16[128,1024]{1,0:T(8,128)(2,1)} %bitcast.22, bf16[16,1024]{1,0:T(8,128)(2,1)} %bitcast.26, bf16[16,1024]{1,0:T(8,128)(2,1)} %bitcast.27, ...), custom_call_target="tpu_custom_call" | custom-call | flops 8053063680 | bytes 8388608 | tf_op jit(solution)/shard_map/project/pallas_call | solution.py:104
  11.8 0.0 copy-start
  11.8 0.0 copy-start.2
  11.8 0.1 pad_add_fusion.where_ref
  11.9 0.0 collective-permute-done.b_ref
  11.9 0.8 collective-permute-done.1.c_ref
  12.7 2.7 %collective-permute-done.2.d_ref = bf16[128,1024]{1,0:T(8,128)(2,1)S(1)} collective-permute-done((bf16[128,1024]{1,0:T(8,128)(2,1)}, bf16[128,1024]{1,0:T(8,128)(2,1)S(1)}, u32[]{:S(2)}, u32[]{:S(2)}) %collective-permute-start.2) | collective-permute-done | bytes 262176 | tf_op jit(solution)/shard_map/ppermute | solution.py:431
  15.4 4.4 %all-to-all-start = ((bf16[16,144,256]{2,1,0:T(8,128)(2,1)}), bf16[16,144,256]{2,1,0:T(8,128)(2,1)S(1)}, u32[]{:S(2)}, u32[]{:S(2)}) async-start(bf16[16,144,256]{2,1,0:T(8,128)(2,1)} %get-tuple-element.34), calls=%async_computation | async-start | bytes 2359296 | tf_op jit(solution)/shard_map/all_to_all | solution.py:456
  20.5 0.0 copy-done
  20.5 0.0 copy-done.2
  20.5 0.4 gather.1.n0
  20.9 2.0 %collective-permute-start.3 = (bf16[512,1024]{1,0:T(8,128)(2,1)S(1)}, bf16[512,1024]{1,0:T(8,128)(2,1)S(1)}, u32[]{:S(2)}, u32[]{:S(2)}) collective-permute-start(bf16[512,1024]{1,0:T(8,128)(2,1)S(1)} %gather.1.n0), channel_id=1, source_target_pairs={{0,4},{1,5},{2,6},{3,7},{4,0},{5,1},{6,2},{7,3},{8,12},{9,13},{10,... | collective-permute-start | bytes 3145736 | tf_op jit(solution)/shard_map/ppermute | solution.py:431
  22.9 2.7 %collective-permute-start.4 = (bf16[512,1024]{1,0:T(8,128)(2,1)S(1)}, bf16[512,1024]{1,0:T(8,128)(2,1)}, u32[]{:S(2)}, u32[]{:S(2)}) collective-permute-start(bf16[512,1024]{1,0:T(8,128)(2,1)S(1)} %gather.1.n0), channel_id=1, source_target_pairs={{0,8},{1,9},{2,10},{3,11},{4,12},{5,13},{6,14},{7,15},{8,0},{9,1},... | collective-permute-start | bytes 3145736 | tf_op jit(solution)/shard_map/ppermute | solution.py:431
  25.6 0.1 collective-permute-start.5
  25.7 11.4 %all-to-all-done.in_ref = bf16[16,144,256]{2,1,0:T(8,128)(2,1)S(1)} async-done(((bf16[16,144,256]{2,1,0:T(8,128)(2,1)}), bf16[16,144,256]{2,1,0:T(8,128)(2,1)S(1)}, u32[]{:S(2)}, u32[]{:S(2)}) %all-to-all-start) | async-done | bytes 1179680 | tf_op jit(solution)/shard_map/all_to_all | solution.py:456
  37.1 14.8 %attend.1.g0.g1.g2.g3.g4.g5.g6.g7 = bf16[16,256,128]{2,1,0:T(8,128)(2,1)} custom-call(s32[1]{0:T(128)S(6)} %copy.16.count_ref, s32[1]{0:T(128)S(6)} %copy.17.past_ref, bf16[16,144,256]{2,1,0:T(8,128)(2,1)S(1)} %all-to-all-done.in_ref), custom_call_target="tpu_custom_call" | custom-call | flops 14495514624 | bytes 3145728 | tf_op jit(solution)/shard_map/attend/pallas_call | solution.py:243
  51.9 4.5 %all-to-all-start.1 = ((bf16[16,256,128]{2,1,0:T(8,128)(2,1)}), bf16[16,256,128]{2,1,0:T(8,128)(2,1)S(1)}, u32[]{:S(2)}, u32[]{:S(2)}) async-start(bf16[16,256,128]{2,1,0:T(8,128)(2,1)} %attend.1.g0.g1.g2.g3.g4.g5.g6.g7), calls=%async_computation.1 | async-start | bytes 2097152 | tf_op jit(solution)/shard_map/all_to_all | solution.py:460
  56.5 0.0 collective-permute-done.3.n1
  56.5 1.2 %collective-permute-done.4.n2 = bf16[512,1024]{1,0:T(8,128)(2,1)} collective-permute-done((bf16[512,1024]{1,0:T(8,128)(2,1)S(1)}, bf16[512,1024]{1,0:T(8,128)(2,1)}, u32[]{:S(2)}, u32[]{:S(2)}) %collective-permute-start.4) | collective-permute-done | bytes 1048608 | tf_op jit(solution)/shard_map/ppermute | solution.py:431
  57.6 0.0 collective-permute-done.5.n3
  57.6 3.5 %weigh.1 = (f32[4,192,128]{2,1,0:T(8,128)S(1)}, bf16[4,192,128]{2,1,0:T(8,128)(2,1)S(1)}) custom-call(s32[18]{0:T(128)S(1)} %pad_add_fusion.where_ref, bf16[512,1024]{1,0:T(8,128)(2,1)S(1)} %gather.1.n0, bf16[512,1024]{1,0:T(8,128)(2,1)S(1)} %collective-permute-done.3.n1, bf16[512,1024]{1,0:T(8,128)(2,1)} %collective-permute-done.4.n2, ...), custom_call_target="tpu_custom_call" | custom-call | flops 1 | bytes 1 | tf_op jit(solution)/shard_map/weigh/pallas_call | solution.py:291
  61.2 1.3 %collective-permute-start.6 = (bf16[4,192,128]{2,1,0:T(8,128)(2,1)S(1)}, bf16[4,192,128]{2,1,0:T(8,128)(2,1)S(1)}, u32[]{:S(2)}, u32[]{:S(2)}) collective-permute-start(bf16[4,192,128]{2,1,0:T(8,128)(2,1)S(1)} %get-tuple-element.36), channel_id=1, source_target_pairs={{0,16},{16,0},{32,48},{48,32},{64,80},{80,64},{96,112},{112,96},{1... | collective-permute-start | bytes 589832 | tf_op jit(solution)/shard_map/ppermute | solution.py:439
  62.5 1.1 %collective-permute-done.6.came_ref = bf16[4,192,128]{2,1,0:T(8,128)(2,1)S(1)} collective-permute-done((bf16[4,192,128]{2,1,0:T(8,128)(2,1)S(1)}, bf16[4,192,128]{2,1,0:T(8,128)(2,1)S(1)}, u32[]{:S(2)}, u32[]{:S(2)}) %collective-permute-start.6) | collective-permute-done | bytes 196640 | tf_op jit(solution)/shard_map/ppermute | solution.py:439
  63.6 0.6 pair.1
  64.2 2.0 %collective-permute-start.7 = (bf16[192,128]{1,0:T(8,128)(2,1)S(1)}, bf16[192,128]{1,0:T(8,128)(2,1)S(1)}, u32[]{:S(2)}, u32[]{:S(2)}) collective-permute-start(bf16[192,128]{1,0:T(8,128)(2,1)S(1)} %get-tuple-element.38), channel_id=1, source_target_pairs={{0,32},{16,48},{32,64},{48,80},{64,96},{80,112},{96,0},{112,16},{1... | collective-permute-start | bytes 147464 | tf_op jit(solution)/shard_map/ppermute | solution.py:435
  66.2 3.6 %collective-permute-start.8 = (bf16[192,128]{1,0:T(8,128)(2,1)S(1)}, bf16[192,128]{1,0:T(8,128)(2,1)S(1)}, u32[]{:S(2)}, u32[]{:S(2)}) collective-permute-start(bf16[192,128]{1,0:T(8,128)(2,1)S(1)} %get-tuple-element.39), channel_id=1, source_target_pairs={{0,64},{16,80},{32,96},{48,112},{64,0},{80,16},{96,32},{112,48},{1... | collective-permute-start | bytes 147464 | tf_op jit(solution)/shard_map/ppermute | solution.py:435
  69.8 1.0 %collective-permute-start.9 = (bf16[192,128]{1,0:T(8,128)(2,1)S(1)}, bf16[192,128]{1,0:T(8,128)(2,1)S(1)}, u32[]{:S(2)}, u32[]{:S(2)}) collective-permute-start(bf16[192,128]{1,0:T(8,128)(2,1)S(1)} %get-tuple-element.40), channel_id=1, source_target_pairs={{0,96},{16,112},{32,0},{48,16},{64,32},{80,48},{96,64},{112,80},{1... | collective-permute-start | bytes 147464 | tf_op jit(solution)/shard_map/ppermute | solution.py:435
  70.8 0.0 collective-permute-done.7.a_ref
  70.8 2.0 %collective-permute-done.8.b_ref = bf16[192,128]{1,0:T(8,128)(2,1)S(1)} collective-permute-done((bf16[192,128]{1,0:T(8,128)(2,1)S(1)}, bf16[192,128]{1,0:T(8,128)(2,1)S(1)}, u32[]{:S(2)}, u32[]{:S(2)}) %collective-permute-start.8) | collective-permute-done | bytes 49184 | tf_op jit(solution)/shard_map/ppermute | solution.py:435
  72.8 1.1 %collective-permute-done.9.c_ref = bf16[192,128]{1,0:T(8,128)(2,1)S(1)} collective-permute-done((bf16[192,128]{1,0:T(8,128)(2,1)S(1)}, bf16[192,128]{1,0:T(8,128)(2,1)S(1)}, u32[]{:S(2)}, u32[]{:S(2)}) %collective-permute-start.9) | collective-permute-done | bytes 49184 | tf_op jit(solution)/shard_map/ppermute | solution.py:435
  73.9 0.7 line.1
  74.6 0.0 all-to-all-done.1.g_ref
  74.6 0.0 copy-start.4
  74.6 5.2 %all-to-all-start.2 = ((bf16[16,16,128]{2,1,0:T(8,128)(2,1)}), bf16[16,16,128]{2,1,0:T(8,128)(2,1)S(1)}, u32[]{:S(2)}, u32[]{:S(2)}) async-start(bf16[16,16,128]{2,1,0:T(8,128)(2,1)} %line.1), calls=%async_computation.2 | async-start | bytes 131072 | tf_op jit(solution)/shard_map/all_to_all | solution.py:465
  79.8 0.0 copy-done.4
  79.8 0.0 copy-start.1
  79.8 0.0 copy-start.3
  79.8 6.2 %finish.1 = (bf16[128,1024]{1,0:T(8,128)(2,1)}, bf16[128,1024]{1,0:T(8,128)(2,1)}) custom-call(s32[1]{0:T(128)S(6)} %sub.17.live_ref, bf16[128,1024]{1,0:T(8,128)(2,1)} %bitcast.16, bf16[128,1024]{1,0:T(8,128)(2,1)} %bitcast.23, f32[1,1024]{1,0:T(1,128)} %bitcast.19, bf16[16,256,128]{2,1,0:T(8,128)(2,1)} %copy-done.4, bf16[1024,1024]{1,0:T(8,128)(2,1)} %wq_ref.3, ...), custom_call_target="tpu_custom_call" | custom-call | flops 805306368 | bytes 8388608 | tf_op jit(solution)/shard_map/finish/pallas_call | solution.py:376
  86.1 1.4 %all-to-all-done.2.in_ref = bf16[16,16,128]{2,1,0:T(8,128)(2,1)S(1)} async-done(((bf16[16,16,128]{2,1,0:T(8,128)(2,1)}), bf16[16,16,128]{2,1,0:T(8,128)(2,1)S(1)}, u32[]{:S(2)}, u32[]{:S(2)}) %all-to-all-start.2) | async-done | bytes 65568 | tf_op jit(solution)/shard_map/all_to_all | solution.py:465
  87.4 0.0 copy-done.1
  87.4 0.0 copy-done.3
  87.4 0.7 settle.1
  (1 shorter events, 0.0 us)
Async XLA Ops:
  0.6 11.3 %collective-permute-start = (bf16[128,1024]{1,0:T(8,128)(2,1)}, bf16[128,1024]{1,0:T(8,128)(2,1)S(1)}, u32[]{:S(2)}, u32[]{:S(2)}) collective-permute-start(bf16[128,1024]{1,0:T(8,128)(2,1)} %bitcast.12), channel_id=1, source_target_pairs={{0,1},{1,0},{2,3},{3,2},{4,5},{5,4},{6,7},{7,6},{8,9},{9,8},{10,11... | collective-permute-start | bytes 786440 | tf_op jit(solution)/shard_map/ppermute | solution.py:431
  2.4 10.4 %collective-permute-start.1 = (bf16[128,1024]{1,0:T(8,128)(2,1)}, bf16[128,1024]{1,0:T(8,128)(2,1)S(1)}, u32[]{:S(2)}, u32[]{:S(2)}) collective-permute-start(bf16[128,1024]{1,0:T(8,128)(2,1)} %bitcast.13), channel_id=1, source_target_pairs={{0,2},{1,3},{2,0},{3,1},{4,6},{5,7},{6,4},{7,5},{8,10},{9,11},{10,... | collective-permute-start | bytes 786440 | tf_op jit(solution)/shard_map/ppermute | solution.py:431
  5.3 10.2 %collective-permute-start.2 = (bf16[128,1024]{1,0:T(8,128)(2,1)}, bf16[128,1024]{1,0:T(8,128)(2,1)S(1)}, u32[]{:S(2)}, u32[]{:S(2)}) collective-permute-start(bf16[128,1024]{1,0:T(8,128)(2,1)} %bitcast.14), channel_id=1, source_target_pairs={{0,3},{1,2},{2,1},{3,0},{4,7},{5,6},{6,5},{7,4},{8,11},{9,10},{10,... | collective-permute-start | bytes 786440 | tf_op jit(solution)/shard_map/ppermute | solution.py:431
  11.8 8.8 %copy-start = (bf16[1,128,1024]{2,1,0:T(8,128)(2,1)S(1)}, bf16[1,128,1024]{2,1,0:T(8,128)(2,1)}, u32[]{:S(2)}) copy-start(bf16[1,128,1024]{2,1,0:T(8,128)(2,1)} %param.10) | copy-start | bytes 786436
  11.8 8.8 %copy-start.2 = (f32[1024]{0:T(1024)S(1)}, f32[1024]{0:T(1024)}, u32[]{:S(2)}) copy-start(f32[1024]{0:T(1024)} %param.15) | copy-start | bytes 12292
  15.4 21.7 %all-to-all-start = ((bf16[16,144,256]{2,1,0:T(8,128)(2,1)}), bf16[16,144,256]{2,1,0:T(8,128)(2,1)S(1)}, u32[]{:S(2)}, u32[]{:S(2)}) async-start(bf16[16,144,256]{2,1,0:T(8,128)(2,1)} %get-tuple-element.34), calls=%async_computation | async-start | bytes 2359296 | tf_op jit(solution)/shard_map/all_to_all | solution.py:456
  20.9 35.5 %collective-permute-start.3 = (bf16[512,1024]{1,0:T(8,128)(2,1)S(1)}, bf16[512,1024]{1,0:T(8,128)(2,1)S(1)}, u32[]{:S(2)}, u32[]{:S(2)}) collective-permute-start(bf16[512,1024]{1,0:T(8,128)(2,1)S(1)} %gather.1.n0), channel_id=1, source_target_pairs={{0,4},{1,5},{2,6},{3,7},{4,0},{5,1},{6,2},{7,3},{8,12},{9,13},{10,... | collective-permute-start | bytes 3145736 | tf_op jit(solution)/shard_map/ppermute | solution.py:431
  22.9 34.7 %collective-permute-start.4 = (bf16[512,1024]{1,0:T(8,128)(2,1)S(1)}, bf16[512,1024]{1,0:T(8,128)(2,1)}, u32[]{:S(2)}, u32[]{:S(2)}) collective-permute-start(bf16[512,1024]{1,0:T(8,128)(2,1)S(1)} %gather.1.n0), channel_id=1, source_target_pairs={{0,8},{1,9},{2,10},{3,11},{4,12},{5,13},{6,14},{7,15},{8,0},{9,1},... | collective-permute-start | bytes 3145736 | tf_op jit(solution)/shard_map/ppermute | solution.py:431
  25.6 32.0 %collective-permute-start.5 = (bf16[512,1024]{1,0:T(8,128)(2,1)S(1)}, bf16[512,1024]{1,0:T(8,128)(2,1)}, u32[]{:S(2)}, u32[]{:S(2)}) collective-permute-start(bf16[512,1024]{1,0:T(8,128)(2,1)S(1)} %gather.1.n0), channel_id=1, source_target_pairs={{0,12},{1,13},{2,14},{3,15},{4,8},{5,9},{6,10},{7,11},{8,4},{9,5},... | collective-permute-start | bytes 3145736 | tf_op jit(solution)/shard_map/ppermute | solution.py:431
  51.9 22.7 %all-to-all-start.1 = ((bf16[16,256,128]{2,1,0:T(8,128)(2,1)}), bf16[16,256,128]{2,1,0:T(8,128)(2,1)S(1)}, u32[]{:S(2)}, u32[]{:S(2)}) async-start(bf16[16,256,128]{2,1,0:T(8,128)(2,1)} %attend.1.g0.g1.g2.g3.g4.g5.g6.g7), calls=%async_computation.1 | async-start | bytes 2097152 | tf_op jit(solution)/shard_map/all_to_all | solution.py:460
  61.2 2.4 %collective-permute-start.6 = (bf16[4,192,128]{2,1,0:T(8,128)(2,1)S(1)}, bf16[4,192,128]{2,1,0:T(8,128)(2,1)S(1)}, u32[]{:S(2)}, u32[]{:S(2)}) collective-permute-start(bf16[4,192,128]{2,1,0:T(8,128)(2,1)S(1)} %get-tuple-element.36), channel_id=1, source_target_pairs={{0,16},{16,0},{32,48},{48,32},{64,80},{80,64},{96,112},{112,96},{1... | collective-permute-start | bytes 589832 | tf_op jit(solution)/shard_map/ppermute | solution.py:439
  64.2 6.6 %collective-permute-start.7 = (bf16[192,128]{1,0:T(8,128)(2,1)S(1)}, bf16[192,128]{1,0:T(8,128)(2,1)S(1)}, u32[]{:S(2)}, u32[]{:S(2)}) collective-permute-start(bf16[192,128]{1,0:T(8,128)(2,1)S(1)} %get-tuple-element.38), channel_id=1, source_target_pairs={{0,32},{16,48},{32,64},{48,80},{64,96},{80,112},{96,0},{112,16},{1... | collective-permute-start | bytes 147464 | tf_op jit(solution)/shard_map/ppermute | solution.py:435
  66.2 6.6 %collective-permute-start.8 = (bf16[192,128]{1,0:T(8,128)(2,1)S(1)}, bf16[192,128]{1,0:T(8,128)(2,1)S(1)}, u32[]{:S(2)}, u32[]{:S(2)}) collective-permute-start(bf16[192,128]{1,0:T(8,128)(2,1)S(1)} %get-tuple-element.39), channel_id=1, source_target_pairs={{0,64},{16,80},{32,96},{48,112},{64,0},{80,16},{96,32},{112,48},{1... | collective-permute-start | bytes 147464 | tf_op jit(solution)/shard_map/ppermute | solution.py:435
  69.8 4.1 %collective-permute-start.9 = (bf16[192,128]{1,0:T(8,128)(2,1)S(1)}, bf16[192,128]{1,0:T(8,128)(2,1)S(1)}, u32[]{:S(2)}, u32[]{:S(2)}) collective-permute-start(bf16[192,128]{1,0:T(8,128)(2,1)S(1)} %get-tuple-element.40), channel_id=1, source_target_pairs={{0,96},{16,112},{32,0},{48,16},{64,32},{80,48},{96,64},{112,80},{1... | collective-permute-start | bytes 147464 | tf_op jit(solution)/shard_map/ppermute | solution.py:435
  74.6 5.2 %copy-start.4 = (bf16[16,256,128]{2,1,0:T(8,128)(2,1)}, bf16[16,256,128]{2,1,0:T(8,128)(2,1)S(1)}, u32[]{:S(2)}) copy-start(bf16[16,256,128]{2,1,0:T(8,128)(2,1)S(1)} %all-to-all-done.1.g_ref) | copy-start | bytes 3145732
  74.6 12.8 %all-to-all-start.2 = ((bf16[16,16,128]{2,1,0:T(8,128)(2,1)}), bf16[16,16,128]{2,1,0:T(8,128)(2,1)S(1)}, u32[]{:S(2)}, u32[]{:S(2)}) async-start(bf16[16,16,128]{2,1,0:T(8,128)(2,1)} %line.1), calls=%async_computation.2 | async-start | bytes 131072 | tf_op jit(solution)/shard_map/all_to_all | solution.py:465
  79.8 7.7 %copy-start.1 = (bf16[48,1024]{1,0:T(8,128)(2,1)S(1)}, bf16[48,1024]{1,0:T(8,128)(2,1)}, u32[]{:S(2)}) copy-start(bf16[48,1024]{1,0:T(8,128)(2,1)} %get-tuple-element.45.w_ref) | copy-start | bytes 294916
  79.8 7.7 %copy-start.3 = (f32[1024]{0:T(1024)S(1)}, f32[1024]{0:T(1024)}, u32[]{:S(2)}) copy-start(f32[1024]{0:T(1024)} %param.15) | copy-start | bytes 12292
